TPU v7x, 32 devices: a whole 2x2x4 slice. The times are simulated.
32 devices in a mesh: grp: 4 (over y, x), fsdp: 8 (over z, core).
Axes of the slice: x: 2, y: 2, z: 4, core: 2. Of those that a mesh axis runs over, the one named last changes fastest.
Arguments:
- tokens: int32 [2, 4, 2048], P(None, 'grp', 'fsdp'), may hold values from 0 to 32127
- routes: int32 [2, 4, 2048, 1], P(None, 'grp', 'fsdp'), may hold values from 0 to 1; in each aligned block of 256 rows (0 to 255, 256 to 511, ..., all dimensions but the last counted through in order) at most 192 rows name the same one
- segments: int32 [2, 4, 2048], P(None, 'grp', 'fsdp'), may hold values from 0 to 2, as said below
- loss_pos: int32 [2, 4, 128], P(None, 'grp', 'fsdp'), may hold values from 0 to 253, as said below
- embedding: float32 [32128, 768], P('fsdp'), may hold values from -6 to 6
- embedding_first: float32 [4, 32128, 768], P('grp', 'fsdp'), may hold values from -1.1920929e-07 to 1.1920929e-07
- embedding_second: float32 [4, 32128, 768], P('grp', 'fsdp'), may hold values from 1.5808284e-14 to 2.1077713e-13
- embedding_outer: float32 [32128, 768], P('fsdp'), may hold values from -3 to 3
- attention: float32 [5, 768, 768], P(None, 'fsdp'), may hold values from -0.21875 to 0.21875
- attention_first: float32 [4, 5, 768, 768], P('grp', None, 'fsdp'), may hold values from -4.7683716e-07 to 4.7683716e-07
- attention_second: float32 [4, 5, 768, 768], P('grp', None, 'fsdp'), may hold values from 1.5808284e-14 to 2.1077713e-13
- attention_outer: float32 [5, 768, 768], P(None, 'fsdp'), may hold values from -0.0625 to 0.0625
- experts: float32 [2, 2, 768, 3072], P(None, None, None, 'fsdp'), may hold values from -0.21875 to 0.21875
- experts_first: float32 [4, 2, 2, 768, 3072], P('grp', None, None, None, 'fsdp'), may hold values from -4.7683716e-07 to 4.7683716e-07
- experts_second: float32 [4, 2, 2, 768, 3072], P('grp', None, None, None, 'fsdp'), may hold values from 3.952071e-15 to 5.2694282e-14
- experts_outer: float32 [2, 2, 768, 3072], P(None, None, None, 'fsdp'), may hold values from -0.0625 to 0.0625
- vectors: float32 [6, 768], replicated, may hold values from -0.35 to 1.6, as said below
- vectors_first: float32 [4, 6, 768], P('grp'), may hold values from -1.9073486e-06 to 1.9073486e-06
- vectors_second: float32 [4, 6, 768], P('grp'), may hold values from 2.5293255e-13 to 3.372434e-12
- vectors_outer: float32 [6, 768], replicated, may hold values from -0.625 to 0.625
Outputs:
- losses: float32 [4, 2], P('grp')
- gradient_norms: float32 [4, 2], P('grp')
- embedding_moment: float32 [4, 32128, 768], P('grp', 'fsdp')
- embedding_square: float32 [4, 32128, 768], P('grp', 'fsdp')
- embedding_master: float32 [32128, 768], P('fsdp')
- embedding_momentum: float32 [32128, 768], P('fsdp')
- embedding_copy: bfloat16 [32128, 768], P('fsdp')
- attention_moment: float32 [4, 5, 768, 768], P('grp', None, 'fsdp')
- attention_square: float32 [4, 5, 768, 768], P('grp', None, 'fsdp')
- attention_master: float32 [5, 768, 768], P(None, 'fsdp')
- attention_momentum: float32 [5, 768, 768], P(None, 'fsdp')
- attention_copy: bfloat16 [5, 768, 768], P(None, 'fsdp')
- experts_moment: float32 [4, 2, 2, 768, 3072], P('grp', None, None, None, 'fsdp')
- experts_square: float32 [4, 2, 2, 768, 3072], P('grp', None, None, None, 'fsdp')
- experts_master: float32 [2, 2, 768, 3072], P(None, None, None, 'fsdp')
- experts_momentum: float32 [2, 2, 768, 3072], P(None, None, None, 'fsdp')
- experts_copy: bfloat16 [2, 2, 768, 3072], P(None, None, None, 'fsdp')
- vectors_gradient: float32 [4, 6, 768], P('grp')
- vectors_moment: float32 [4, 6, 768], P('grp')
- vectors_square: float32 [4, 6, 768], P('grp')
- vectors_master: float32 [6, 768], replicated
- vectors_momentum: float32 [6, 768], replicated
Inputs may be any that keep to these rules, and one draw needn't show every extreme that they name: `segments`: on each device's 256 slots: 0 for a first document, 1 for a second one, 2 for padding at the end; each document present has 64 slots or more; in every step and group one device holds a single document of 256 slots. `loss_pos`: A position on the device, inside a document that has two more slots after it. `routes`: at most 192 of one device's 256 tokens name the same expert. `vectors`: rows 0 to 3 near one, the router's rows small.
All inputs are finite; a program needn't handle non-finite values.
Results may differ from a plain program's by a relative error of at most 0.033.
Values may be sent and summed in bfloat16 or wider, within the bound.
A program may use at most 448 MiB of HBM per device.

v0:
```python
import math

import jax
import jax.numpy as jnp
from jax import lax
from jax.sharding import PartitionSpec as P

D = 768
HEADS = 12
HEAD_DIM = 64
EXPERTS = 2
STEP0 = 5
CAP = 192


HIGH = lax.Precision.HIGHEST
EPSILON = 1e-06
ATTN_GAIN = 8.0
SECOND_WEIGHT = 0.3
BETA_ONE = 0.9
BETA_TWO = 0.95
ADAM_EPS = 1e-08
DECAY = 0.1
LR_EMBED = 0.5
LR_MATRIX = 0.012
LR_GAIN = 0.3
LR_ROUTER = 0.012
OUTER_RATE = 0.7
OUTER_MOMENTUM = 0.9


def for_sending(value):

    def short(part):
        return part.astype(jnp.bfloat16) if part.dtype == jnp.float32 else part

    return jax.tree.map(short, value)


def smooth_act(values):
    return jax.nn.gelu(values, approximate=True)


def norm_apply(x, gain_row):
    factor = lax.rsqrt(jnp.mean(x * x, axis=-1, keepdims=True) + EPSILON)
    return (x * factor * gain_row, factor)


def norm_back(x, factor, gain_row, upstream):
    normed = x * factor
    gain_grad = jnp.sum(upstream * normed, axis=0)
    scaled = upstream * gain_row
    return (
        factor * (scaled - normed * jnp.mean(scaled * normed, axis=-1, keepdims=True)),
        gain_grad,
    )


def score_block(queries, keys_all, allowed):
    scores = jnp.einsum(
        "qhd,khd->hqk", queries, keys_all, preferred_element_type=jnp.float32
    ) * HEAD_DIM ** (-0.5)
    return jnp.where(allowed[None], scores, -1e30)


def attend(queries, keys_all, values_all, allowed):
    scores = score_block(queries, keys_all, allowed)
    highest = jnp.max(scores, axis=-1, keepdims=True)
    exponent = jnp.exp(scores - highest)
    totals = jnp.sum(exponent, axis=-1, keepdims=True)
    probs_low = (exponent / totals).astype(jnp.bfloat16)
    attended = jnp.einsum("hqk,khd->qhd", probs_low, values_all, preferred_element_type=jnp.float32)
    return (attended, highest + jnp.log(totals))


def attend_back(queries, keys_all, values_all, allowed, logsum, upstream):
    probs_full = jnp.exp(score_block(queries, keys_all, allowed) - logsum)
    dprobs = jnp.einsum("qhd,khd->hqk", upstream, values_all, preferred_element_type=jnp.float32)
    spread = jnp.sum(probs_full * dprobs, axis=-1, keepdims=True)
    dscores = (probs_full * (dprobs - spread)).astype(jnp.bfloat16)
    factor_qk = HEAD_DIM ** (-0.5)
    query_grad = (
        jnp.einsum("hqk,khd->qhd", dscores, keys_all, preferred_element_type=jnp.float32)
        * factor_qk
    )
    key_grad = (
        jnp.einsum("hqk,qhd->khd", dscores, queries, preferred_element_type=jnp.float32) * factor_qk
    )
    value_grad = jnp.einsum(
        "hqk,qhd->khd",
        probs_full.astype(jnp.bfloat16),
        upstream,
        preferred_element_type=jnp.float32,
    )
    return (query_grad, key_grad, value_grad)


def expert_slots(route_ids):
    onehot = (route_ids[:, None] == jnp.arange(EXPERTS, dtype=jnp.int32)[None, :]).astype(jnp.int32)
    return (jnp.sum(jnp.cumsum(onehot, axis=0) * onehot, axis=1) - 1, onehot)


def layer_forward(attn_low, expert_low, vector_w, x_embed, seg_ids, route_ids):
    count_rows, width_model = x_embed.shape
    a_float, a_factor = norm_apply(x_embed, vector_w[0])
    a = a_float.astype(jnp.bfloat16)
    triple = jnp.einsum("td,jde->jte", a, attn_low[0:3], preferred_element_type=jnp.float32).astype(
        jnp.bfloat16
    )
    heads_qkv = triple.reshape(3, count_rows, HEADS, HEAD_DIM)
    places = jnp.arange(count_rows)
    allowed = (places[None, :] <= places[:, None]) & (seg_ids[:, None] == seg_ids[None, :])
    attended, logsum = attend(heads_qkv[0], heads_qkv[1], heads_qkv[2], allowed)
    attended_low = attended.reshape(count_rows, width_model).astype(jnp.bfloat16)
    x_attn = x_embed + ATTN_GAIN * jnp.dot(
        attended_low, attn_low[3], preferred_element_type=jnp.float32
    )
    b, b_factor = norm_apply(x_attn, vector_w[1])
    router_probs = jax.nn.softmax(jnp.dot(b, vector_w[4:].T, precision=HIGH), axis=-1)
    slot_ids, onehot = expert_slots(route_ids)
    gating = jnp.sum(router_probs * onehot, axis=1)
    buffer_in = (
        jnp.zeros((EXPERTS, CAP, width_model), jnp.bfloat16)
        .at[route_ids, slot_ids]
        .set(b.astype(jnp.bfloat16))
    )
    hidden_pre = jnp.einsum(
        "ecd,edf->ecf", buffer_in, expert_low[:, 0], preferred_element_type=jnp.float32
    )
    hidden_act = smooth_act(hidden_pre).astype(jnp.bfloat16)
    buffer_out = jnp.einsum(
        "ecf,edf->ecd", hidden_act, expert_low[:, 1], preferred_element_type=jnp.float32
    )
    returned = buffer_out[route_ids, slot_ids]
    x_final = x_attn + gating[:, None] * returned
    kept_values = (
        x_embed,
        a_factor,
        a,
        heads_qkv,
        allowed,
        logsum,
        attended_low,
        x_attn,
        b_factor,
        b,
        router_probs,
        onehot,
        gating,
        slot_ids,
        buffer_in,
        hidden_pre,
        hidden_act,
        returned,
    )
    return (x_final, kept_values)


def expert_backward(expert_low, vector_w, kept_values, dx_final, route_ids):
    (
        x_embed,
        a_factor,
        a,
        heads_qkv,
        allowed,
        logsum,
        attended_low,
        x_attn,
        b_factor,
        b,
        router_probs,
        onehot,
        gating,
        slot_ids,
        buffer_in,
        hidden_pre,
        hidden_act,
        returned,
    ) = kept_values
    width_model = x_embed.shape[1]
    dgating = jnp.sum(dx_final * returned, axis=1)
    dreturned = (gating[:, None] * dx_final).astype(jnp.bfloat16)
    dbuffer_out = (
        jnp.zeros((EXPERTS, CAP, width_model), jnp.bfloat16).at[route_ids, slot_ids].set(dreturned)
    )
    down_grad = jnp.einsum(
        "ecf,ecd->edf", hidden_act, dbuffer_out, preferred_element_type=jnp.float32
    )
    dhidden = jnp.einsum(
        "ecd,edf->ecf", dbuffer_out, expert_low[:, 1], preferred_element_type=jnp.float32
    )
    unused, act_back = jax.vjp(smooth_act, hidden_pre)
    dhidden_pre = act_back(dhidden)[0].astype(jnp.bfloat16)
    up_grad = jnp.einsum("ecd,ecf->edf", buffer_in, dhidden_pre, preferred_element_type=jnp.float32)
    dbuffer_in = jnp.einsum(
        "ecf,edf->ecd", dhidden_pre, expert_low[:, 0], preferred_element_type=jnp.float32
    )
    dnormed = dbuffer_in[route_ids, slot_ids]
    prob_grad = onehot * dgating[:, None]
    dlogit = router_probs * (prob_grad - jnp.sum(router_probs * prob_grad, axis=1, keepdims=True))
    drouter = jnp.dot(dlogit.T, b, precision=HIGH)
    dnormed = dnormed + jnp.dot(dlogit, vector_w[4:], precision=HIGH)
    dx_attn_part, gain_ffn = norm_back(x_attn, b_factor, vector_w[1], dnormed)
    return (dx_final + dx_attn_part, jnp.stack([up_grad, down_grad], axis=1), gain_ffn, drouter)


def attention_backward(attn_low, vector_w, kept_values, dx_attn):
    (
        x_embed,
        a_factor,
        a,
        heads_qkv,
        allowed,
        logsum,
        attended_low,
        x_attn,
        b_factor,
        b,
        router_probs,
        onehot,
        gating,
        slot_ids,
        buffer_in,
        hidden_pre,
        hidden_act,
        returned,
    ) = kept_values
    count_rows, width_model = x_embed.shape
    dbranch = dx_attn.astype(jnp.bfloat16)
    dwout = ATTN_GAIN * jnp.dot(attended_low.T, dbranch, preferred_element_type=jnp.float32)
    dattended = (
        ATTN_GAIN * jnp.dot(dbranch, attn_low[3].T, preferred_element_type=jnp.float32)
    ).astype(jnp.bfloat16)
    query_grad, key_grad, value_grad = attend_back(
        heads_qkv[0],
        heads_qkv[1],
        heads_qkv[2],
        allowed,
        logsum,
        dattended.reshape(count_rows, HEADS, HEAD_DIM),
    )
    dtriple = (
        jnp.stack([query_grad, key_grad, value_grad])
        .reshape(3, count_rows, width_model)
        .astype(jnp.bfloat16)
    )
    dproject = jnp.einsum("td,jte->jde", a, dtriple, preferred_element_type=jnp.float32)
    dinput = jnp.einsum("jte,jde->td", dtriple, attn_low[0:3], preferred_element_type=jnp.float32)
    dx_embed_part, gain_attn = norm_back(x_embed, a_factor, vector_w[0], dinput)
    dlayer = jnp.concatenate([dproject, dwout[None]], axis=0)
    return (dx_attn + dx_embed_part, dlayer, gain_attn)


def adam_update(weight, first_moment, second, gradient, step_float, rate_here, decay_here):
    first_new = BETA_ONE * first_moment + (1.0 - BETA_ONE) * gradient
    second_new = BETA_TWO * second + (1.0 - BETA_TWO) * gradient * gradient
    first_hat = first_new / (1.0 - BETA_ONE**step_float)
    second_hat = second_new / (1.0 - BETA_TWO**step_float)
    weight_new = weight - rate_here * (
        first_hat / (jnp.sqrt(second_hat) + ADAM_EPS) + decay_here * weight
    )
    return (weight_new, first_new, second_new)


def shards(
    tokens,
    routes,
    segments,
    loss_pos,
    embedding,
    embedding_first,
    embedding_second,
    embedding_outer,
    attention,
    attention_first,
    attention_second,
    attention_outer,
    experts,
    experts_first,
    experts_second,
    experts_outer,
    vectors,
    vectors_first,
    vectors_second,
    vectors_outer,
):
    inner_count = tokens.shape[0]
    vocab_shard = embedding.shape[0]
    vocab_start = lax.axis_index("fsdp") * vocab_shard
    group_count = lax.axis_size("grp")
    row_total = lax.axis_size("fsdp") * loss_pos.shape[2]
    threshold = 0.05 / math.sqrt(row_total)
    logit_scale = 2.0 * D ** (-0.5)
    all_ids = lax.all_gather(tokens[:, 0, :], "fsdp", axis=1, tiled=True)
    vocab_places = jnp.arange(vocab_shard)
    head_weights = jnp.array([1.0, SECOND_WEIGHT], jnp.float32)
    vector_rates = jnp.where(jnp.arange(vectors.shape[0])[:, None] < 4, LR_GAIN, LR_ROUTER)
    rate_list = (LR_EMBED, LR_MATRIX, LR_MATRIX, vector_rates)
    decay_list = (DECAY, DECAY, DECAY, 0.0)
    weights_now = (embedding, attention, experts, vectors)
    first_now = (embedding_first[0], attention_first[0], experts_first[0], vectors_first[0])
    second_now = (embedding_second[0], attention_second[0], experts_second[0], vectors_second[0])
    loss_list = []
    norm_list = []
    for inner_step in range(inner_count):
        embed_w, attn_w, expert_w, vector_w = weights_now
        embed_low = embed_w.astype(jnp.bfloat16)
        attn_low, expert_low = (
            lax.all_gather(attn_w.astype(jnp.bfloat16), "fsdp", axis=1, tiled=True),
            lax.all_gather(expert_w.astype(jnp.bfloat16), "fsdp", axis=3, tiled=True),
        )
        ids_group = all_ids[inner_step]
        ids_local = tokens[inner_step, 0]
        seg_ids = segments[inner_step, 0]
        route_ids = routes[inner_step, 0, :, 0]
        pick_ids = loss_pos[inner_step, 0]
        chosen = ids_group - vocab_start
        inside = (chosen >= 0) & (chosen < vocab_shard)
        looked = jnp.take(embed_low, jnp.clip(chosen, 0, vocab_shard - 1), axis=0).astype(
            jnp.float32
        )
        x_embed = lax.psum_scatter(
            jnp.where(inside[:, None], looked, 0.0).astype(jnp.bfloat16),
            "fsdp",
            scatter_dimension=0,
            tiled=True,
        ).astype(jnp.float32)
        x_final, kept_values = layer_forward(
            attn_low, expert_low, vector_w, x_embed, seg_ids, route_ids
        )
        z_rows = x_final[pick_ids]
        first_float, first_factor = norm_apply(z_rows, vector_w[2])
        first_rows = first_float.astype(jnp.bfloat16)
        middle = jnp.dot(first_rows, attn_low[4], preferred_element_type=jnp.float32)
        second_float, second_factor = norm_apply(middle, vector_w[3])
        targets = jnp.stack([ids_local[pick_ids + 1], ids_local[pick_ids + 2]])
        rows_all, targets_all = (
            lax.all_gather(
                jnp.stack([first_rows, second_float.astype(jnp.bfloat16)]),
                "fsdp",
                axis=1,
                tiled=True,
            ),
            lax.all_gather(targets, "fsdp", axis=1, tiled=True),
        )
        logits = (
            jnp.einsum("jrd,vd->jrv", rows_all, embed_low, preferred_element_type=jnp.float32)
            * logit_scale
        )
        relative = targets_all - vocab_start
        onehot_target = (vocab_places[None, None, :] == relative[:, :, None]).astype(jnp.float32)
        target_part = jnp.sum(onehot_target * logits, axis=-1)
        local_top = jnp.max(logits, axis=-1)
        row_top = lax.pmax(local_top, "fsdp")
        sum_exp, target_logit = lax.psum(
            (jnp.sum(jnp.exp(logits - row_top[:, :, None]), axis=-1), target_part), "fsdp"
        )
        logsum = row_top + jnp.log(sum_exp)
        loss_list.append(jnp.sum(head_weights[:, None] * (logsum - target_logit)) / row_total)
        dlogits = (
            (jnp.exp(logits - logsum[:, :, None]) - onehot_target)
            * (head_weights / row_total)[:, None, None]
        ).astype(jnp.bfloat16)
        dembed = (
            jnp.einsum("jrv,jrd->vd", dlogits, rows_all, preferred_element_type=jnp.float32)
            * logit_scale
        )
        drows = (
            jnp.einsum("jrv,vd->jrd", dlogits, embed_low, preferred_element_type=jnp.float32)
            * logit_scale
        )
        drows_own = lax.psum_scatter(
            drows.astype(jnp.bfloat16), "fsdp", scatter_dimension=1, tiled=True
        ).astype(jnp.float32)
        attn_low, expert_low = (
            lax.all_gather(attn_w.astype(jnp.bfloat16), "fsdp", axis=1, tiled=True),
            lax.all_gather(expert_w.astype(jnp.bfloat16), "fsdp", axis=3, tiled=True),
        )
        dmiddle, gain_mtp = norm_back(middle, second_factor, vector_w[3], drows_own[1])
        dmiddle_low = dmiddle.astype(jnp.bfloat16)
        dsecond_proj = jnp.dot(first_rows.T, dmiddle_low, preferred_element_type=jnp.float32)
        dfirst = drows_own[0] + jnp.dot(
            dmiddle_low, attn_low[4].T, preferred_element_type=jnp.float32
        )
        dz_rows, gain_final = norm_back(z_rows, first_factor, vector_w[2], dfirst)
        dx_final = jnp.zeros_like(x_final).at[pick_ids].add(dz_rows)
        dx_attn, dexperts, gain_ffn, drouter = expert_backward(
            expert_low, vector_w, kept_values, dx_final, route_ids
        )
        dx_embed, dlayer, gain_attn = attention_backward(attn_low, vector_w, kept_values, dx_attn)
        dattn_full = jnp.concatenate([dlayer, dsecond_proj[None]], axis=0)
        dattn, dexpert = (
            lax.psum_scatter(
                dattn_full.astype(jnp.bfloat16), "fsdp", scatter_dimension=1, tiled=True
            ).astype(jnp.float32),
            lax.psum_scatter(
                dexperts.astype(jnp.bfloat16), "fsdp", scatter_dimension=3, tiled=True
            ).astype(jnp.float32),
        )
        gather_chosen = ids_group - vocab_start
        gather_inside = (gather_chosen >= 0) & (gather_chosen < vocab_shard)
        seg_index = jnp.where(gather_inside, gather_chosen, vocab_shard)
        added = jax.ops.segment_sum(
            lax.all_gather(dx_embed.astype(jnp.bfloat16), "fsdp", axis=0, tiled=True).astype(
                jnp.float32
            ),
            seg_index,
            num_segments=vocab_shard + 1,
        )
        dembed = dembed + added[:vocab_shard]
        dvector_part = jnp.concatenate(
            [jnp.stack([gain_attn, gain_ffn, gain_final, gain_mtp]), drouter], axis=0
        )
        squares = jnp.sum(dembed * dembed) + jnp.sum(dattn * dattn) + jnp.sum(dexpert * dexpert)
        dvector, squares_all = lax.psum((dvector_part, squares), "fsdp")
        norm_value = jnp.sqrt(squares_all + jnp.sum(dvector * dvector))
        norm_list.append(norm_value)
        factor = jnp.minimum(1.0, threshold / norm_value)
        gradients = (dembed * factor, dattn * factor, dexpert * factor, dvector * factor)
        step_float = float(STEP0 + inner_step + 1)
        results = [
            adam_update(
                weights_now[k],
                first_now[k],
                second_now[k],
                gradients[k],
                step_float,
                rate_list[k],
                decay_list[k],
            )
            for k in range(4)
        ]
        weights_now = tuple((element[0] for element in results))
        first_now = tuple((element[1] for element in results))
        second_now = tuple((element[2] for element in results))
    masters = (embedding, attention, experts, vectors)
    outers = (embedding_outer, attention_outer, experts_outer, vectors_outer)
    deltas = tuple((master - current for master, current in zip(masters, weights_now)))
    summed = jax.tree.map(
        lambda part: part.astype(jnp.float32), lax.psum(for_sending(deltas), "grp")
    )
    new_outer = []
    new_master = []
    for k in range(4):
        delta_mean = summed[k] / group_count
        outer_new = OUTER_MOMENTUM * outers[k] + delta_mean
        new_outer.append(outer_new)
        new_master.append(masters[k] - OUTER_RATE * (delta_mean + OUTER_MOMENTUM * outer_new))
    return (
        jnp.stack(loss_list)[None],
        jnp.stack(norm_list)[None],
        first_now[0][None],
        second_now[0][None],
        new_master[0],
        new_outer[0],
        new_master[0].astype(jnp.bfloat16),
        first_now[1][None],
        second_now[1][None],
        new_master[1],
        new_outer[1],
        new_master[1].astype(jnp.bfloat16),
        first_now[2][None],
        second_now[2][None],
        new_master[2],
        new_outer[2],
        new_master[2].astype(jnp.bfloat16),
        gradients[3][None],
        first_now[3][None],
        second_now[3][None],
        new_master[3],
        new_outer[3],
    )


def solution(mesh):
    return jax.shard_map(
        shards,
        mesh=mesh,
        in_specs=(
            P(None, "grp", "fsdp"),
            P(None, "grp", "fsdp", None),
            P(None, "grp", "fsdp"),
            P(None, "grp", "fsdp"),
            P("fsdp", None),
            P("grp", "fsdp", None),
            P("grp", "fsdp", None),
            P("fsdp", None),
            P(None, "fsdp", None),
            P("grp", None, "fsdp", None),
            P("grp", None, "fsdp", None),
            P(None, "fsdp", None),
            P(None, None, None, "fsdp"),
            P("grp", None, None, None, "fsdp"),
            P("grp", None, None, None, "fsdp"),
            P(None, None, None, "fsdp"),
            P(),
            P("grp", None, None),
            P("grp", None, None),
            P(),
        ),
        out_specs=(
            P("grp", None),
            P("grp", None),
            P("grp", "fsdp", None),
            P("grp", "fsdp", None),
            P("fsdp", None),
            P("fsdp", None),
            P("fsdp", None),
            P("grp", None, "fsdp", None),
            P("grp", None, "fsdp", None),
            P(None, "fsdp", None),
            P(None, "fsdp", None),
            P(None, "fsdp", None),
            P("grp", None, None, None, "fsdp"),
            P("grp", None, None, None, "fsdp"),
            P(None, None, None, "fsdp"),
            P(None, None, None, "fsdp"),
            P(None, None, None, "fsdp"),
            P("grp", None, None),
            P("grp", None, None),
            P("grp", None, None),
            P(),
            P(),
        ),
        check_vma=False,
    )
```

profile of v0, /device:TPU:0, one launch (start us, length us, event | category | flops | bytes accessed | tf_op | source)
XLA Modules:
  0.0 2088.4 jit_solution(13665904444709205677)
XLA Ops:
  7.2 13.7 all-gather
  30.0 12.0 gather_fusion.10
  56.4 8.9 all-gather.2
  65.3 10.8 all-gather.1
  84.2 61.7 %all-gather.10.cloned.1.call-done = bf16[5,768,768]{2,1,0:T(8,128)(2,1)} async-done(((bf16[5,96,768]{2,1,0:T(8,128)(2,1)}), bf16[5,768,768]{2,1,0:T(8,128)(2,1)}) %all-gather.10.cloned.1.call-update) | async-done | bytes 5898256 | tf_op jit(solution)/shard_map/all_gather | solution.py:309
  159.3 37.5 %scatter_fusion = bf16[2,192,768]{2,1,0:T(8,128)(2,1)} fusion(bf16[2,192,768]{2,1,0:T(8,128)(2,1)} %broadcast.841.clone, s32[256]{0:T(256)S(1)} %bitcast.493, bf16[256,768]{1,0:T(8,128)(2,1)} %multiply_convert_fusion.11), kind=kCustom, calls=%fused_computation.12 | custom fusion | bytes 1181696 | tf_op jit(solution)/shard_map/scatter | solution.py:125
  200.6 114.4 %all-gather.12.cloned.1.call-done = bf16[2,2,768,3072]{3,2,0,1:T(8,128)(2,1)} async-done(((bf16[2,2,768,384]{3,2,0,1:T(8,128)(2,1)}), bf16[2,2,768,3072]{3,2,0,1:T(8,128)(2,1)}) %all-gather.12.cloned.1.call-update) | async-done | bytes 18874384 | tf_op jit(solution)/shard_map/all_gather | solution.py:310
  320.9 9.1 fusion.5
  343.7 14.7 all_gather.40
  366.7 14.6 pmax.14
  385.0 14.3 psum.84
  409.2 27.7 %reduce-scatter.19.cloned.1.call-done = bf16[2,16,768]{2,1,0:T(8,128)(2,1)} async-done(((bf16[2,128,768]{2,1,0:T(8,128)(2,1)}), bf16[2,16,768]{2,1,0:T(8,128)(2,1)}) %reduce-scatter.19.cloned.1.call-update) | async-done | bytes 49168 | tf_op jit(solution)/shard_map/reduce_scatter | solution.py:372
  449.3 37.5 %scatter_fusion.1 = bf16[2,192,768]{2,1,0:T(8,128)(2,1)} fusion(bf16[2,192,768]{2,1,0:T(8,128)(2,1)} %broadcast.841.clone.1, s32[256]{0:T(256)S(1)} %bitcast.494, bf16[256,768]{1,0:T(8,128)(2,1)} %get-tuple-element.192), kind=kCustom, calls=%fused_computation.14 | custom fusion | bytes 1181696 | tf_op jit(solution)/shard_map/scatter | solution.py:184
  535.2 12.1 copy.297
  560.5 8.8 convert_bitcast_fusion.2
  569.3 11.9 pad_maximum_fusion
  581.2 46.8 %copy.299 = bf16[2,2,768,3072]{2,0,1,3:T(2,128)(2,1)} copy(bf16[2,2,768,3072]{3,2,0,1:T(8,128)(2,1)} %pad_maximum_fusion) | data formatting | bytes 37748736
  628.0 40.5 %reshape.1016 = bf16[3072,3072]{1,0:T(8,128)(2,1)} reshape(bf16[3072,2,2,768]{3,2,1,0:T(2,128)(2,1)} %bitcast.485) | data formatting | bytes 37748736
  670.7 20.0 scatter_custom_fusion.3
  690.7 11.6 multiply_reduce_fusion.1
  707.5 147.5 %reduce-scatter.27.cloned.1.call-done = bf16[384,3072]{1,0:T(8,128)(2,1)} async-done(((bf16[3072,3072]{1,0:T(8,128)(2,1)}), bf16[384,3072]{1,0:T(8,128)(2,1)}) %reduce-scatter.27.cloned.1.call-update) | async-done | bytes 2359312
  869.9 26.2 %all-reduce.1 = (f32[]{:T(128)}, f32[6,768]{1,0:T(8,128)S(1)}) all-reduce(f32[]{:T(128)S(6)} %add.561, f32[6,768]{1,0:T(8,128)S(1)} %concatenate.32), channel_id=1, replica_groups=mesh['grp'=4,'fsdp'=8] {'fsdp'}, use_global_device_ids=true, to_apply=%region_37.39 | all-reduce | flops 4609 | bytes 36872 | tf_op jit(solution)/shard_map/psum | solution.py:415
  898.1 29.2 %fusion.244 = (bf16[4016,768]{1,0:T(8,128)(2,1)}, f32[4016,768]{1,0:T(8,128)}, f32[4016,768]{1,0:T(8,128)}) fusion(f32[4016,768]{1,0:T(8,128)} %param.27, f32[4016,768]{1,0:T(8,128)} %get-tuple-element.235, f32[]{:T(128)S(6)} %min.25, f32[1,4016,768]{2,1,0:T(8,128)} %param.28, f32[1,4016,768]{2,1,0:T(8,128)} %param.29), kind=kLoop, calls=%fused_computation.503 | loop fusion | flops 52432896 | bytes 80191488 | tf_op jit(solution)/shard_map/convert_element_type | solution.py:307
  927.3 13.6 gather_fusion.11
  972.6 10.6 reduce-scatter.21.cloned.1.call-done
  984.4 61.6 %all-gather.16.cloned.1.call-done = bf16[5,768,768]{2,1,0:T(8,128)(2,1)} async-done(((bf16[5,96,768]{2,1,0:T(8,128)(2,1)}), bf16[5,768,768]{2,1,0:T(8,128)(2,1)}) %all-gather.16.cloned.1.call-update) | async-done | bytes 5898256 | tf_op jit(solution)/shard_map/all_gather | solution.py:309
  1057.0 37.3 %scatter_fusion.2 = bf16[2,192,768]{2,1,0:T(8,128)(2,1)} fusion(bf16[2,192,768]{2,1,0:T(8,128)(2,1)} %broadcast.841.clone.2, s32[256]{0:T(256)S(1)} %bitcast.491, bf16[256,768]{1,0:T(8,128)(2,1)} %multiply_convert_fusion.10), kind=kCustom, calls=%fused_computation.16 | custom fusion | bytes 1181696 | tf_op jit(solution)/shard_map/scatter | solution.py:125
  1097.5 117.5 %all-gather.18.cloned.1.call-done = bf16[2,2,768,3072]{3,2,0,1:T(8,128)(2,1)} async-done(((bf16[2,2,768,384]{3,2,0,1:T(8,128)(2,1)}), bf16[2,2,768,3072]{3,2,0,1:T(8,128)(2,1)}) %all-gather.18.cloned.1.call-update) | async-done | bytes 18874384 | tf_op jit(solution)/shard_map/all_gather | solution.py:310
  1220.8 9.1 fusion.9
  1243.5 14.7 all_gather.45
  1266.5 14.6 pmax.15
  1284.9 14.3 psum.88
  1309.0 27.6 %reduce-scatter.23.cloned.1.call-done = bf16[2,16,768]{2,1,0:T(8,128)(2,1)} async-done(((bf16[2,128,768]{2,1,0:T(8,128)(2,1)}), bf16[2,16,768]{2,1,0:T(8,128)(2,1)}) %reduce-scatter.23.cloned.1.call-update) | async-done | bytes 49168 | tf_op jit(solution)/shard_map/reduce_scatter | solution.py:372
  1349.0 37.4 %scatter_fusion.3 = bf16[2,192,768]{2,1,0:T(8,128)(2,1)} fusion(bf16[2,192,768]{2,1,0:T(8,128)(2,1)} %broadcast.841, s32[256]{0:T(256)S(1)} %bitcast.492, bf16[256,768]{1,0:T(8,128)(2,1)} %get-tuple-element.190), kind=kCustom, calls=%fused_computation.18 | custom fusion | bytes 1181696 | tf_op jit(solution)/shard_map/scatter | solution.py:184
  1435.1 12.2 copy.301
  1460.5 8.8 convert_bitcast_fusion
  1469.3 11.8 pad_maximum_fusion.1
  1481.1 46.9 %copy.303 = bf16[2,2,768,3072]{2,0,1,3:T(2,128)(2,1)} copy(bf16[2,2,768,3072]{3,2,0,1:T(8,128)(2,1)} %pad_maximum_fusion.1) | data formatting | bytes 37748736
  1528.0 40.5 %reshape.1020 = bf16[3072,3072]{1,0:T(8,128)(2,1)} reshape(bf16[3072,2,2,768]{3,2,1,0:T(2,128)(2,1)} %bitcast.486) | data formatting | bytes 37748736
  1570.4 20.0 scatter_custom_fusion.7
  1590.4 11.6 multiply_reduce_fusion
  1607.2 148.3 %reduce-scatter.31.cloned.1.call-done = bf16[384,3072]{1,0:T(8,128)(2,1)} async-done(((bf16[3072,3072]{1,0:T(8,128)(2,1)}), bf16[384,3072]{1,0:T(8,128)(2,1)}) %reduce-scatter.31.cloned.1.call-update) | async-done | bytes 2359312
  1773.2 26.2 %all-reduce = (f32[2,128]{1,0:T(2,128)S(1)}, f32[2,128]{1,0:T(2,128)S(1)}, f32[]{:T(128)}, f32[6,768]{1,0:T(8,128)S(1)}) all-reduce(f32[2,128]{1,0:T(2,128)S(1)} %copy-done.131, f32[2,128]{1,0:T(2,128)S(1)} %copy-done.132, f32[]{:T(128)S(6)} %add.603, f32[6,768]{1,0:T(8,128)S(1)} %concatenate.35), channel_id=1, replica_groups=mesh['grp'=4,'fsdp'=8] {'fsdp'}, use_global_device_ids=true, to_apply=%region_19.21 | all-reduce | flops 5121 | bytes 40968 | tf_op jit(solution)/shard_map/psum | solution.py:355
  1808.1 13.8 fusion.66
  1822.0 28.3 %subtract_convert_fusion = (bf16[4016,768]{1,0:T(8,128)(2,1)}, f32[1,4016,768]{2,1,0:T(8,128)}, f32[1,4016,768]{2,1,0:T(8,128)}) fusion(f32[4016,768]{1,0:T(8,128)S(1)} %bitcast.482, f32[4016,768]{1,0:T(8,128)} %get-tuple-element.252, f32[]{:T(128)S(6)} %min.28, f32[4016,768]{1,0:T(8,128)} %get-tuple-element.166, f32[4016,768]{1,0:T(8,128)} %get-tuple-element.167), kind=kLoop, calls=%fused_computation.34 | loop fusion | flops 80191488 | bytes 80191488 | tf_op jit(solution)/shard_map/convert_element_type | solution.py:35
  1873.5 16.1 psum.95
  1891.4 148.9 %all-reduce.5.cloned.1.call-done = (bf16[4016,768]{1,0:T(8,128)(2,1)}, bf16[5,96,768]{1,2,0:T(8,128)(2,1)}, bf16[2,2,768,384]{3,2,0,1:T(8,128)(2,1)}) async-done(((bf16[4016,768]{1,0:T(8,128)(2,1)}, bf16[5,96,768]{1,2,0:T(8,128)(2,1)}, bf16[2,2,768,384]{3,2,0,1:T(8,128)(2,1)}), (bf16[4016,768]{1,0:T(8,128)(2,1)}, bf16[5,96,768]{1,2,0:T(8,128)(2,1)}, ...) | async-done | bytes 9265168 | tf_op jit(solution)/shard_map/psum | solution.py:440
  2064.6 17.0 fusion.251
  (568 shorter events, 423.9 us)
Async XLA Ops:
  7.2 75.9 %reduce-scatter.17.cloned.1.call-start = ((), (), s32[]{:S(2)}) async-start(), calls=%async_computation.8 | async-start | bytes 3538944 | tf_op jit(solution)/shard_map/reduce_scatter | solution.py:322
  44.2 101.7 %all-gather.10.cloned.1.call-start = ((), (), s32[]{:S(2)}) async-start(), calls=%async_computation.9 | async-start | bytes 6635520 | tf_op jit(solution)/shard_map/all_gather | solution.py:309
  46.6 31.5 %copy-start.48 = (f32[6,768]{1,0:T(8,128)S(1)}, f32[6,768]{1,0:T(8,128)}, u32[]{:S(2)}) copy-start(f32[6,768]{1,0:T(8,128)} %param.39) | copy-start | bytes 55300
  46.6 32.1 %copy-start.135 = (s32[2,1,256]{2,1,0:T(1,128)S(1)}, s32[2,1,256]{2,1,0:T(1,128)}, u32[]{:S(2)}) copy-start(s32[2,1,256]{2,1,0:T(1,128)} %param.25) | copy-start | bytes 6148
  46.6 268.4 %all-gather.12.cloned.1.call-start = ((), (), s32[]{:S(2)}) async-start(), calls=%async_computation.10 | async-start | bytes 21233664 | tf_op jit(solution)/shard_map/all_gather | solution.py:310
  51.0 386.0 %reduce-scatter.19.cloned.1.call-start = ((), (), s32[]{:S(2)}) async-start(), calls=%async_computation.11 | async-start | bytes 442368 | tf_op jit(solution)/shard_map/reduce_scatter | solution.py:372
  51.0 94.9 %copy-start.77 = (s32[1,1,256,1]{2,3,1,0:T(1,128)}, s32[1,1,256,1]{2,3,1,0:T(1,128)S(1)}, u32[]{:S(2)}) copy-start(s32[1,1,256,1]{2,3,1,0:T(1,128)S(1)} %get-tuple-element.205) | copy-start | bytes 3076
  51.1 94.9 %copy-start.81 = (s32[1,1,256,1]{2,3,1,0:T(1,128)}, s32[1,1,256,1]{2,3,1,0:T(1,128)S(1)}, u32[]{:S(2)}) copy-start(s32[1,1,256,1]{2,3,1,0:T(1,128)S(1)} %get-tuple-element.206) | copy-start | bytes 3076
  53.6 92.3 %copy-start.137 = (s32[16]{0:T(128)}, s32[16]{0:T(128)S(1)}, u32[]{:S(2)}) copy-start(s32[16]{0:T(128)S(1)} %get-tuple-element.210) | copy-start | bytes 196
  78.7 67.2 %copy-start.96 = (f32[768]{0:T(1024)}, f32[768]{0:T(1024)S(1)}, u32[]{:S(2)}) copy-start(f32[768]{0:T(1024)S(1)} %get-tuple-element.138) | copy-start | bytes 9220
  84.2 61.7 %copy-start.127 = (f32[256]{0:T(256)}, f32[256]{0:T(256)S(1)}, u32[]{:S(2)}) copy-start(f32[256]{0:T(256)S(1)} %add_rsqrt_fusion.3) | copy-start | bytes 3076
  407.8 262.9 %all-gather.14.cloned.1.call-start = ((), (), s32[]{:S(2)}) async-start(), calls=%async_computation.12 | async-start | bytes 3538944 | tf_op jit(solution)/shard_map/all_gather | solution.py:404
  508.3 12.4 copy-start.115
  529.4 172.9 %reduce-scatter.25.cloned.1.call-start = ((), (), s32[]{:S(2)}) async-start(), calls=%async_computation.18 | async-start | bytes 6635520
  555.8 299.3 %reduce-scatter.27.cloned.1.call-start = ((), (), s32[]{:S(2)}) async-start(), calls=%async_computation.19 | async-start | bytes 21233664
  668.6 314.6 %reduce-scatter.21.cloned.1.call-start = ((), (), s32[]{:S(2)}) async-start(), calls=%async_computation.13 | async-start | bytes 3538944 | tf_op jit(solution)/shard_map/reduce_scatter | solution.py:322
  670.7 20.0 copy-start.34
  670.7 20.0 copy-start.94
  670.7 20.0 copy-start.105
  670.7 20.0 copy-start.120
  705.1 247.7 %copy-start.16 = (bf16[5,96,768]{1,2,0:T(8,128)(2,1)}, bf16[5,96,768]{1,2,0:T(8,128)(2,1)S(1)}, u32[]{:S(2)}) copy-start(bf16[5,96,768]{1,2,0:T(8,128)(2,1)S(1)} %copy.298) | copy-start | bytes 2211844
  867.4 93.1 %copy-start.4 = (bf16[2,2,768,384]{3,2,0,1:T(8,128)(2,1)}, bf16[2,2,768,384]{3,2,0,1:T(8,128)(2,1)S(1)}, u32[]{:S(2)}) copy-start(bf16[2,2,768,384]{3,2,0,1:T(8,128)(2,1)S(1)} %copy.300) | copy-start | bytes 7077892
  896.1 75.2 %copy-start.62 = (f32[6,768]{1,0:T(8,128)}, f32[6,768]{1,0:T(8,128)S(1)}, u32[]{:S(2)}) copy-start(f32[6,768]{1,0:T(8,128)S(1)} %get-tuple-element.148) | copy-start | bytes 55300
  927.3 13.6 copy-start.122
  944.4 101.5 %all-gather.16.cloned.1.call-start = ((), (), s32[]{:S(2)}) async-start(), calls=%async_computation.14 | async-start | bytes 6635520 | tf_op jit(solution)/shard_map/all_gather | solution.py:309
  960.4 254.5 %all-gather.18.cloned.1.call-start = ((), (), s32[]{:S(2)}) async-start(), calls=%async_computation.15 | async-start | bytes 21233664 | tf_op jit(solution)/shard_map/all_gather | solution.py:310
  968.9 367.8 %reduce-scatter.23.cloned.1.call-start = ((), (), s32[]{:S(2)}) async-start(), calls=%async_computation.16 | async-start | bytes 442368 | tf_op jit(solution)/shard_map/reduce_scatter | solution.py:372
  970.0 79.4 %copy-start.133 = (f32[6]{0:T(128)}, f32[6]{0:T(128)S(1)}, u32[]{:S(2)}) copy-start(f32[6]{0:T(128)S(1)} %compare_select_fusion.12) | copy-start | bytes 76
  972.6 76.7 %copy-start.98 = (f32[768]{0:T(1024)}, f32[768]{0:T(1024)S(1)}, u32[]{:S(2)}) copy-start(f32[768]{0:T(1024)S(1)} %get-tuple-element.134) | copy-start | bytes 9220
  984.4 65.0 %copy-start.129 = (f32[256]{0:T(256)}, f32[256]{0:T(256)S(1)}, u32[]{:S(2)}) copy-start(f32[256]{0:T(256)S(1)} %add_rsqrt_fusion.1) | copy-start | bytes 3076
  1054.4 41.9 %copy-start.78 = (s32[1,1,256,1]{2,3,1,0:T(1,128)S(1)}, s32[1,1,256,1]{2,3,1,0:T(1,128)}, u32[]{:S(2)}) copy-start(s32[1,1,256,1]{2,3,1,0:T(1,128)} %copy-done.77) | copy-start | bytes 3076
  1307.6 262.8 %all-gather.20.cloned.1.call-start = ((), (), s32[]{:S(2)}) async-start(), calls=%async_computation.17 | async-start | bytes 3538944 | tf_op jit(solution)/shard_map/all_gather | solution.py:404
  1407.9 12.4 copy-start.117
  1429.3 172.8 %reduce-scatter.29.cloned.1.call-start = ((), (), s32[]{:S(2)}) async-start(), calls=%async_computation.20 | async-start | bytes 6635520
  1455.7 299.8 %reduce-scatter.31.cloned.1.call-start = ((), (), s32[]{:S(2)}) async-start(), calls=%async_computation.21 | async-start | bytes 21233664
  1568.6 471.7 %all-reduce.5.cloned.1.call-start = ((), (), s32[]{:S(2)}) async-start(), calls=%async_computation.22 | async-start | bytes 19021824 | tf_op jit(solution)/shard_map/psum | solution.py:440
  1570.4 20.1 copy-start.36
  1570.4 20.1 copy-start.95
  1570.4 20.1 copy-start.108
  1570.4 20.0 copy-start.121
  1604.8 150.8 %copy-start.18 = (bf16[5,96,768]{1,2,0:T(8,128)(2,1)}, bf16[5,96,768]{1,2,0:T(8,128)(2,1)S(1)}, u32[]{:S(2)}) copy-start(bf16[5,96,768]{1,2,0:T(8,128)(2,1)S(1)} %copy.302) | copy-start | bytes 2211844
  1762.0 11.1 copy-start.132
  1762.0 39.3 %copy-start.6 = (f32[5,96,768]{1,2,0:T(8,128)S(1)}, f32[5,96,768]{1,2,0:T(8,128)}, u32[]{:S(2)}) copy-start(f32[5,96,768]{1,2,0:T(8,128)} %copy.241) | copy-start | bytes 4423684
  1762.1 39.3 %copy-start.17 = (bf16[5,96,768]{1,2,0:T(8,128)(2,1)S(1)}, bf16[5,96,768]{1,2,0:T(8,128)(2,1)}, u32[]{:S(2)}) copy-start(bf16[5,96,768]{1,2,0:T(8,128)(2,1)} %copy-done.16) | copy-start | bytes 2211844
  1801.4 20.5 slice-start
  1808.1 13.9 slice-start.1
  1808.1 13.9 slice-start.2
  1866.4 24.4 %copy-start.91 = (f32[6,768]{1,0:T(8,128)S(1)}, f32[6,768]{1,0:T(8,128)}, u32[]{:S(2)}) copy-start(f32[6,768]{1,0:T(8,128)} %param.42) | copy-start | bytes 55300
  (113 other events, 384.8 us)
Sparse Core Ops, SparseCore 0:
  44.3 38.7 reduce-scatter.16
  85.2 60.6 all-gather.9
  148.1 166.8 all-gather.11
  407.9 28.9 reduce-scatter.18
  529.5 36.5 all-gather.13
  569.0 64.9 reduce-scatter.24
  668.8 186.2 reduce-scatter.26
  944.6 38.6 reduce-scatter.20
  985.4 60.5 all-gather.15
  1048.0 166.8 all-gather.17
  1307.7 28.8 reduce-scatter.22
  1429.4 37.2 all-gather.19
  1469.7 64.9 reduce-scatter.28
  1568.7 186.7 reduce-scatter.30
  1850.5 189.7 all-reduce.4
where the time goes:
time: 2110 us; the launch traced here: 2090 us
  waiting for transfers between devices  869 us (41%)
  local copies, waits for them, and re-layouts  526 us (25%)
  other arithmetic  278 us (13%)
  matrix products  201 us (10%)
  blocking collectives  189 us (9%)
  between operations  24.1 us (1%)
    unnamed x326, local copies, waits for them, and re-layouts  312 us
    unnamed x19, waiting for transfers between devices  296 us
    all_gather x2, waiting for transfers between devices, shards(): lax.all_gather(expert_w.astype(jnp.bfloat16), 'fsdp', axis=3, tiled=True)  232 us
    psum x1, waiting for transfers between devices, shards(): lax.psum(for_sending(deltas), 'grp')  149 us
    all_gather x2, waiting for transfers between devices, shards(): lax.all_gather(attn_w.astype(jnp.bfloat16), 'fsdp', axis=1, tiled=True)  123 us
    scatter x2, local copies, waits for them, and re-layouts, expert_backward(): jnp.zeros((EXPERTS, CAP, width_model), jnp.bfloat16).at[route_ids, slot_ids]  74.9 us
    scatter x2, local copies, waits for them, and re-layouts, layer_forward(): buffer_in = jnp.zeros((EXPERTS, CAP, width_model), jnp.bfloat16).at[route...  74.8 us
    reduce_scatter x2, waiting for transfers between devices, shards(): lax.psum_scatter(drows.astype(jnp.bfloat16), 'fsdp', scatter_dimension=1,...  55.4 us
  transfers between devices with their start and end apart: 15, of which 11 were waited for; matrix products, arithmetic and copies ran while one was open for 25% of the time, Pallas kernels for 0%

commit v1 on v0

v1 whole, which is shorter than its diff:
```python
import math

import jax
import jax.numpy as jnp
from jax import lax
from jax.sharding import PartitionSpec as P

D = 768
HEADS = 12
HEAD_DIM = 64
EXPERTS = 2
STEP0 = 5
CAP = 192


HIGH = lax.Precision.HIGHEST
EPSILON = 1e-06
ATTN_GAIN = 8.0
SECOND_WEIGHT = 0.3
BETA_ONE = 0.9
BETA_TWO = 0.95
ADAM_EPS = 1e-08
DECAY = 0.1
LR_EMBED = 0.5
LR_MATRIX = 0.012
LR_GAIN = 0.3
LR_ROUTER = 0.012
OUTER_RATE = 0.7
OUTER_MOMENTUM = 0.9


def for_sending(value):

    def short(part):
        return part.astype(jnp.bfloat16) if part.dtype == jnp.float32 else part

    return jax.tree.map(short, value)


def smooth_act(values):
    return jax.nn.gelu(values, approximate=True)


def norm_apply(x, gain_row):
    factor = lax.rsqrt(jnp.mean(x * x, axis=-1, keepdims=True) + EPSILON)
    return (x * factor * gain_row, factor)


def norm_back(x, factor, gain_row, upstream):
    normed = x * factor
    gain_grad = jnp.sum(upstream * normed, axis=0)
    scaled = upstream * gain_row
    return (
        factor * (scaled - normed * jnp.mean(scaled * normed, axis=-1, keepdims=True)),
        gain_grad,
    )


def rows_forward(attn_low, vector_w, x_embed, seg_ids, pick_ids):
    a_float, a_factor = norm_apply(x_embed, vector_w[0])
    a = a_float.astype(jnp.bfloat16)
    a_rows = a[pick_ids]
    q = jnp.dot(a_rows, attn_low[0], preferred_element_type=jnp.float32).astype(jnp.bfloat16)
    k = jnp.dot(a, attn_low[1], preferred_element_type=jnp.float32).astype(jnp.bfloat16)
    v = jnp.dot(a, attn_low[2], preferred_element_type=jnp.float32).astype(jnp.bfloat16)
    places = jnp.arange(x_embed.shape[0])
    allowed = (places[None, :] <= pick_ids[:, None]) & (
        seg_ids[pick_ids][:, None] == seg_ids[None, :]
    )
    count = pick_ids.shape[0]
    head_of = jnp.arange(D) // HEAD_DIM
    head_mask = (head_of[None, None, :] == jnp.arange(HEADS)[:, None, None])
    q_wide = jnp.where(head_mask, q[None], 0).reshape(HEADS * count, D)
    scores = jnp.einsum("rd,td->rt", q_wide, k, preferred_element_type=jnp.float32) * HEAD_DIM ** (-0.5)
    allowed = jnp.tile(allowed, (HEADS, 1))
    scores = jnp.where(allowed, scores, -1e30)
    exponent = jnp.exp(scores - jnp.max(scores, axis=-1, keepdims=True))
    probs = exponent / jnp.sum(exponent, axis=-1, keepdims=True)
    spread = jnp.dot(probs.astype(jnp.bfloat16), v, preferred_element_type=jnp.float32)
    o = jnp.sum(jnp.where(head_mask, spread.reshape(HEADS, count, D), 0.0), axis=0).astype(jnp.bfloat16)
    x_attn = x_embed[pick_ids] + ATTN_GAIN * jnp.dot(o, attn_low[3], preferred_element_type=jnp.float32)
    return x_attn, (a_factor, a, a_rows, q_wide, k, v, probs, o, head_mask)


def rows_backward(attn_low, vector_w, x_embed, kept, dx_attn, pick_ids):
    a_factor, a, a_rows, q_wide, k, v, probs, o, head_mask = kept
    count = pick_ids.shape[0]
    dbranch = dx_attn.astype(jnp.bfloat16)
    dwout = ATTN_GAIN * jnp.dot(o.T, dbranch, preferred_element_type=jnp.float32)
    do = (ATTN_GAIN * jnp.dot(dbranch, attn_low[3].T, preferred_element_type=jnp.float32)).astype(jnp.bfloat16)
    do_wide = jnp.where(head_mask, do[None], 0).reshape(HEADS * count, D)
    dprobs = jnp.einsum("rd,td->rt", do_wide, v, preferred_element_type=jnp.float32)
    dscores = (probs * (dprobs - jnp.sum(probs * dprobs, axis=-1, keepdims=True))).astype(jnp.bfloat16)
    factor_qk = HEAD_DIM ** (-0.5)
    dq = jnp.dot(dscores, k, preferred_element_type=jnp.float32).reshape(HEADS, count, D)
    dq = (jnp.sum(jnp.where(head_mask, dq, 0.0), axis=0) * factor_qk).astype(jnp.bfloat16)
    dk = (jnp.dot(dscores.T, q_wide, preferred_element_type=jnp.float32) * factor_qk).astype(jnp.bfloat16)
    dv = jnp.dot(probs.astype(jnp.bfloat16).T, do_wide, preferred_element_type=jnp.float32).astype(jnp.bfloat16)
    dlayer = jnp.stack(
        [
            jnp.dot(a_rows.T, dq, preferred_element_type=jnp.float32),
            jnp.dot(a.T, dk, preferred_element_type=jnp.float32),
            jnp.dot(a.T, dv, preferred_element_type=jnp.float32),
            dwout,
        ]
    )
    places = jnp.arange(x_embed.shape[0])
    pick_mask = (places[:, None] == pick_ids[None, :]).astype(jnp.float32)
    dinput = jnp.dot(dk, attn_low[1].T, preferred_element_type=jnp.float32)
    dinput = dinput + jnp.dot(dv, attn_low[2].T, preferred_element_type=jnp.float32)
    dq_in = jnp.dot(dq, attn_low[0].T, preferred_element_type=jnp.float32)
    dinput = dinput + jnp.dot(pick_mask, dq_in, precision=HIGH)
    dx, gain_attn = norm_back(x_embed, a_factor, vector_w[0], dinput)
    return dx + jnp.dot(pick_mask, dx_attn, precision=HIGH), dlayer, gain_attn


def gather_rows(value, axis=0):
    return lax.all_gather(value, "fsdp", axis=axis, tiled=True)


def scatter_rows(value, axis=0):
    return lax.psum_scatter(
        value.astype(jnp.bfloat16), "fsdp", scatter_dimension=axis, tiled=True
    ).astype(jnp.float32)


def adam_update(weight, first_moment, second, gradient, step_float, rate_here, decay_here):
    first_new = BETA_ONE * first_moment + (1.0 - BETA_ONE) * gradient
    second_new = BETA_TWO * second + (1.0 - BETA_TWO) * gradient * gradient
    first_hat = first_new / (1.0 - BETA_ONE**step_float)
    second_hat = second_new / (1.0 - BETA_TWO**step_float)
    weight_new = weight - rate_here * (
        first_hat / (jnp.sqrt(second_hat) + ADAM_EPS) + decay_here * weight
    )
    return (weight_new, first_new, second_new)


def shards(
    tokens,
    routes,
    segments,
    loss_pos,
    embedding,
    embedding_first,
    embedding_second,
    embedding_outer,
    attention,
    attention_first,
    attention_second,
    attention_outer,
    experts,
    experts_first,
    experts_second,
    experts_outer,
    vectors,
    vectors_first,
    vectors_second,
    vectors_outer,
):
    inner_count = tokens.shape[0]
    vocab_shard = embedding.shape[0]
    vocab_start = lax.axis_index("fsdp") * vocab_shard
    group_count = lax.axis_size("grp")
    row_total = lax.axis_size("fsdp") * loss_pos.shape[2]
    threshold = 0.05 / math.sqrt(row_total)
    logit_scale = 2.0 * D ** (-0.5)
    all_ids = lax.all_gather(tokens[:, 0, :], "fsdp", axis=1, tiled=True)
    vocab_places = jnp.arange(vocab_shard)
    head_weights = jnp.array([1.0, SECOND_WEIGHT], jnp.float32)
    vector_rates = jnp.where(jnp.arange(vectors.shape[0])[:, None] < 4, LR_GAIN, LR_ROUTER)
    rate_list = (LR_EMBED, LR_MATRIX, LR_MATRIX, vector_rates)
    decay_list = (DECAY, DECAY, DECAY, 0.0)
    weights_now = (embedding, attention, experts, vectors)
    first_now = (embedding_first[0], attention_first[0], experts_first[0], vectors_first[0])
    second_now = (embedding_second[0], attention_second[0], experts_second[0], vectors_second[0])
    loss_list = []
    norm_list = []
    for inner_step in range(inner_count):
        embed_w, attn_w, expert_w, vector_w = weights_now
        embed_low = embed_w.astype(jnp.bfloat16)
        attn_low = lax.all_gather(attn_w.astype(jnp.bfloat16), "fsdp", axis=1, tiled=True)
        expert_low = expert_w.astype(jnp.bfloat16)
        ids_group = all_ids[inner_step]
        ids_local = tokens[inner_step, 0]
        seg_ids = segments[inner_step, 0]
        route_ids = routes[inner_step, 0, :, 0]
        pick_ids = loss_pos[inner_step, 0]
        chosen = ids_group - vocab_start
        inside = (chosen >= 0) & (chosen < vocab_shard)
        looked = jnp.take(embed_low, jnp.clip(chosen, 0, vocab_shard - 1), axis=0).astype(
            jnp.float32
        )
        x_embed = lax.psum_scatter(
            jnp.where(inside[:, None], looked, 0.0).astype(jnp.bfloat16),
            "fsdp",
            scatter_dimension=0,
            tiled=True,
        ).astype(jnp.float32)
        x_attn, kept = rows_forward(attn_low, vector_w, x_embed, seg_ids, pick_ids)
        b, b_factor = norm_apply(x_attn, vector_w[1])
        router_probs = jax.nn.softmax(jnp.dot(b, vector_w[4:].T, precision=HIGH), axis=-1)
        row_routes = route_ids[pick_ids]
        onehot = (row_routes[:, None] == jnp.arange(EXPERTS)[None, :]).astype(jnp.float32)
        gating = jnp.sum(router_probs * onehot, axis=1)
        b_all = gather_rows(b.astype(jnp.bfloat16))
        routes_all = gather_rows(row_routes)
        route_mask = routes_all[None, :, None] == jnp.arange(EXPERTS)[:, None, None]
        hidden_pre = jnp.einsum("cd,edf->ecf", b_all, expert_low[:, 0], preferred_element_type=jnp.float32)
        hidden_act = jnp.where(route_mask, smooth_act(hidden_pre), 0.0).astype(jnp.bfloat16)
        y_part = jnp.einsum("ecf,edf->cd", hidden_act, expert_low[:, 1], preferred_element_type=jnp.float32)
        returned = scatter_rows(y_part)
        z_rows = x_attn + gating[:, None] * returned
        first_float, first_factor = norm_apply(z_rows, vector_w[2])
        first_rows = first_float.astype(jnp.bfloat16)
        middle = jnp.dot(first_rows, attn_low[4], preferred_element_type=jnp.float32)
        second_float, second_factor = norm_apply(middle, vector_w[3])
        targets = jnp.stack([ids_local[pick_ids + 1], ids_local[pick_ids + 2]])
        rows_all, targets_all = (
            lax.all_gather(
                jnp.stack([first_rows, second_float.astype(jnp.bfloat16)]),
                "fsdp",
                axis=1,
                tiled=True,
            ),
            lax.all_gather(targets, "fsdp", axis=1, tiled=True),
        )
        logits = (
            jnp.einsum("jrd,vd->jrv", rows_all, embed_low, preferred_element_type=jnp.float32)
            * logit_scale
        )
        relative = targets_all - vocab_start
        onehot_target = (vocab_places[None, None, :] == relative[:, :, None]).astype(jnp.float32)
        target_part = jnp.sum(onehot_target * logits, axis=-1)
        local_top = jnp.max(logits, axis=-1)
        local_sum = jnp.sum(jnp.exp(logits - local_top[:, :, None]), axis=-1)
        parts = lax.all_gather(jnp.stack([local_top, local_sum, target_part]), "fsdp")
        row_top = jnp.max(parts[:, 0], axis=0)
        sum_exp = jnp.sum(parts[:, 1] * jnp.exp(parts[:, 0] - row_top), axis=0)
        target_logit = jnp.sum(parts[:, 2], axis=0)
        logsum = row_top + jnp.log(sum_exp)
        loss_list.append(jnp.sum(head_weights[:, None] * (logsum - target_logit)) / row_total)
        dlogits = (
            (jnp.exp(logits - logsum[:, :, None]) - onehot_target)
            * (head_weights / row_total)[:, None, None]
        ).astype(jnp.bfloat16)
        dembed = (
            jnp.einsum("jrv,jrd->vd", dlogits, rows_all, preferred_element_type=jnp.float32)
            * logit_scale
        )
        drows = (
            jnp.einsum("jrv,vd->jrd", dlogits, embed_low, preferred_element_type=jnp.float32)
            * logit_scale
        )
        drows_own = lax.psum_scatter(
            drows.astype(jnp.bfloat16), "fsdp", scatter_dimension=1, tiled=True
        ).astype(jnp.float32)
        dmiddle, gain_mtp = norm_back(middle, second_factor, vector_w[3], drows_own[1])
        dmiddle_low = dmiddle.astype(jnp.bfloat16)
        dsecond_proj = jnp.dot(first_rows.T, dmiddle_low, preferred_element_type=jnp.float32)
        dfirst = drows_own[0] + jnp.dot(
            dmiddle_low, attn_low[4].T, preferred_element_type=jnp.float32
        )
        dz_rows, gain_final = norm_back(z_rows, first_factor, vector_w[2], dfirst)
        dgating = jnp.sum(dz_rows * returned, axis=1)
        dy_all = gather_rows((gating[:, None] * dz_rows).astype(jnp.bfloat16))
        dy_masked = jnp.where(route_mask, dy_all[None], 0)
        down_grad = jnp.einsum("ecf,ecd->edf", hidden_act, dy_masked, preferred_element_type=jnp.float32)
        dhidden = jnp.einsum("ecd,edf->ecf", dy_masked, expert_low[:, 1], preferred_element_type=jnp.float32)
        unused, act_back = jax.vjp(smooth_act, hidden_pre)
        dhidden_pre = act_back(dhidden)[0].astype(jnp.bfloat16)
        up_grad = jnp.einsum("cd,ecf->edf", b_all, dhidden_pre, preferred_element_type=jnp.float32)
        dexpert = jnp.stack([up_grad, down_grad], axis=1)
        db_part = jnp.einsum("ecf,edf->cd", dhidden_pre, expert_low[:, 0], preferred_element_type=jnp.float32)
        dnormed = scatter_rows(db_part)
        prob_grad = onehot * dgating[:, None]
        dlogit = router_probs * (prob_grad - jnp.sum(router_probs * prob_grad, axis=1, keepdims=True))
        drouter = jnp.dot(dlogit.T, b, precision=HIGH)
        dnormed = dnormed + jnp.dot(dlogit, vector_w[4:], precision=HIGH)
        dx_part, gain_ffn = norm_back(x_attn, b_factor, vector_w[1], dnormed)
        dx_embed, dlayer, gain_attn = rows_backward(
            attn_low, vector_w, x_embed, kept, dz_rows + dx_part, pick_ids
        )
        dattn = scatter_rows(jnp.concatenate([dlayer, dsecond_proj[None]], axis=0), axis=1)
        gather_chosen = ids_group - vocab_start
        gather_inside = (gather_chosen >= 0) & (gather_chosen < vocab_shard)
        seg_index = jnp.where(gather_inside, gather_chosen, vocab_shard)
        added = jax.ops.segment_sum(
            lax.all_gather(dx_embed.astype(jnp.bfloat16), "fsdp", axis=0, tiled=True).astype(
                jnp.float32
            ),
            seg_index,
            num_segments=vocab_shard + 1,
        )
        dembed = dembed + added[:vocab_shard]
        dvector_part = jnp.concatenate(
            [jnp.stack([gain_attn, gain_ffn, gain_final, gain_mtp]), drouter], axis=0
        )
        squares = jnp.sum(dembed * dembed) + jnp.sum(dattn * dattn) + jnp.sum(dexpert * dexpert)
        dvector, squares_all = lax.psum((dvector_part, squares), "fsdp")
        norm_value = jnp.sqrt(squares_all + jnp.sum(dvector * dvector))
        norm_list.append(norm_value)
        factor = jnp.minimum(1.0, threshold / norm_value)
        gradients = (dembed * factor, dattn * factor, dexpert * factor, dvector * factor)
        step_float = float(STEP0 + inner_step + 1)
        results = [
            adam_update(
                weights_now[k],
                first_now[k],
                second_now[k],
                gradients[k],
                step_float,
                rate_list[k],
                decay_list[k],
            )
            for k in range(4)
        ]
        weights_now = tuple((element[0] for element in results))
        first_now = tuple((element[1] for element in results))
        second_now = tuple((element[2] for element in results))
    masters = (embedding, attention, experts, vectors)
    outers = (embedding_outer, attention_outer, experts_outer, vectors_outer)
    deltas = tuple((master - current for master, current in zip(masters, weights_now)))
    summed = jax.tree.map(
        lambda part: part.astype(jnp.float32), lax.psum(for_sending(deltas), "grp")
    )
    new_outer = []
    new_master = []
    for k in range(4):
        delta_mean = summed[k] / group_count
        outer_new = OUTER_MOMENTUM * outers[k] + delta_mean
        new_outer.append(outer_new)
        new_master.append(masters[k] - OUTER_RATE * (delta_mean + OUTER_MOMENTUM * outer_new))
    return (
        jnp.stack(loss_list)[None],
        jnp.stack(norm_list)[None],
        first_now[0][None],
        second_now[0][None],
        new_master[0],
        new_outer[0],
        new_master[0].astype(jnp.bfloat16),
        first_now[1][None],
        second_now[1][None],
        new_master[1],
        new_outer[1],
        new_master[1].astype(jnp.bfloat16),
        first_now[2][None],
        second_now[2][None],
        new_master[2],
        new_outer[2],
        new_master[2].astype(jnp.bfloat16),
        gradients[3][None],
        first_now[3][None],
        second_now[3][None],
        new_master[3],
        new_outer[3],
    )


def solution(mesh):
    return jax.shard_map(
        shards,
        mesh=mesh,
        in_specs=(
            P(None, "grp", "fsdp"),
            P(None, "grp", "fsdp", None),
            P(None, "grp", "fsdp"),
            P(None, "grp", "fsdp"),
            P("fsdp", None),
            P("grp", "fsdp", None),
            P("grp", "fsdp", None),
            P("fsdp", None),
            P(None, "fsdp", None),
            P("grp", None, "fsdp", None),
            P("grp", None, "fsdp", None),
            P(None, "fsdp", None),
            P(None, None, None, "fsdp"),
            P("grp", None, None, None, "fsdp"),
            P("grp", None, None, None, "fsdp"),
            P(None, None, None, "fsdp"),
            P(),
            P("grp", None, None),
            P("grp", None, None),
            P(),
        ),
        out_specs=(
            P("grp", None),
            P("grp", None),
            P("grp", "fsdp", None),
            P("grp", "fsdp", None),
            P("fsdp", None),
            P("fsdp", None),
            P("fsdp", None),
            P("grp", None, "fsdp", None),
            P("grp", None, "fsdp", None),
            P(None, "fsdp", None),
            P(None, "fsdp", None),
            P(None, "fsdp", None),
            P("grp", None, None, None, "fsdp"),
            P("grp", None, None, None, "fsdp"),
            P(None, None, None, "fsdp"),
            P(None, None, None, "fsdp"),
            P(None, None, None, "fsdp"),
            P("grp", None, None),
            P("grp", None, None),
            P("grp", None, None),
            P(),
            P(),
        ),
        check_vma=False,
    )
```

time: 2110 us -> 1260 us (0.60)
  local copies, waits for them, and re-layouts: 526 us -> 106 us
  waiting for transfers between devices: 869 us -> 536 us
  matrix products: 201 us -> 127 us
  other arithmetic: 278 us -> 229 us
  blocking collectives: 189 us -> 226 us
    unnamed x19 -> x15, waiting for transfers between devices: 296 us -> 0.25 us
    unnamed x326 -> x292, local copies, waits for them, and re-layouts: 312 us -> 62.6 us
    all_gather x2 -> x0, waiting for transfers between devices: 232 us -> none  [shards(): lax.all_gather(expert_w.astype(jnp.bfloat16), 'fsdp', axis=3, tiled=True)]
    reduce_scatter x0 -> x6, waiting for transfers between devices: none -> 186 us  [scatter_rows(): lax.psum_scatter(value.astype(jnp.bfloat16), 'fsdp', scatter_dimension=ax...]
    scatter x4 -> x0, local copies, waits for them, and re-layouts: 150 us -> none  [the longest x2 74.9 us: expert_backward(): jnp.zeros((EXPERTS, CAP, width_model), jnp.bfloat16).at[route_ids, slot_ids]]
    all_gather x0 -> x6, blocking collectives: none -> 86.8 us  [the longest x4 58.4 us: gather_rows(): return lax.all_gather(value, 'fsdp', axis=axis, tiled=True)]
    dot_general x42 -> x58, matrix products: 136 us -> 78.2 us  [the longest x2 4.2 us: rows_backward(): jnp.dot(a.T, dv, preferred_element_type=jnp.float32)]
    psum x3 -> x0, blocking collectives: 54.8 us -> none  [shards(): lax.psum((jnp.sum(jnp.exp(logits - row_top[:, :, None]), axis=-1), target...]
  transfers between devices with their start and end apart: 15 -> 15, of which waited for: 11 -> 15; matrix products, arithmetic and copies ran while one was open for 25% -> 15% of each run, Pallas kernels for 0% -> 0%
where the time goes in v1:
time: 1260 us; the launch traced here: 1250 us
  waiting for transfers between devices  536 us (43%)
  other arithmetic  229 us (18%)
  blocking collectives  226 us (18%)
  matrix products  127 us (10%)
  local copies, waits for them, and re-layouts  106 us (8%)
  between operations  25 us (2%)
    reduce_scatter x6, waiting for transfers between devices, scatter_rows(): lax.psum_scatter(value.astype(jnp.bfloat16), 'fsdp', scatter_dimension=ax...  186 us
    psum x1, waiting for transfers between devices, shards(): lax.psum(for_sending(deltas), 'grp')  135 us
    all_gather x2, waiting for transfers between devices, shards(): lax.all_gather(attn_w.astype(jnp.bfloat16), 'fsdp', axis=1, tiled=True)  111 us
    unnamed x292, local copies, waits for them, and re-layouts  62.6 us
    all_gather x4, blocking collectives, gather_rows(): return lax.all_gather(value, 'fsdp', axis=axis, tiled=True)  58.4 us
    reduce_scatter x2, waiting for transfers between devices, shards(): lax.psum_scatter(drows.astype(jnp.bfloat16), 'fsdp', scatter_dimension=1,...  57.9 us
    psum x2, blocking collectives, shards(): dvector, squares_all = lax.psum((dvector_part, squares), 'fsdp')  52.9 us
    convert_element_type x3, other arithmetic, short(): return part.astype(jnp.bfloat16) if part.dtype == jnp.float32 else part  43.7 us
  transfers between devices with their start and end apart: 15, of which 15 were waited for; matrix products, arithmetic and copies ran while one was open for 15% of the time, Pallas kernels for 0%

profile of v1, /device:TPU:0, one launch (start us, length us, event | category | flops | bytes accessed | tf_op | source)
XLA Modules:
  0.0 1250.7 jit_solution(10836874591001525437)
XLA Ops:
  7.2 13.7 %all-gather = s32[2,1,2048]{2,1,0:T(1,128)S(1)} all-gather(s32[2,1,256]{2,1,0:T(1,128)} %param.23), channel_id=2, replica_groups=mesh['grp'=4,'fsdp'=8] {'fsdp'}, dimensions={2}, use_global_device_ids=true | all-gather | bytes 18432 | tf_op jit(solution)/shard_map/all_gather | solution.py:167
  22.2 7.8 convert_element_type.265
  30.0 13.6 %gather_fusion.12 = bf16[2048,768]{1,0:T(8,128)(2,1)} fusion(bf16[4016,768]{1,0:T(8,128)(2,1)} %convert_element_type.265, s32[2048]{0:T(1024)S(1)} %get-tuple-element.245), kind=kCustom, calls=%fused_computation.clone | custom fusion | bytes 6299648 | tf_op jit(solution)/shard_map/jit(_take)/gather | solution.py:190
  55.4 8.9 all-gather.5
  64.3 10.2 all-gather.6
  77.0 7.3 all-reduce.2
  92.3 56.7 %all-gather.12.cloned.1.call-done = bf16[5,768,768]{2,1,0:T(8,128)(2,1)} async-done(((bf16[5,96,768]{2,1,0:T(8,128)(2,1)}), bf16[5,768,768]{2,1,0:T(8,128)(2,1)}) %all-gather.12.cloned.1.call-update) | async-done | bytes 5898256 | tf_op jit(solution)/shard_map/all_gather | solution.py:181
  157.2 14.1 %all_gather.60 = bf16[128,768]{1,0:T(8,128)(2,1)S(1)} all-gather(bf16[16,768]{1,0:T(8,128)(2,1)S(1)} %multiply_convert_fusion.19), channel_id=1, replica_groups=mesh['grp'=4,'fsdp'=8] {'fsdp'}, dimensions={0}, use_global_device_ids=true | all-gather | bytes 221184 | tf_op jit(solution)/shard_map/all_gather | solution.py:118
  174.0 28.7 %reduce-scatter.13.cloned.1.call-done = bf16[16,768]{1,0:T(8,128)(2,1)} async-done(((bf16[128,768]{1,0:T(8,128)(2,1)}), bf16[16,768]{1,0:T(8,128)(2,1)}) %reduce-scatter.13.cloned.1.call-update) | async-done | bytes 24592 | tf_op jit(solution)/shard_map/reduce_scatter | solution.py:122
  205.7 14.5 %all_gather.61 = bf16[2,128,768]{2,1,0:T(8,128)(2,1)S(1)} all-gather(bf16[2,16,768]{2,1,0:T(8,128)(2,1)S(1)} %pad_maximum_fusion.2), channel_id=1, replica_groups=mesh['grp'=4,'fsdp'=8] {'fsdp'}, dimensions={1}, use_global_device_ids=true | all-gather | bytes 442368 | tf_op jit(solution)/shard_map/all_gather | solution.py:219
  225.4 14.1 %all-gather.2 = f32[24,2,128]{2,1,0:T(2,128)S(1)} all-gather(f32[3,2,128]{2,1,0:T(2,128)S(1)} %pad_maximum_fusion.4), channel_id=4, replica_groups=mesh['grp'=4,'fsdp'=8] {'fsdp'}, dimensions={0}, use_global_device_ids=true | all-gather | bytes 27648 | tf_op jit(solution)/shard_map/all_gather | solution.py:236
  243.0 28.9 %reduce-scatter.15.cloned.1.call-done = bf16[2,16,768]{2,1,0:T(8,128)(2,1)} async-done(((bf16[2,128,768]{2,1,0:T(8,128)(2,1)}), bf16[2,16,768]{2,1,0:T(8,128)(2,1)}) %reduce-scatter.15.cloned.1.call-update) | async-done | bytes 49168 | tf_op jit(solution)/shard_map/reduce_scatter | solution.py:254
  276.3 15.1 %all_gather.65 = bf16[128,768]{1,0:T(8,128)(2,1)} all-gather(bf16[16,768]{1,0:T(8,128)(2,1)S(1)} %multiply_convert_fusion.14), channel_id=1, replica_groups=mesh['grp'=4,'fsdp'=8] {'fsdp'}, dimensions={0}, use_global_device_ids=true | all-gather | bytes 221184 | tf_op jit(solution)/shard_map/all_gather | solution.py:118
  296.8 28.6 %reduce-scatter.17.cloned.1.call-done = bf16[16,768]{1,0:T(8,128)(2,1)} async-done(((bf16[128,768]{1,0:T(8,128)(2,1)}), bf16[16,768]{1,0:T(8,128)(2,1)}) %reduce-scatter.17.cloned.1.call-update) | async-done | bytes 24592 | tf_op jit(solution)/shard_map/reduce_scatter | solution.py:122
  356.0 21.1 %all-gather.14.cloned.1.call-done = bf16[2048,768]{1,0:T(8,128)(2,1)} async-done(((bf16[256,768]{1,0:T(8,128)(2,1)}), bf16[2048,768]{1,0:T(8,128)(2,1)}) %all-gather.14.cloned.1.call-update) | async-done | bytes 3145744 | tf_op jit(solution)/shard_map/all_gather | solution.py:288
  377.1 19.9 %scatter_custom_fusion = f32[4017,768]{1,0:T(8,128)} fusion(s32[2048]{0:T(1024)S(1)} %bitcast.558, bf16[2048,768]{1,0:T(8,128)(2,1)} %all-gather.14.cloned.1.call-done, f32[]{:T(128)} %constant.74.clone.1), kind=kCustom, calls=%fused_computation.40 | custom fusion | flops 3145728 | bytes 15485956 | tf_op jit(solution)/shard_map/scatter-add | solution.py:287
  397.0 11.6 multiply_reduce_fusion.1
  408.6 36.5 %reduce-scatter.19.cloned.1.call-done = bf16[5,96,768]{2,1,0:T(8,128)(2,1)} async-done(((bf16[5,768,768]{2,1,0:T(8,128)(2,1)}), bf16[5,96,768]{2,1,0:T(8,128)(2,1)}) %reduce-scatter.19.cloned.1.call-update) | async-done | bytes 737296 | tf_op jit(solution)/shard_map/reduce_scatter | solution.py:122
  449.1 26.2 %all-reduce.4 = (f32[]{:T(128)}, f32[6,768]{1,0:T(8,128)S(1)}) all-reduce(f32[]{:T(128)S(6)} %add.493, f32[6,768]{1,0:T(8,128)S(1)} %concatenate.37), channel_id=1, replica_groups=mesh['grp'=4,'fsdp'=8] {'fsdp'}, use_global_device_ids=true, to_apply=%region_34.36 | all-reduce | flops 4609 | bytes 36872 | tf_op jit(solution)/shard_map/psum | solution.py:299
  477.3 29.1 %fusion.223 = (bf16[4016,768]{1,0:T(8,128)(2,1)}, f32[4016,768]{1,0:T(8,128)}, f32[4016,768]{1,0:T(8,128)}) fusion(f32[4016,768]{1,0:T(8,128)} %param.27, f32[4016,768]{1,0:T(8,128)} %get-tuple-element.225, f32[]{:T(128)S(6)} %min.25, f32[1,4016,768]{2,1,0:T(8,128)} %param.28, f32[1,4016,768]{2,1,0:T(8,128)} %param.29), kind=kLoop, calls=%fused_computation.517 | loop fusion | flops 52432896 | bytes 80191488 | tf_op jit(solution)/shard_map/convert_element_type | solution.py:180
  506.4 13.6 %gather_fusion.13 = bf16[2048,768]{1,0:T(8,128)(2,1)} fusion(bf16[4016,768]{1,0:T(8,128)(2,1)} %get-tuple-element.169, s32[2048]{0:T(1024)S(1)} %copy-done.59), kind=kCustom, calls=%fused_computation.1.clone | custom fusion | bytes 6299648 | tf_op jit(solution)/shard_map/jit(_take)/gather | solution.py:190
  528.4 6.1 copy.161
  535.3 6.1 copy.158
  541.4 6.1 copy.159
  548.4 9.0 fusion.34
  571.1 54.1 %all-gather.16.cloned.1.call-done = bf16[5,768,768]{2,1,0:T(8,128)(2,1)} async-done(((bf16[5,96,768]{2,1,0:T(8,128)(2,1)}), bf16[5,768,768]{2,1,0:T(8,128)(2,1)}) %all-gather.16.cloned.1.call-update) | async-done | bytes 5898256 | tf_op jit(solution)/shard_map/all_gather | solution.py:181
  633.5 14.1 %all_gather.69 = bf16[128,768]{1,0:T(8,128)(2,1)S(1)} all-gather(bf16[16,768]{1,0:T(8,128)(2,1)S(1)} %multiply_convert_fusion.18), channel_id=1, replica_groups=mesh['grp'=4,'fsdp'=8] {'fsdp'}, dimensions={0}, use_global_device_ids=true | all-gather | bytes 221184 | tf_op jit(solution)/shard_map/all_gather | solution.py:118
  651.0 28.2 %reduce-scatter.23.cloned.1.call-done = bf16[16,768]{1,0:T(8,128)(2,1)} async-done(((bf16[128,768]{1,0:T(8,128)(2,1)}), bf16[16,768]{1,0:T(8,128)(2,1)}) %reduce-scatter.23.cloned.1.call-update) | async-done | bytes 24592 | tf_op jit(solution)/shard_map/reduce_scatter | solution.py:122
  682.2 14.5 %all_gather.70 = bf16[2,128,768]{2,1,0:T(8,128)(2,1)S(1)} all-gather(bf16[2,16,768]{2,1,0:T(8,128)(2,1)S(1)} %pad_maximum_fusion.3), channel_id=1, replica_groups=mesh['grp'=4,'fsdp'=8] {'fsdp'}, dimensions={1}, use_global_device_ids=true | all-gather | bytes 442368 | tf_op jit(solution)/shard_map/all_gather | solution.py:219
  702.0 14.3 %all-gather.4 = f32[24,2,128]{2,1,0:T(2,128)S(1)} all-gather(f32[3,2,128]{2,1,0:T(2,128)S(1)} %pad_maximum_fusion.5), channel_id=6, replica_groups=mesh['grp'=4,'fsdp'=8] {'fsdp'}, dimensions={0}, use_global_device_ids=true | all-gather | bytes 27648 | tf_op jit(solution)/shard_map/all_gather | solution.py:236
  720.5 29.0 %reduce-scatter.25.cloned.1.call-done = bf16[2,16,768]{2,1,0:T(8,128)(2,1)} async-done(((bf16[2,128,768]{2,1,0:T(8,128)(2,1)}), bf16[2,16,768]{2,1,0:T(8,128)(2,1)}) %reduce-scatter.25.cloned.1.call-update) | async-done | bytes 49168 | tf_op jit(solution)/shard_map/reduce_scatter | solution.py:254
  755.7 15.1 %all_gather.74 = bf16[128,768]{1,0:T(8,128)(2,1)} all-gather(bf16[16,768]{1,0:T(8,128)(2,1)S(1)} %multiply_convert_fusion.9), channel_id=1, replica_groups=mesh['grp'=4,'fsdp'=8] {'fsdp'}, dimensions={0}, use_global_device_ids=true | all-gather | bytes 221184 | tf_op jit(solution)/shard_map/all_gather | solution.py:118
  778.9 27.4 %reduce-scatter.27.cloned.1.call-done = bf16[16,768]{1,0:T(8,128)(2,1)} async-done(((bf16[128,768]{1,0:T(8,128)(2,1)}), bf16[16,768]{1,0:T(8,128)(2,1)}) %reduce-scatter.27.cloned.1.call-update) | async-done | bytes 24592 | tf_op jit(solution)/shard_map/reduce_scatter | solution.py:122
  840.3 19.0 %all-gather.18.cloned.1.call-done = bf16[2048,768]{1,0:T(8,128)(2,1)} async-done(((bf16[256,768]{1,0:T(8,128)(2,1)}), bf16[2048,768]{1,0:T(8,128)(2,1)}) %all-gather.18.cloned.1.call-update) | async-done | bytes 3145744 | tf_op jit(solution)/shard_map/all_gather | solution.py:288
  859.3 19.9 %scatter_custom_fusion.1 = f32[4017,768]{1,0:T(8,128)} fusion(s32[2048]{0:T(1024)} %bitcast.557, bf16[2048,768]{1,0:T(8,128)(2,1)} %all-gather.18.cloned.1.call-done, f32[]{:T(128)} %constant.74.clone.1), kind=kCustom, calls=%fused_computation.37 | custom fusion | flops 3145728 | bytes 15486464 | tf_op jit(solution)/shard_map/scatter-add | solution.py:287
  879.2 11.6 multiply_reduce_fusion
  890.8 36.3 %reduce-scatter.29.cloned.1.call-done = bf16[5,96,768]{2,1,0:T(8,128)(2,1)} async-done(((bf16[5,768,768]{2,1,0:T(8,128)(2,1)}), bf16[5,96,768]{2,1,0:T(8,128)(2,1)}) %reduce-scatter.29.cloned.1.call-update) | async-done | bytes 737296 | tf_op jit(solution)/shard_map/reduce_scatter | solution.py:122
  931.2 26.8 %all-reduce.3 = (f32[]{:T(128)}, f32[6,768]{1,0:T(8,128)S(1)}) all-reduce(f32[]{:T(128)S(6)} %add.533, f32[6,768]{1,0:T(8,128)} %concatenate.39), channel_id=1, replica_groups=mesh['grp'=4,'fsdp'=8] {'fsdp'}, use_global_device_ids=true, to_apply=%region_75.77 | all-reduce | flops 4609 | bytes 36872 | tf_op jit(solution)/shard_map/psum | solution.py:299
  959.9 12.7 %subtract_convert_fusion.1 = bf16[2,2,768,384]{2,3,0,1:T(8,128)(2,1)} fusion(f32[2,2,768,384]{2,3,0,1:T(8,128)} %copy.161, f32[2,1,768,384]{2,3,0,1:T(8,128)} %bitcast.525, f32[2,1,768,384]{2,3,0,1:T(8,128)} %bitcast.522, f32[]{:T(128)S(6)} %min.28, f32[]{:T(128)S(6)} %min.25, f32[2,1,768,384]{2,3,0,1:T(8,128)} %bitcast.519, ...), kind=kLoop, calls=%fused_computation.74 | loop fusion | flops 42467328 | bytes 25952264 | tf_op jit(solution)/shard_map/convert_element_type | solution.py:35
  972.7 30.9 %subtract_convert_fusion = (bf16[4016,768]{1,0:T(8,128)(2,1)}, f32[1,4016,768]{2,1,0:T(8,128)}, f32[1,4016,768]{2,1,0:T(8,128)}) fusion(f32[4016,768]{1,0:T(8,128)} %param.27, f32[4016,768]{1,0:T(8,128)} %get-tuple-element.242, f32[]{:T(128)S(6)} %min.28, f32[4016,768]{1,0:T(8,128)} %get-tuple-element.170, f32[4016,768]{1,0:T(8,128)} %get-tuple-element.171), kind=kLoop, calls=%fused_computation.28 | loop fusion | flops 80191488 | bytes 80191488 | tf_op jit(solution)/shard_map/convert_element_type | solution.py:35
  1008.1 6.1 copy.175
  1018.0 10.3 fusion.25
  1028.4 6.2 copy.177
  1034.5 6.1 copy.178
  1040.6 17.5 %psum.63 = bf16[6,768]{1,0:T(8,128)(2,1)S(1)} all-reduce(bf16[6,768]{1,0:T(8,128)(2,1)S(1)} %get-tuple-element.187), channel_id=1, replica_groups=mesh['grp'=4,'fsdp'=8] {'grp'}, use_global_device_ids=true, to_apply=%region_85.87 | all-reduce | flops 4608 | bytes 18432 | tf_op jit(solution)/shard_map/psum | solution.py:324
  1059.3 135.2 %all-reduce.8.cloned.1.call-done = (bf16[4016,768]{1,0:T(8,128)(2,1)}, bf16[5,96,768]{2,1,0:T(8,128)(2,1)}, bf16[2,2,768,384]{2,3,0,1:T(8,128)(2,1)}) async-done(((bf16[4016,768]{1,0:T(8,128)(2,1)}, bf16[5,96,768]{2,1,0:T(8,128)(2,1)}, bf16[2,2,768,384]{2,3,0,1:T(8,128)(2,1)}), (bf16[4016,768]{1,0:T(8,128)(2,1)}, bf16[5,96,768]{2,1,0:T(8,128)(2,1)}, ...) | async-done | bytes 9265168 | tf_op jit(solution)/shard_map/psum | solution.py:324
  1194.6 9.5 fusion.246
  1218.6 22.9 %fusion.248 = (bf16[4016,768]{1,0:T(8,128)(2,1)}, f32[4016,768]{1,0:T(8,128)}, f32[4016,768]{1,0:T(8,128)}) fusion(f32[4016,768]{1,0:T(8,128)} %param.27, bf16[4016,768]{1,0:T(8,128)(2,1)} %get-tuple-element.149, f32[4016,768]{1,0:T(8,128)} %param.30), kind=kLoop, calls=%fused_computation.536 | loop fusion | flops 27758592 | bytes 61685760 | tf_op jit(solution)/shard_map/convert_element_type | solution.py:340
  (534 shorter events, 210.9 us)
Async XLA Ops:
  7.2 79.1 %reduce-scatter.11.cloned.1.call-start = ((), (), s32[]{:S(2)}) async-start(), calls=%async_computation.10 | async-start | bytes 3538944 | tf_op jit(solution)/shard_map/reduce_scatter | solution.py:193
  47.3 101.7 %all-gather.12.cloned.1.call-start = ((), (), s32[]{:S(2)}) async-start(), calls=%async_computation.11 | async-start | bytes 6635520 | tf_op jit(solution)/shard_map/all_gather | solution.py:181
  48.3 154.4 %reduce-scatter.13.cloned.1.call-start = ((), (), s32[]{:S(2)}) async-start(), calls=%async_computation.12 | async-start | bytes 221184 | tf_op jit(solution)/shard_map/reduce_scatter | solution.py:122
  49.8 124.2 %copy-start.100 = (s32[16]{0:T(128)}, s32[16]{0:T(128)S(1)}, u32[]{:S(2)}) copy-start(s32[16]{0:T(128)S(1)} %gather_fusion.3) | copy-start | bytes 196
  49.8 34.5 %copy-start.34 = (f32[6,768]{1,0:T(8,128)S(1)}, f32[6,768]{1,0:T(8,128)}, u32[]{:S(2)}) copy-start(f32[6,768]{1,0:T(8,128)} %param.39) | copy-start | bytes 55300
  76.5 78.5 %copy-start.97 = (s32[16]{0:T(128)}, s32[16]{0:T(128)S(1)}, u32[]{:S(2)}) copy-start(s32[16]{0:T(128)S(1)} %gather_fusion.9) | copy-start | bytes 196
  84.3 87.3 %copy-start.122 = (pred[2,128]{1,0:T(4,128)(4,1)}, pred[2,128]{1,0:T(4,128)(4,1)S(1)}, u32[]{:S(2)}) copy-start(pred[2,128]{1,0:T(4,128)(4,1)S(1)} %iota_compare_fusion.13) | copy-start | bytes 772
  84.8 70.2 %copy-start.105 = (s32[16]{0:T(128)}, s32[16]{0:T(128)S(1)}, u32[]{:S(2)}) copy-start(s32[16]{0:T(128)S(1)} %get-tuple-element.208) | copy-start | bytes 196
  90.0 62.6 %copy-start.52 = (bf16[16,768]{1,0:T(8,128)(2,1)}, bf16[16,768]{1,0:T(8,128)(2,1)S(1)}, u32[]{:S(2)}) copy-start(bf16[16,768]{1,0:T(8,128)(2,1)S(1)} %gather_fusion.2) | copy-start | bytes 73732
  92.3 61.0 %copy-start.29 = (bf16[256,768]{1,0:T(8,128)(2,1)S(1)}, bf16[256,768]{1,0:T(8,128)(2,1)}, u32[]{:S(2)}) copy-start(bf16[256,768]{1,0:T(8,128)(2,1)} %copy-done.28) | copy-start | bytes 1179652
  155.0 48.6 %copy-start.40 = (bf16[256,768]{1,0:T(8,128)(2,1)}, bf16[256,768]{1,0:T(8,128)(2,1)S(1)}, u32[]{:S(2)}) copy-start(bf16[256,768]{1,0:T(8,128)(2,1)S(1)} %convolution_convert_fusion.12) | copy-start | bytes 1179652
  155.4 47.3 %copy-start.48 = (bf16[16,768]{1,0:T(8,128)(2,1)}, bf16[16,768]{1,0:T(8,128)(2,1)S(1)}, u32[]{:S(2)}) copy-start(bf16[16,768]{1,0:T(8,128)(2,1)S(1)} %select_reduce_fusion.5) | copy-start | bytes 73732
  173.6 98.3 %reduce-scatter.15.cloned.1.call-start = ((), (), s32[]{:S(2)}) async-start(), calls=%async_computation.13 | async-start | bytes 442368 | tf_op jit(solution)/shard_map/reduce_scatter | solution.py:254
  174.0 50.4 %copy-start.114 = (f32[16]{0:T(128)}, f32[16]{0:T(128)S(1)}, u32[]{:S(2)}) copy-start(f32[16]{0:T(128)S(1)} %get-tuple-element.176) | copy-start | bytes 196
  174.0 151.5 %copy-start.83 = (f32[16,2]{0,1:T(2,128)}, f32[16,2]{0,1:T(2,128)S(1)}, u32[]{:S(2)}) copy-start(f32[16,2]{0,1:T(2,128)S(1)} %get-tuple-element.177) | copy-start | bytes 388
  203.7 72.3 %copy-start.75 = (f32[16]{0:T(128)}, f32[16]{0:T(128)S(1)}, u32[]{:S(2)}) copy-start(f32[16]{0:T(128)S(1)} %add_rsqrt_fusion.6) | copy-start | bytes 196
  203.8 35.8 %slice-start = ((s8[6168576]{0:T(1024)(128)(4,1)}), s8[4194304]{0:T(1024)(128)(4,1)S(1)}, s32[]{:S(2)}) async-start(s8[6168576]{0:T(1024)(128)(4,1)} %bitcast.509), calls=%async_computation.25 | async-start | bytes 8388608
  205.6 67.1 %copy-start.109 = (f32[16]{0:T(128)}, f32[16]{0:T(128)S(1)}, u32[]{:S(2)}) copy-start(f32[16]{0:T(128)S(1)} %add_rsqrt_fusion.5) | copy-start | bytes 196
  239.6 36.4 %copy-start.54 = (bf16[16,768]{1,0:T(8,128)(2,1)S(1)}, bf16[16,768]{1,0:T(8,128)(2,1)}, u32[]{:S(2)}) copy-start(bf16[16,768]{1,0:T(8,128)(2,1)} %reduce-scatter.13.cloned.1.call-done) | copy-start | bytes 73732
  239.6 36.6 %copy-start.115 = (f32[16]{0:T(128)S(1)}, f32[16]{0:T(128)}, u32[]{:S(2)}) copy-start(f32[16]{0:T(128)} %copy-done.114) | copy-start | bytes 196
  239.6 53.5 %copy-start.123 = (pred[2,128]{1,0:T(4,128)(4,1)S(1)}, pred[2,128]{1,0:T(4,128)(4,1)}, u32[]{:S(2)}) copy-start(pred[2,128]{1,0:T(4,128)(4,1)} %copy-done.122) | copy-start | bytes 772
  242.9 53.9 %copy-start.101 = (s32[16]{0:T(128)S(1)}, s32[16]{0:T(128)}, u32[]{:S(2)}) copy-start(s32[16]{0:T(128)} %copy-done.100) | copy-start | bytes 196
  242.9 82.6 %copy-start.93 = (f32[16]{0:T(128)S(1)}, f32[16]{0:T(128)}, u32[]{:S(2)}) copy-start(f32[16]{0:T(128)} %copy-done.92) | copy-start | bytes 196
  242.9 82.5 %reduce-scatter.17.cloned.1.call-start = ((), (), s32[]{:S(2)}) async-start(), calls=%async_computation.14 | async-start | bytes 221184 | tf_op jit(solution)/shard_map/reduce_scatter | solution.py:122
  276.2 51.0 %copy-start.110 = (f32[16]{0:T(128)}, f32[16]{0:T(128)S(1)}, u32[]{:S(2)}) copy-start(f32[16]{0:T(128)S(1)} %get-tuple-element.172) | copy-start | bytes 196
  296.7 34.8 %copy-start.20 = (bf16[256,768]{1,0:T(8,128)(2,1)S(1)}, bf16[256,768]{1,0:T(8,128)(2,1)}, u32[]{:S(2)}) copy-start(bf16[256,768]{1,0:T(8,128)(2,1)} %copy-done.19) | copy-start | bytes 1179652
  296.7 35.8 %copy-start.26 = (bf16[12,16,768]{2,1,0:T(8,128)(2,1)S(1)}, bf16[12,16,768]{2,1,0:T(8,128)(2,1)}, u32[]{:S(2)}) copy-start(bf16[12,16,768]{2,1,0:T(8,128)(2,1)} %copy-done.25) | copy-start | bytes 884740
  296.7 35.8 %copy-start.71 = (f32[192]{0:T(256)S(1)}, f32[192]{0:T(256)}, u32[]{:S(2)}) copy-start(f32[192]{0:T(256)} %copy-done.70) | copy-start | bytes 2308
  296.7 35.8 %copy-start.79 = (f32[192]{0:T(256)S(1)}, f32[192]{0:T(256)}, u32[]{:S(2)}) copy-start(f32[192]{0:T(256)} %copy-done.78) | copy-start | bytes 2308
  296.8 80.3 %all-gather.14.cloned.1.call-start = ((), (), s32[]{:S(2)}) async-start(), calls=%async_computation.15 | async-start | bytes 3538944 | tf_op jit(solution)/shard_map/all_gather | solution.py:288
  340.5 104.5 %reduce-scatter.19.cloned.1.call-start = ((), (), s32[]{:S(2)}) async-start(), calls=%async_computation.16 | async-start | bytes 6635520 | tf_op jit(solution)/shard_map/reduce_scatter | solution.py:122
  348.3 214.1 %reduce-scatter.21.cloned.1.call-start = ((), (), s32[]{:S(2)}) async-start(), calls=%async_computation.17 | async-start | bytes 3538944 | tf_op jit(solution)/shard_map/reduce_scatter | solution.py:193
  475.3 73.0 %copy-start.42 = (f32[6,768]{1,0:T(8,128)}, f32[6,768]{1,0:T(8,128)S(1)}, u32[]{:S(2)}) copy-start(f32[6,768]{1,0:T(8,128)S(1)} %get-tuple-element.148) | copy-start | bytes 55300
  523.6 101.6 %all-gather.16.cloned.1.call-start = ((), (), s32[]{:S(2)}) async-start(), calls=%async_computation.18 | async-start | bytes 6635520 | tf_op jit(solution)/shard_map/all_gather | solution.py:181
  528.1 151.1 %reduce-scatter.23.cloned.1.call-start = ((), (), s32[]{:S(2)}) async-start(), calls=%async_computation.19 | async-start | bytes 221184 | tf_op jit(solution)/shard_map/reduce_scatter | solution.py:122
  547.6 100.6 %copy-start.120 = (pred[2,128]{1,0:T(4,128)(4,1)}, pred[2,128]{1,0:T(4,128)(4,1)S(1)}, u32[]{:S(2)}) copy-start(pred[2,128]{1,0:T(4,128)(4,1)S(1)} %iota_compare_fusion.11) | copy-start | bytes 772
  567.2 64.4 %copy-start.50 = (bf16[16,768]{1,0:T(8,128)(2,1)}, bf16[16,768]{1,0:T(8,128)(2,1)S(1)}, u32[]{:S(2)}) copy-start(bf16[16,768]{1,0:T(8,128)(2,1)S(1)} %gather_fusion.8) | copy-start | bytes 73732
  631.8 48.4 %copy-start.47 = (bf16[16,768]{1,0:T(8,128)(2,1)}, bf16[16,768]{1,0:T(8,128)(2,1)S(1)}, u32[]{:S(2)}) copy-start(bf16[16,768]{1,0:T(8,128)(2,1)S(1)} %select_reduce_fusion.3) | copy-start | bytes 73732
  633.5 45.8 %copy-start.90 = (f32[16]{0:T(128)}, f32[16]{0:T(128)S(1)}, u32[]{:S(2)}) copy-start(f32[16]{0:T(128)S(1)} %add_rsqrt_fusion.4) | copy-start | bytes 196
  650.1 99.3 %reduce-scatter.25.cloned.1.call-start = ((), (), s32[]{:S(2)}) async-start(), calls=%async_computation.20 | async-start | bytes 442368 | tf_op jit(solution)/shard_map/reduce_scatter | solution.py:254
  680.3 36.8 %slice-start.2 = ((s8[6168576]{0:T(1024)(128)(4,1)}), s8[4194304]{0:T(1024)(128)(4,1)S(1)}, s32[]{:S(2)}) async-start(s8[6168576]{0:T(1024)(128)(4,1)} %bitcast.511), calls=%async_computation.27 | async-start | bytes 8388608
  717.1 34.5 %copy-start.73 = (f32[16]{0:T(128)S(1)}, f32[16]{0:T(128)}, u32[]{:S(2)}) copy-start(f32[16]{0:T(128)} %copy-done.72) | copy-start | bytes 196
  720.4 85.9 %reduce-scatter.27.cloned.1.call-start = ((), (), s32[]{:S(2)}) async-start(), calls=%async_computation.21 | async-start | bytes 221184 | tf_op jit(solution)/shard_map/reduce_scatter | solution.py:122
  753.5 57.1 %copy-start.69 = (f32[192]{0:T(256)S(1)}, f32[192]{0:T(256)}, u32[]{:S(2)}) copy-start(f32[192]{0:T(256)} %copy-done.68) | copy-start | bytes 2308
  755.0 53.0 %copy-start.36 = (f32[16,768]{1,0:T(8,128)}, f32[16,768]{1,0:T(8,128)S(1)}, u32[]{:S(2)}) copy-start(f32[16,768]{1,0:T(8,128)S(1)} %get-tuple-element.163) | copy-start | bytes 147460
  777.6 81.7 %all-gather.18.cloned.1.call-start = ((), (), s32[]{:S(2)}) async-start(), calls=%async_computation.22 | async-start | bytes 3538944 | tf_op jit(solution)/shard_map/all_gather | solution.py:288
  822.7 104.4 %reduce-scatter.29.cloned.1.call-start = ((), (), s32[]{:S(2)}) async-start(), calls=%async_computation.23 | async-start | bytes 6635520 | tf_op jit(solution)/shard_map/reduce_scatter | solution.py:122
  833.5 361.0 %all-reduce.8.cloned.1.call-start = ((), (), s32[]{:S(2)}) async-start(), calls=%async_computation.24 | async-start | bytes 18530304 | tf_op jit(solution)/shard_map/psum | solution.py:324
  (104 other events, 1171.3 us)
Sparse Core Ops, SparseCore 0:
  47.4 38.8 reduce-scatter.10
  88.5 60.4 all-gather.11
  173.8 28.9 reduce-scatter.12
  243.1 28.8 reduce-scatter.14
  296.9 28.5 reduce-scatter.16
  340.6 36.3 all-gather.13
  380.1 64.9 reduce-scatter.18
  523.8 38.5 reduce-scatter.20
  564.6 60.5 all-gather.15
  650.3 28.9 reduce-scatter.22
  720.5 28.8 reduce-scatter.24
  777.7 28.4 reduce-scatter.26
  822.8 36.4 all-gather.17
  862.1 64.9 reduce-scatter.28
  1008.1 186.3 all-reduce.7

commit v2 on v1

--- a/solution.py
+++ b/solution.py
@@ -1,8 +1,11 @@
+import functools
 import math
 
 import jax
 import jax.numpy as jnp
 from jax import lax
+from jax.experimental import pallas as pl
+from jax.experimental.pallas import tpu as pltpu
 from jax.sharding import PartitionSpec as P
 
 D = 768
@@ -124,6 +127,677 @@
     ).astype(jnp.float32)
 
 
+TILE = 512
+MESH = pl.DeviceIdType.MESH
+F32 = jnp.float32
+LOW = jnp.bfloat16
+X_IN, B_ROWS, Y_PART, HEAD_ROWS, TOPS, D_ROWS, DY_ROWS, DB_PART = range(8)
+ROWS_ONE, P_A, ROWS_TWO, DS_A, G_OUT, D_VEC, EXCHANGES = range(8, 15)
+
+
+def dot_nn(left, right):
+    return lax.dot_general(left, right, (((1,), (0,)), ((), ())), preferred_element_type=F32)
+
+
+def dot_nt(left, right):
+    return lax.dot_general(left, right, (((1,), (1,)), ((), ())), preferred_element_type=F32)
+
+
+def dot_tn(left, right):
+    return lax.dot_general(left, right, (((0,), (0,)), ((), ())), preferred_element_type=F32)
+
+
+def lanes(shape):
+    return lax.broadcasted_iota(jnp.int32, shape, len(shape) - 1)
+
+
+def sublanes(shape):
+    return lax.broadcasted_iota(jnp.int32, shape, len(shape) - 2)
+
+
+def norm_factor(x):
+    return lax.rsqrt(jnp.mean(x * x, axis=-1, keepdims=True) + EPSILON)
+
+
+def norm_grad(x, factor, gain_row, upstream):
+    normed = x * factor
+    scaled = upstream * gain_row
+    back = factor * (scaled - normed * jnp.mean(scaled * normed, axis=-1, keepdims=True))
+    return back, jnp.sum(upstream * normed, axis=0, keepdims=True)
+
+
+GELU_C = math.sqrt(2.0 / math.pi)
+
+
+def gelu_of(u):
+    return 0.5 * u * (1.0 + jnp.tanh(GELU_C * (u + 0.044715 * (u * u * u))))
+
+
+def gelu_slope(u):
+    t = jnp.tanh(GELU_C * (u + 0.044715 * (u * u * u)))
+    return 0.5 * (1.0 + t) + 0.5 * u * (1.0 - t * t) * GELU_C * (1.0 + 3.0 * 0.044715 * u * u)
+
+
+def rows_at_once(n, slots):
+    return max(g for g in range(1, n + 1) if n % g == 0 and g * slots <= 512)
+
+
+def step_kernel(
+    dims,
+    id_col, id_lane, slot_col, slot_lane, pick_col, pick_lane, seg_rows, seg_lane,
+    route_col, route_all, target_lane, vec, eb, attn, expw,
+    dembed_out, dattn_out, dexp_out, dvec_out, loss_out,
+    xs, xr, gr, ball, ys, yr, rows, tops, drs, drr, dyall, dbs, dbr,
+    one, pas, par, two, dss, dsr, dvec, logit_s, dlog_s, pre_s, hid_s, dpre_s, flip_s, tile_s,
+    send, recv, out_sem,
+):
+    n, slots, vocab, vocab_rows, hidden = dims
+    row_count = pick_col.shape[0]
+    tokens = slot_col.shape[0]
+    all_rows = n * row_count
+    wide = HEADS * row_count
+    shard = D // n
+    row_total = float(all_rows)
+    scale = 2.0 * D ** (-0.5)
+    factor_qk = HEAD_DIM ** (-0.5)
+    me = lax.axis_index("fsdp")
+
+    def others(body):
+        def one_step(k, carry):
+            body(k, lax.rem(me + k, n))
+            return carry
+
+        lax.fori_loop(1, n, one_step, 0)
+
+    def link(which, k, source, target, peer, origin):
+        return pltpu.make_async_remote_copy(
+            src_ref=source,
+            dst_ref=target,
+            send_sem=send.at[which, k],
+            recv_sem=recv.at[which, origin],
+            device_id={"fsdp": peer},
+            device_id_type=MESH,
+        )
+
+    def spread(which, buffer):
+        others(lambda k, peer: link(which, k, buffer.at[me], buffer.at[me], peer, me).start())
+
+    def deal(which, source, target):
+        others(lambda k, peer: link(which, k, source.at[peer], target.at[me], peer, me).start())
+
+    def arrive(which, target):
+        others(
+            lambda k, peer: link(which, k, target.at[peer], target.at[peer], peer, peer).wait_recv()
+        )
+
+    def sent(which, source):
+        others(lambda k, peer: link(which, k, source.at[peer], source.at[peer], peer, me).wait_send())
+
+    def tiled(body, carry):
+        whole = vocab_rows // TILE
+        carry = lax.fori_loop(
+            0, whole, lambda i, c: body(i, pl.multiple_of(i * TILE, TILE), TILE, c), carry
+        )
+        if vocab_rows % TILE:
+            carry = body(whole, whole * TILE, vocab_rows % TILE, carry)
+        return carry
+
+    def added(buffer):
+        total = buffer[0].astype(F32)
+        for j in range(1, n):
+            total = total + buffer[j].astype(F32)
+        return total
+
+    barrier = pltpu.get_barrier_semaphore()
+    others(
+        lambda k, peer: pl.semaphore_signal(
+            barrier, inc=1, device_id={"fsdp": peer}, device_id_type=MESH
+        )
+    )
+    pl.semaphore_wait(barrier, n - 1)
+
+    group = rows_at_once(n, slots)
+    chunk = group * slots
+
+    def look(c, carry):
+        ids = id_col[pl.ds(pl.multiple_of(c * chunk, chunk), chunk), :]
+
+        def add(i, start, size, acc):
+            hit = (lanes((chunk, size)) + start == ids).astype(F32).astype(LOW)
+            return acc + dot_nn(hit, eb[pl.ds(start, size), :])
+
+        found = tiled(add, jnp.zeros((chunk, D), F32))
+        xs[pl.ds(c * group, group)] = found.astype(LOW).reshape(group, slots, D)
+        return carry
+
+    lax.fori_loop(0, n // group, look, 0)
+    deal(X_IN, xs, xr)
+    xr[me] = xs[me]
+    arrive(X_IN, xr)
+    x = jnp.zeros((tokens, D), F32)
+    for c in range(n // group):
+        hit = (lanes((tokens, chunk)) + c * chunk == slot_col[...]).astype(F32).astype(LOW)
+        x = x + dot_nn(hit, xr[c * group : (c + 1) * group].reshape(chunk, D))
+
+    gain_a, gain_b, gain_c, gain_d = (vec[i : i + 1, :] for i in range(4))
+    x_factor = norm_factor(x)
+    a = (x * x_factor * gain_a).astype(LOW)
+    pick = (lanes((row_count, tokens)) == pick_col[...]).astype(F32).astype(LOW)
+    x_rows = dot_nn(pick, x.astype(LOW))
+    a_rows = dot_nn(pick, a).astype(LOW)
+    q = dot_nn(a_rows, attn[0]).astype(LOW)
+    k = dot_nn(a, attn[1]).astype(LOW)
+    v = dot_nn(a, attn[2]).astype(LOW)
+    head_mask = (
+        lax.shift_right_logical(lanes((HEADS, row_count, D)), HEAD_DIM.bit_length() - 1)
+        == lax.broadcasted_iota(jnp.int32, (HEADS, row_count, D), 0)
+    )
+
+    def widen(low_rows):
+        return (
+            jnp.where(head_mask, low_rows.astype(F32)[None], 0.0).reshape(wide, D).astype(LOW)
+        )
+
+    def narrow(values):
+        return jnp.sum(jnp.where(head_mask, values.reshape(HEADS, row_count, D), 0.0), axis=0)
+
+    q_wide = widen(q)
+    scores = dot_nt(q_wide, k) * factor_qk
+    allowed = (lanes((row_count, tokens)) <= pick_col[...]) & (seg_lane[...] == seg_rows[...])
+    scores = jnp.where(
+        allowed[None], scores.reshape(HEADS, row_count, tokens), -1e30
+    ).reshape(wide, tokens)
+    exponent = jnp.exp(scores - jnp.max(scores, axis=-1, keepdims=True))
+    probs = exponent / jnp.sum(exponent, axis=-1, keepdims=True)
+    probs_low = probs.astype(LOW)
+    o = narrow(dot_nn(probs_low, v)).astype(LOW)
+    x_attn = x_rows + ATTN_GAIN * dot_nn(o, attn[3])
+
+    b_factor = norm_factor(x_attn)
+    b = x_attn * b_factor * gain_b
+    ball[me] = b.astype(LOW)
+    spread(B_ROWS, ball)
+    router_rows = [vec[4 + e : 5 + e, :] for e in range(EXPERTS)]
+    router_logits = [jnp.sum(b * row, axis=-1, keepdims=True) for row in router_rows]
+    highest = router_logits[0]
+    for value in router_logits[1:]:
+        highest = jnp.maximum(highest, value)
+    router_exp = [jnp.exp(value - highest) for value in router_logits]
+    router_sum = sum(router_exp[1:], router_exp[0])
+    router_probs = [value / router_sum for value in router_exp]
+    chosen = [(route_col[...] == e).astype(F32) for e in range(EXPERTS)]
+    gate = sum([p * c for p, c in zip(router_probs[1:], chosen[1:])], router_probs[0] * chosen[0])
+    one[me, 0] = a_rows
+    one[me, 1] = o
+    one[me, 2] = q
+    a_turned = a.astype(F32).T.astype(LOW)
+    pas[...] = dot_nt(a_turned, probs_low).reshape(n, shard, wide).astype(LOW)
+    arrive(B_ROWS, ball)
+    b_all = ball[...].reshape(all_rows, D)
+    y_part = jnp.zeros((all_rows, D), F32)
+    for e in range(EXPERTS):
+        pre = dot_nn(b_all, expw[e, 0])
+        pre_s[e] = pre
+        hid = jnp.where(route_all[...] == e, gelu_of(pre), 0.0).astype(LOW)
+        hid_s[e] = hid
+        y_part = y_part + dot_nt(hid, expw[e, 1])
+    ys[...] = y_part.astype(LOW).reshape(n, row_count, D)
+    deal(Y_PART, ys, yr)
+    yr[me] = ys[me]
+    arrive(Y_PART, yr)
+    y = added(yr)
+    z = x_attn + gate * y
+
+    z_factor = norm_factor(z)
+    first = (z * z_factor * gain_c).astype(LOW)
+    middle = dot_nn(first, attn[4])
+    middle_factor = norm_factor(middle)
+    rows[me, 0] = first
+    rows[me, 1] = (middle * middle_factor * gain_d).astype(LOW)
+    spread(HEAD_ROWS, rows)
+    spread(ROWS_ONE, one)
+    deal(P_A, pas, par)
+    par[me] = pas[me]
+    arrive(HEAD_ROWS, rows)
+    loss_rows = 2 * all_rows
+    head_rows = rows[...].reshape(loss_rows, D)
+
+    def target_hit(start, size):
+        return sublanes((size, loss_rows)) + start == target_lane[...]
+
+    def logits_tile(i, start, size, carry):
+        top, total, at_target = carry
+        value = dot_nt(eb[pl.ds(start, size), :], head_rows) * scale
+        if vocab_rows != vocab:
+            value = jnp.where(sublanes((size, loss_rows)) + start < vocab, value, -1e30)
+        logit_s[pl.ds(start, size), :] = value
+        hit = target_hit(start, size)
+        at_target = at_target + jnp.sum(jnp.where(hit, value, 0.0), axis=0, keepdims=True)
+        new_top = jnp.maximum(top, jnp.max(value, axis=0, keepdims=True))
+        total = total * jnp.exp(top - new_top) + jnp.sum(
+            jnp.exp(value - new_top), axis=0, keepdims=True
+        )
+        return new_top, total, at_target
+
+    nothing = jnp.zeros((1, loss_rows), F32)
+    top, total, at_target = tiled(logits_tile, (nothing - 1e30, nothing, nothing))
+    place = sublanes((8, loss_rows))
+    tops[me] = jnp.where(
+        place == 0, top, jnp.where(place == 1, total, jnp.where(place == 2, at_target, 0.0))
+    )
+    spread(TOPS, tops)
+    arrive(TOPS, tops)
+    top = tops[0, 0:1]
+    for j in range(1, n):
+        top = jnp.maximum(top, tops[j, 0:1])
+    total, at_target = nothing, nothing
+    for j in range(n):
+        total = total + tops[j, 1:2] * jnp.exp(tops[j, 0:1] - top)
+        at_target = at_target + tops[j, 2:3]
+    logsum = top + jnp.log(total)
+    is_first = lax.rem(lanes((1, loss_rows)), 2 * row_count) < row_count
+    weight = jnp.where(is_first, 1.0, SECOND_WEIGHT) / row_total
+    loss = jnp.sum(weight * (logsum - at_target), axis=-1, keepdims=True)
+    loss_out[...] = jnp.broadcast_to(loss, loss_out.shape)
+
+    def dlogits_tile(i, start, size, acc):
+        soft = jnp.exp(logit_s[pl.ds(start, size), :] - logsum)
+        low = ((soft - target_hit(start, size).astype(F32)) * weight).astype(LOW)
+        dlog_s[pl.ds(start, size), :] = low
+        return acc + dot_tn(low, eb[pl.ds(start, size), :])
+
+    drows = tiled(dlogits_tile, jnp.zeros((loss_rows, D), F32)) * scale
+    drs[...] = drows.astype(LOW).reshape(n, 2 * row_count, D)
+    deal(D_ROWS, drs, drr)
+    drr[me] = drs[me]
+    arrive(D_ROWS, drr)
+    drow = added(drr)
+    dmiddle, gain_mtp = norm_grad(middle, middle_factor, gain_d, drow[row_count:])
+    dmiddle_low = dmiddle.astype(LOW)
+    dfirst = drow[:row_count] + dot_nt(dmiddle_low, attn[4])
+    dz, gain_final = norm_grad(z, z_factor, gain_c, dfirst)
+
+    dgate = jnp.sum(dz * y, axis=-1, keepdims=True)
+    dyall[me] = (gate * dz).astype(LOW)
+    spread(DY_ROWS, dyall)
+    arrive(DY_ROWS, dyall)
+    dy_all = dyall[...].reshape(all_rows, D)
+    db_part = jnp.zeros((all_rows, D), F32)
+    for e in range(EXPERTS):
+        dhid = dot_nn(dy_all, expw[e, 1])
+        slope = jnp.where(route_all[...] == e, gelu_slope(pre_s[e]), 0.0)
+        dpre = (slope * dhid).astype(LOW)
+        dpre_s[e] = dpre
+        db_part = db_part + dot_nt(dpre, expw[e, 0])
+    dbs[...] = db_part.astype(LOW).reshape(n, row_count, D)
+    deal(DB_PART, dbs, dbr)
+    dbr[me] = dbs[me]
+    squares = jnp.zeros((1, D), F32)
+
+    def squared(values):
+        return jnp.sum(values * values, axis=0, keepdims=True)
+
+    hidden_squares = jnp.zeros((1, hidden), F32)
+    for e in range(EXPERTS):
+        up = dot_tn(b_all, dpre_s[e])
+        down = dot_tn(dy_all, hid_s[e])
+        dexp_out[e, 0] = up
+        dexp_out[e, 1] = down
+        hidden_squares = hidden_squares + squared(up) + squared(down)
+    arrive(DB_PART, dbr)
+    prob_grads = [c * dgate for c in chosen]
+    mixed = sum([p * g for p, g in zip(router_probs[1:], prob_grads[1:])], router_probs[0] * prob_grads[0])
+    dlogits = [p * (g - mixed) for p, g in zip(router_probs, prob_grads)]
+    drouter = [jnp.sum(g * b, axis=0, keepdims=True) for g in dlogits]
+    dnormed = added(dbr)
+    for g, row in zip(dlogits, router_rows):
+        dnormed = dnormed + g * row
+    dx_part, gain_ffn = norm_grad(x_attn, b_factor, gain_b, dnormed)
+    dx_attn = dz + dx_part
+
+    dbranch = dx_attn.astype(LOW)
+    do = (ATTN_GAIN * dot_nt(dbranch, attn[3])).astype(LOW)
+    do_wide = widen(do)
+    dprobs = dot_nt(do_wide, v)
+    dscores = (probs * (dprobs - jnp.sum(probs * dprobs, axis=-1, keepdims=True))).astype(LOW)
+    dq = (narrow(dot_nn(dscores, k)) * factor_qk).astype(LOW)
+    two[me, 0] = do
+    two[me, 1] = dq
+    two[me, 2] = dbranch
+    two[me, 3] = dmiddle_low
+    dk = (dot_tn(dscores, q_wide) * factor_qk).astype(LOW)
+    dv = dot_tn(probs_low, do_wide).astype(LOW)
+    dinput = dot_nt(dk, attn[1]) + dot_nt(dv, attn[2])
+    dx, gain_attn = norm_grad(x, x_factor, gain_a, dinput)
+    row_back, gain_more = norm_grad(x_rows, norm_factor(x_rows), gain_a, dot_nt(dq, attn[0]))
+    spots = (sublanes((tokens, row_count)) == pick_lane[...]).astype(F32)
+    dx = dx + lax.dot_general(
+        spots, row_back + dx_attn, (((1,), (0,)), ((), ())), precision=HIGH,
+        preferred_element_type=F32,
+    )
+    dx_low = dx.astype(LOW)
+    sent(X_IN, xs)
+    for c in range(n // group):
+        hit = (sublanes((chunk, tokens)) + c * chunk == slot_lane[...]).astype(F32).astype(LOW)
+        xs[c * group : (c + 1) * group] = dot_nn(hit, dx_low).astype(LOW).reshape(group, slots, D)
+    deal(G_OUT, xs, gr)
+    gr[me] = xs[me]
+    spread(ROWS_TWO, two)
+    dss[...] = dot_nt(a_turned, dscores).reshape(n, shard, wide).astype(LOW)
+    deal(DS_A, dss, dsr)
+    dsr[me] = dss[me]
+
+    arrive(ROWS_ONE, one)
+    arrive(P_A, par)
+    arrive(ROWS_TWO, two)
+    arrive(DS_A, dsr)
+    mine = pl.ds(pl.multiple_of(me * shard, 8), shard)
+
+    def own_rows(left, right):
+        flip_s[...] = left.astype(F32).reshape(all_rows, D).T
+        return dot_nn(flip_s[mine, :].astype(LOW), right.reshape(all_rows, D))
+
+    dkey = jnp.zeros((shard, D), F32)
+    dvalue = jnp.zeros((shard, D), F32)
+    for j in range(n):
+        dkey = dkey + dot_nn(dsr[j], widen(one[j, 2]))
+        dvalue = dvalue + dot_nn(par[j], widen(two[j, 0]))
+    parts = (
+        own_rows(one[:, 0], two[:, 1]),
+        dkey * factor_qk,
+        dvalue,
+        ATTN_GAIN * own_rows(one[:, 1], two[:, 2]),
+        own_rows(rows[:, 0], two[:, 3]),
+    )
+    for i, part in enumerate(parts):
+        dattn_out[i] = part
+        squares = squares + squared(part)
+
+    arrive(G_OUT, gr)
+    whole = vocab_rows // TILE
+
+    def leave(i, start, size):
+        slot = lax.rem(i, 2)
+        return pltpu.make_async_copy(
+            tile_s.at[slot, pl.ds(0, size)], dembed_out.at[pl.ds(start, size)], out_sem.at[slot]
+        )
+
+    def dembed_tile(i, start, size, acc):
+        value = scale * dot_nn(dlog_s[pl.ds(start, size), :], head_rows)
+        for c in range(n // group):
+            ids = id_lane[:, c * chunk : (c + 1) * chunk]
+            hit = (sublanes((size, chunk)) + start == ids).astype(F32).astype(LOW)
+            value = value + dot_nn(hit, gr[c * group : (c + 1) * group].reshape(chunk, D))
+
+        def free():
+            leave(i - 2, start - 2 * TILE, TILE).wait()
+
+        if isinstance(i, int):
+            if i >= 2:
+                free()
+        else:
+            pl.when(i >= 2)(free)
+        tile_s[lax.rem(i, 2), pl.ds(0, size)] = value
+        leave(i, start, size).start()
+        return acc + squared(value)
+
+    squares = tiled(dembed_tile, squares)
+    tiles = [(i, i * TILE, TILE) for i in range(whole)]
+    if vocab_rows % TILE:
+        tiles.append((whole, whole * TILE, vocab_rows % TILE))
+    total_squares = jnp.sum(squares, axis=-1, keepdims=True) + jnp.sum(
+        hidden_squares, axis=-1, keepdims=True
+    )
+    line = sublanes((8, D))
+    share = jnp.broadcast_to(total_squares, (8, D))
+    for i, value in enumerate([gain_attn + gain_more, gain_ffn, gain_final, gain_mtp] + drouter):
+        share = jnp.where(line == i, value, share)
+    dvec[me] = share
+    spread(D_VEC, dvec)
+    arrive(D_VEC, dvec)
+    dvec_out[...] = added(dvec)
+    for i, start, size in tiles[-2:]:
+        leave(i, start, size).wait()
+    for which, source in (
+        (B_ROWS, ball), (Y_PART, ys), (HEAD_ROWS, rows), (TOPS, tops), (D_ROWS, drs),
+        (DY_ROWS, dyall), (DB_PART, dbs), (ROWS_ONE, one), (P_A, pas), (ROWS_TWO, two),
+        (DS_A, dss), (G_OUT, xs), (D_VEC, dvec),
+    ):
+        sent(which, source)
+
+
+def run_step(n, slots, vocab, number, ints, vec, embed_low, attn_low, expert_low):
+    vocab_rows = -(-vocab // 16) * 16
+    if vocab_rows != vocab:
+        embed_low = jnp.pad(embed_low, ((0, vocab_rows - vocab), (0, 0)))
+    row_count = ints["pick_col"].shape[0]
+    hidden = expert_low.shape[3]
+    shard = D // n
+    all_rows = n * row_count
+    wide = HEADS * row_count
+    vmem = pl.BlockSpec(memory_space=pltpu.VMEM)
+    low = lambda *shape: pltpu.VMEM(shape, LOW)
+    wide_float = lambda *shape: pltpu.VMEM(shape, F32)
+    names = (
+        "id_col", "id_lane", "slot_col", "slot_lane", "pick_col", "pick_lane", "seg_rows",
+        "seg_lane", "route_col", "route_all", "target_lane",
+    )
+    outs = pl.pallas_call(
+        functools.partial(step_kernel, (n, slots, vocab, vocab_rows, hidden)),
+        out_shape=(
+            jax.ShapeDtypeStruct((vocab_rows, D), F32),
+            jax.ShapeDtypeStruct((5, shard, D), F32),
+            jax.ShapeDtypeStruct((EXPERTS, 2, D, hidden), F32),
+            jax.ShapeDtypeStruct((8, D), F32),
+            jax.ShapeDtypeStruct((8, 128), F32),
+        ),
+        in_specs=[vmem] * 15,
+        out_specs=(pl.BlockSpec(memory_space=pl.ANY), vmem, vmem, vmem, vmem),
+        scratch_shapes=[
+            low(n, slots, D), low(n, slots, D), low(n, slots, D),
+            low(n, row_count, D), low(n, row_count, D), low(n, row_count, D),
+            low(n, 2, row_count, D), wide_float(n, 8, 2 * all_rows),
+            low(n, 2 * row_count, D), low(n, 2 * row_count, D),
+            low(n, row_count, D), low(n, row_count, D), low(n, row_count, D),
+            low(n, 3, row_count, D), low(n, shard, wide), low(n, shard, wide),
+            low(n, 4, row_count, D), low(n, shard, wide), low(n, shard, wide),
+            wide_float(n, 8, D),
+            wide_float(vocab_rows, 2 * all_rows), low(vocab_rows, 2 * all_rows),
+            wide_float(EXPERTS, all_rows, hidden), low(EXPERTS, all_rows, hidden),
+            low(EXPERTS, all_rows, hidden), wide_float(D, all_rows), wide_float(2, TILE, D),
+            pltpu.SemaphoreType.DMA((EXCHANGES, n)),
+            pltpu.SemaphoreType.DMA((EXCHANGES, n)),
+            pltpu.SemaphoreType.DMA((2,)),
+        ],
+        compiler_params=pltpu.CompilerParams(
+            collective_id=number, has_side_effects=True, vmem_limit_bytes=60 * 1024 * 1024
+        ),
+        name="inner_step",
+    )(*[ints[name] for name in names], vec, embed_low, attn_low, expert_low)
+    return (outs[0][:vocab],) + outs[1:]
+
+
+def prepare(n, slots, vocab, tokens, routes, segments, loss_pos):
+    steps, count = tokens.shape
+    start = lax.axis_index("fsdp") * vocab
+    row_count = loss_pos.shape[1]
+    owner = tokens // vocab
+    places = jnp.arange(count)
+    earlier = places[None, None, :] < places[None, :, None]
+    same = tokens[:, :, None] == tokens[:, None, :]
+    first = jnp.logical_not(jnp.any(same & earlier, axis=2))
+    same_owner = owner[:, :, None] == owner[:, None, :]
+    rank = jnp.sum((same_owner & earlier & first[:, None, :]).astype(jnp.int32), axis=2)
+    own_slot = owner * slots + rank
+    slot = jnp.sum(jnp.where(same & first[:, None, :], own_slot[:, None, :], 0), axis=2)
+    at_slot = (own_slot[:, :, None] == jnp.arange(n * slots)[None, None, :]) & first[:, :, None]
+    ids = jnp.sum(jnp.where(at_slot, tokens[:, :, None] + 1, 0), axis=1) - 1
+    picked = loss_pos[:, :, None] == places[None, None, :]
+    shifted = lambda by: jnp.sum(
+        jnp.where(loss_pos[:, :, None] + by == places[None, None, :], tokens[:, None, :], 0), axis=2
+    )
+    row_routes = jnp.sum(jnp.where(picked, routes[:, None, :], 0), axis=2)
+    row_segs = jnp.sum(jnp.where(picked, segments[:, None, :], 0), axis=2)
+    most = jnp.broadcast_to(jnp.max(jnp.where(first, rank, 0)), (steps, 1))
+    packed = jnp.concatenate([ids, row_routes, shifted(1), shifted(2), most], axis=1)
+    world = lax.all_gather(packed, ("grp", "fsdp"))
+    fits = jnp.max(world[:, 0, -1]) < slots
+    everyone = lax.dynamic_slice_in_dim(world, lax.axis_index("grp") * n, n, axis=0)[:, :, :-1]
+    wanted = lax.dynamic_slice_in_dim(everyone, lax.axis_index("fsdp") * slots, slots, axis=2) - start
+    after = n * slots
+    result = []
+    for s in range(steps):
+        want = wanted[:, s].reshape(n * slots)
+        targets = everyone[:, s, after + row_count :].reshape(1, n * 2 * row_count) - start
+        result.append(
+            dict(
+                id_col=want[:, None],
+                id_lane=want[None, :],
+                slot_col=slot[s][:, None],
+                slot_lane=slot[s][None, :],
+                pick_col=loss_pos[s][:, None],
+                pick_lane=loss_pos[s][None, :],
+                seg_rows=row_segs[s][:, None],
+                seg_lane=segments[s][None, :],
+                route_col=row_routes[s][:, None],
+                route_all=everyone[:, s, after : after + row_count].reshape(n * row_count, 1),
+                target_lane=targets,
+            )
+        )
+    return result, fits
+
+
+def general_step(tokens, routes, segments, loss_pos, all_ids, inner_step, weights):
+    embed_w, attn_w, expert_w, vector_w = weights
+    vocab_shard = embed_w.shape[0]
+    vocab_start = lax.axis_index("fsdp") * vocab_shard
+    row_total = lax.axis_size("fsdp") * loss_pos.shape[2]
+    logit_scale = 2.0 * D ** (-0.5)
+    vocab_places = jnp.arange(vocab_shard)
+    head_weights = jnp.array([1.0, SECOND_WEIGHT], jnp.float32)
+    embed_low = embed_w.astype(jnp.bfloat16)
+    attn_low = lax.all_gather(attn_w.astype(jnp.bfloat16), "fsdp", axis=1, tiled=True)
+    expert_low = expert_w.astype(jnp.bfloat16)
+    ids_group = all_ids[inner_step]
+    ids_local = tokens[inner_step, 0]
+    seg_ids = segments[inner_step, 0]
+    route_ids = routes[inner_step, 0, :, 0]
+    pick_ids = loss_pos[inner_step, 0]
+    chosen = ids_group - vocab_start
+    inside = (chosen >= 0) & (chosen < vocab_shard)
+    looked = jnp.take(embed_low, jnp.clip(chosen, 0, vocab_shard - 1), axis=0).astype(
+        jnp.float32
+    )
+    x_embed = lax.psum_scatter(
+        jnp.where(inside[:, None], looked, 0.0).astype(jnp.bfloat16),
+        "fsdp",
+        scatter_dimension=0,
+        tiled=True,
+    ).astype(jnp.float32)
+    x_attn, kept = rows_forward(attn_low, vector_w, x_embed, seg_ids, pick_ids)
+    b, b_factor = norm_apply(x_attn, vector_w[1])
+    router_probs = jax.nn.softmax(jnp.dot(b, vector_w[4:].T, precision=HIGH), axis=-1)
+    row_routes = route_ids[pick_ids]
+    onehot = (row_routes[:, None] == jnp.arange(EXPERTS)[None, :]).astype(jnp.float32)
+    gating = jnp.sum(router_probs * onehot, axis=1)
+    b_all = gather_rows(b.astype(jnp.bfloat16))
+    routes_all = gather_rows(row_routes)
+    route_mask = routes_all[None, :, None] == jnp.arange(EXPERTS)[:, None, None]
+    hidden_pre = jnp.einsum("cd,edf->ecf", b_all, expert_low[:, 0], preferred_element_type=jnp.float32)
+    hidden_act = jnp.where(route_mask, smooth_act(hidden_pre), 0.0).astype(jnp.bfloat16)
+    y_part = jnp.einsum("ecf,edf->cd", hidden_act, expert_low[:, 1], preferred_element_type=jnp.float32)
+    returned = scatter_rows(y_part)
+    z_rows = x_attn + gating[:, None] * returned
+    first_float, first_factor = norm_apply(z_rows, vector_w[2])
+    first_rows = first_float.astype(jnp.bfloat16)
+    middle = jnp.dot(first_rows, attn_low[4], preferred_element_type=jnp.float32)
+    second_float, second_factor = norm_apply(middle, vector_w[3])
+    targets = jnp.stack([ids_local[pick_ids + 1], ids_local[pick_ids + 2]])
+    rows_all, targets_all = (
+        lax.all_gather(
+            jnp.stack([first_rows, second_float.astype(jnp.bfloat16)]),
+            "fsdp",
+            axis=1,
+            tiled=True,
+        ),
+        lax.all_gather(targets, "fsdp", axis=1, tiled=True),
+    )
+    logits = (
+        jnp.einsum("jrd,vd->jrv", rows_all, embed_low, preferred_element_type=jnp.float32)
+        * logit_scale
+    )
+    relative = targets_all - vocab_start
+    onehot_target = (vocab_places[None, None, :] == relative[:, :, None]).astype(jnp.float32)
+    target_part = jnp.sum(onehot_target * logits, axis=-1)
+    local_top = jnp.max(logits, axis=-1)
+    local_sum = jnp.sum(jnp.exp(logits - local_top[:, :, None]), axis=-1)
+    parts = lax.all_gather(jnp.stack([local_top, local_sum, target_part]), "fsdp")
+    row_top = jnp.max(parts[:, 0], axis=0)
+    sum_exp = jnp.sum(parts[:, 1] * jnp.exp(parts[:, 0] - row_top), axis=0)
+    target_logit = jnp.sum(parts[:, 2], axis=0)
+    logsum = row_top + jnp.log(sum_exp)
+    loss = (jnp.sum(head_weights[:, None] * (logsum - target_logit)) / row_total)
+    dlogits = (
+        (jnp.exp(logits - logsum[:, :, None]) - onehot_target)
+        * (head_weights / row_total)[:, None, None]
+    ).astype(jnp.bfloat16)
+    dembed = (
+        jnp.einsum("jrv,jrd->vd", dlogits, rows_all, preferred_element_type=jnp.float32)
+        * logit_scale
+    )
+    drows = (
+        jnp.einsum("jrv,vd->jrd", dlogits, embed_low, preferred_element_type=jnp.float32)
+        * logit_scale
+    )
+    drows_own = lax.psum_scatter(
+        drows.astype(jnp.bfloat16), "fsdp", scatter_dimension=1, tiled=True
+    ).astype(jnp.float32)
+    dmiddle, gain_mtp = norm_back(middle, second_factor, vector_w[3], drows_own[1])
+    dmiddle_low = dmiddle.astype(jnp.bfloat16)
+    dsecond_proj = jnp.dot(first_rows.T, dmiddle_low, preferred_element_type=jnp.float32)
+    dfirst = drows_own[0] + jnp.dot(
+        dmiddle_low, attn_low[4].T, preferred_element_type=jnp.float32
+    )
+    dz_rows, gain_final = norm_back(z_rows, first_factor, vector_w[2], dfirst)
+    dgating = jnp.sum(dz_rows * returned, axis=1)
+    dy_all = gather_rows((gating[:, None] * dz_rows).astype(jnp.bfloat16))
+    dy_masked = jnp.where(route_mask, dy_all[None], 0)
+    down_grad = jnp.einsum("ecf,ecd->edf", hidden_act, dy_masked, preferred_element_type=jnp.float32)
+    dhidden = jnp.einsum("ecd,edf->ecf", dy_masked, expert_low[:, 1], preferred_element_type=jnp.float32)
+    unused, act_back = jax.vjp(smooth_act, hidden_pre)
+    dhidden_pre = act_back(dhidden)[0].astype(jnp.bfloat16)
+    up_grad = jnp.einsum("cd,ecf->edf", b_all, dhidden_pre, preferred_element_type=jnp.float32)
+    dexpert = jnp.stack([up_grad, down_grad], axis=1)
+    db_part = jnp.einsum("ecf,edf->cd", dhidden_pre, expert_low[:, 0], preferred_element_type=jnp.float32)
+    dnormed = scatter_rows(db_part)
+    prob_grad = onehot * dgating[:, None]
+    dlogit = router_probs * (prob_grad - jnp.sum(router_probs * prob_grad, axis=1, keepdims=True))
+    drouter = jnp.dot(dlogit.T, b, precision=HIGH)
+    dnormed = dnormed + jnp.dot(dlogit, vector_w[4:], precision=HIGH)
+    dx_part, gain_ffn = norm_back(x_attn, b_factor, vector_w[1], dnormed)
+    dx_embed, dlayer, gain_attn = rows_backward(
+        attn_low, vector_w, x_embed, kept, dz_rows + dx_part, pick_ids
+    )
+    dattn = scatter_rows(jnp.concatenate([dlayer, dsecond_proj[None]], axis=0), axis=1)
+    gather_chosen = ids_group - vocab_start
+    gather_inside = (gather_chosen >= 0) & (gather_chosen < vocab_shard)
+    seg_index = jnp.where(gather_inside, gather_chosen, vocab_shard)
+    added = jax.ops.segment_sum(
+        lax.all_gather(dx_embed.astype(jnp.bfloat16), "fsdp", axis=0, tiled=True).astype(
+            jnp.float32
+        ),
+        seg_index,
+        num_segments=vocab_shard + 1,
+    )
+    dembed = dembed + added[:vocab_shard]
+    dvector_part = jnp.concatenate(
+        [jnp.stack([gain_attn, gain_ffn, gain_final, gain_mtp]), drouter], axis=0
+    )
+    squares = jnp.sum(dembed * dembed) + jnp.sum(dattn * dattn) + jnp.sum(dexpert * dexpert)
+    dvector, squares_all = lax.psum((dvector_part, squares), "fsdp")
+    return dembed, dattn, dexpert, dvector, squares_all, loss
+
+
 def adam_update(weight, first_moment, second, gradient, step_float, rate_here, decay_here):
     first_new = BETA_ONE * first_moment + (1.0 - BETA_ONE) * gradient
     second_new = BETA_TWO * second + (1.0 - BETA_TWO) * gradient * gradient
@@ -135,11 +809,8 @@
     return (weight_new, first_new, second_new)
 
 
-def shards(
-    tokens,
-    routes,
-    segments,
-    loss_pos,
+def window(
+    step,
     embedding,
     embedding_first,
     embedding_second,
@@ -156,17 +827,11 @@
     vectors_first,
     vectors_second,
     vectors_outer,
+    inner_count,
+    row_total,
 ):
-    inner_count = tokens.shape[0]
-    vocab_shard = embedding.shape[0]
-    vocab_start = lax.axis_index("fsdp") * vocab_shard
     group_count = lax.axis_size("grp")
-    row_total = lax.axis_size("fsdp") * loss_pos.shape[2]
     threshold = 0.05 / math.sqrt(row_total)
-    logit_scale = 2.0 * D ** (-0.5)
-    all_ids = lax.all_gather(tokens[:, 0, :], "fsdp", axis=1, tiled=True)
-    vocab_places = jnp.arange(vocab_shard)
-    head_weights = jnp.array([1.0, SECOND_WEIGHT], jnp.float32)
     vector_rates = jnp.where(jnp.arange(vectors.shape[0])[:, None] < 4, LR_GAIN, LR_ROUTER)
     rate_list = (LR_EMBED, LR_MATRIX, LR_MATRIX, vector_rates)
     decay_list = (DECAY, DECAY, DECAY, 0.0)
@@ -176,127 +841,8 @@
     loss_list = []
     norm_list = []
     for inner_step in range(inner_count):
-        embed_w, attn_w, expert_w, vector_w = weights_now
-        embed_low = embed_w.astype(jnp.bfloat16)
-        attn_low = lax.all_gather(attn_w.astype(jnp.bfloat16), "fsdp", axis=1, tiled=True)
-        expert_low = expert_w.astype(jnp.bfloat16)
-        ids_group = all_ids[inner_step]
-        ids_local = tokens[inner_step, 0]
-        seg_ids = segments[inner_step, 0]
-        route_ids = routes[inner_step, 0, :, 0]
-        pick_ids = loss_pos[inner_step, 0]
-        chosen = ids_group - vocab_start
-        inside = (chosen >= 0) & (chosen < vocab_shard)
-        looked = jnp.take(embed_low, jnp.clip(chosen, 0, vocab_shard - 1), axis=0).astype(
-            jnp.float32
-        )
-        x_embed = lax.psum_scatter(
-            jnp.where(inside[:, None], looked, 0.0).astype(jnp.bfloat16),
-            "fsdp",
-            scatter_dimension=0,
-            tiled=True,
-        ).astype(jnp.float32)
-        x_attn, kept = rows_forward(attn_low, vector_w, x_embed, seg_ids, pick_ids)
-        b, b_factor = norm_apply(x_attn, vector_w[1])
-        router_probs = jax.nn.softmax(jnp.dot(b, vector_w[4:].T, precision=HIGH), axis=-1)
-        row_routes = route_ids[pick_ids]
-        onehot = (row_routes[:, None] == jnp.arange(EXPERTS)[None, :]).astype(jnp.float32)
-        gating = jnp.sum(router_probs * onehot, axis=1)
-        b_all = gather_rows(b.astype(jnp.bfloat16))
-        routes_all = gather_rows(row_routes)
-        route_mask = routes_all[None, :, None] == jnp.arange(EXPERTS)[:, None, None]
-        hidden_pre = jnp.einsum("cd,edf->ecf", b_all, expert_low[:, 0], preferred_element_type=jnp.float32)
-        hidden_act = jnp.where(route_mask, smooth_act(hidden_pre), 0.0).astype(jnp.bfloat16)
-        y_part = jnp.einsum("ecf,edf->cd", hidden_act, expert_low[:, 1], preferred_element_type=jnp.float32)
-        returned = scatter_rows(y_part)
-        z_rows = x_attn + gating[:, None] * returned
-        first_float, first_factor = norm_apply(z_rows, vector_w[2])
-        first_rows = first_float.astype(jnp.bfloat16)
-        middle = jnp.dot(first_rows, attn_low[4], preferred_element_type=jnp.float32)
-        second_float, second_factor = norm_apply(middle, vector_w[3])
-        targets = jnp.stack([ids_local[pick_ids + 1], ids_local[pick_ids + 2]])
-        rows_all, targets_all = (
-            lax.all_gather(
-                jnp.stack([first_rows, second_float.astype(jnp.bfloat16)]),
-                "fsdp",
-                axis=1,
-                tiled=True,
-            ),
-            lax.all_gather(targets, "fsdp", axis=1, tiled=True),
-        )
-        logits = (
-            jnp.einsum("jrd,vd->jrv", rows_all, embed_low, preferred_element_type=jnp.float32)
-            * logit_scale
-        )
-        relative = targets_all - vocab_start
-        onehot_target = (vocab_places[None, None, :] == relative[:, :, None]).astype(jnp.float32)
-        target_part = jnp.sum(onehot_target * logits, axis=-1)
-        local_top = jnp.max(logits, axis=-1)
-        local_sum = jnp.sum(jnp.exp(logits - local_top[:, :, None]), axis=-1)
-        parts = lax.all_gather(jnp.stack([local_top, local_sum, target_part]), "fsdp")
-        row_top = jnp.max(parts[:, 0], axis=0)
-        sum_exp = jnp.sum(parts[:, 1] * jnp.exp(parts[:, 0] - row_top), axis=0)
-        target_logit = jnp.sum(parts[:, 2], axis=0)
-        logsum = row_top + jnp.log(sum_exp)
-        loss_list.append(jnp.sum(head_weights[:, None] * (logsum - target_logit)) / row_total)
-        dlogits = (
-            (jnp.exp(logits - logsum[:, :, None]) - onehot_target)
-            * (head_weights / row_total)[:, None, None]
-        ).astype(jnp.bfloat16)
-        dembed = (
-            jnp.einsum("jrv,jrd->vd", dlogits, rows_all, preferred_element_type=jnp.float32)
-            * logit_scale
-        )
-        drows = (
-            jnp.einsum("jrv,vd->jrd", dlogits, embed_low, preferred_element_type=jnp.float32)
-            * logit_scale
-        )
-        drows_own = lax.psum_scatter(
-            drows.astype(jnp.bfloat16), "fsdp", scatter_dimension=1, tiled=True
-        ).astype(jnp.float32)
-        dmiddle, gain_mtp = norm_back(middle, second_factor, vector_w[3], drows_own[1])
-        dmiddle_low = dmiddle.astype(jnp.bfloat16)
-        dsecond_proj = jnp.dot(first_rows.T, dmiddle_low, preferred_element_type=jnp.float32)
-        dfirst = drows_own[0] + jnp.dot(
-            dmiddle_low, attn_low[4].T, preferred_element_type=jnp.float32
-        )
-        dz_rows, gain_final = norm_back(z_rows, first_factor, vector_w[2], dfirst)
-        dgating = jnp.sum(dz_rows * returned, axis=1)
-        dy_all = gather_rows((gating[:, None] * dz_rows).astype(jnp.bfloat16))
-        dy_masked = jnp.where(route_mask, dy_all[None], 0)
-        down_grad = jnp.einsum("ecf,ecd->edf", hidden_act, dy_masked, preferred_element_type=jnp.float32)
-        dhidden = jnp.einsum("ecd,edf->ecf", dy_masked, expert_low[:, 1], preferred_element_type=jnp.float32)
-        unused, act_back = jax.vjp(smooth_act, hidden_pre)
-        dhidden_pre = act_back(dhidden)[0].astype(jnp.bfloat16)
-        up_grad = jnp.einsum("cd,ecf->edf", b_all, dhidden_pre, preferred_element_type=jnp.float32)
-        dexpert = jnp.stack([up_grad, down_grad], axis=1)
-        db_part = jnp.einsum("ecf,edf->cd", dhidden_pre, expert_low[:, 0], preferred_element_type=jnp.float32)
-        dnormed = scatter_rows(db_part)
-        prob_grad = onehot * dgating[:, None]
-        dlogit = router_probs * (prob_grad - jnp.sum(router_probs * prob_grad, axis=1, keepdims=True))
-        drouter = jnp.dot(dlogit.T, b, precision=HIGH)
-        dnormed = dnormed + jnp.dot(dlogit, vector_w[4:], precision=HIGH)
-        dx_part, gain_ffn = norm_back(x_attn, b_factor, vector_w[1], dnormed)
-        dx_embed, dlayer, gain_attn = rows_backward(
-            attn_low, vector_w, x_embed, kept, dz_rows + dx_part, pick_ids
-        )
-        dattn = scatter_rows(jnp.concatenate([dlayer, dsecond_proj[None]], axis=0), axis=1)
-        gather_chosen = ids_group - vocab_start
-        gather_inside = (gather_chosen >= 0) & (gather_chosen < vocab_shard)
-        seg_index = jnp.where(gather_inside, gather_chosen, vocab_shard)
-        added = jax.ops.segment_sum(
-            lax.all_gather(dx_embed.astype(jnp.bfloat16), "fsdp", axis=0, tiled=True).astype(
-                jnp.float32
-            ),
-            seg_index,
-            num_segments=vocab_shard + 1,
-        )
-        dembed = dembed + added[:vocab_shard]
-        dvector_part = jnp.concatenate(
-            [jnp.stack([gain_attn, gain_ffn, gain_final, gain_mtp]), drouter], axis=0
-        )
-        squares = jnp.sum(dembed * dembed) + jnp.sum(dattn * dattn) + jnp.sum(dexpert * dexpert)
-        dvector, squares_all = lax.psum((dvector_part, squares), "fsdp")
+        dembed, dattn, dexpert, dvector, squares_all, loss = step(inner_step, weights_now)
+        loss_list.append(loss)
         norm_value = jnp.sqrt(squares_all + jnp.sum(dvector * dvector))
         norm_list.append(norm_value)
         factor = jnp.minimum(1.0, threshold / norm_value)
@@ -354,6 +900,79 @@
         new_master[3],
         new_outer[3],
     )
+
+
+def shards(
+    tokens,
+    routes,
+    segments,
+    loss_pos,
+    embedding,
+    embedding_first,
+    embedding_second,
+    embedding_outer,
+    attention,
+    attention_first,
+    attention_second,
+    attention_outer,
+    experts,
+    experts_first,
+    experts_second,
+    experts_outer,
+    vectors,
+    vectors_first,
+    vectors_second,
+    vectors_outer,
+):
+    inner_count = tokens.shape[0]
+    vocab_shard = embedding.shape[0]
+    n = lax.axis_size("fsdp")
+    row_total = n * loss_pos.shape[2]
+    slots = 48
+    steps, fits = prepare(
+        n, slots, vocab_shard, tokens[:, 0], routes[:, 0, :, 0], segments[:, 0], loss_pos[:, 0]
+    )
+    attn_start = lax.all_gather(attention.astype(jnp.bfloat16), "fsdp", axis=1, tiled=True)
+    state = (
+        embedding,
+        embedding_first,
+        embedding_second,
+        embedding_outer,
+        attention,
+        attention_first,
+        attention_second,
+        attention_outer,
+        experts,
+        experts_first,
+        experts_second,
+        experts_outer,
+        vectors,
+        vectors_first,
+        vectors_second,
+        vectors_outer,
+    )
+
+    def quick(*state):
+        def step(inner_step, weights):
+            embed_w, attn_w, expert_w, vector_w = weights
+            if inner_step == 0:
+                attn_low = attn_start
+            else:
+                attn_low = lax.all_gather(attn_w.astype(jnp.bfloat16), "fsdp", axis=1, tiled=True)
+            dembed, dattn, dexpert, dvector_all, loss = run_step(
+                n, slots, vocab_shard, 1, steps[inner_step], vector_w,
+                embed_w.astype(jnp.bfloat16), attn_low, expert_w.astype(jnp.bfloat16),
+            )
+            return dembed, dattn, dexpert, dvector_all[:6], dvector_all[6, 0], loss[0, 0]
+
+        return window(step, *state, inner_count, row_total)
+
+    def general(*state):
+        all_ids = lax.all_gather(tokens[:, 0, :], "fsdp", axis=1, tiled=True)
+        step = functools.partial(general_step, tokens, routes, segments, loss_pos, all_ids)
+        return window(step, *state, inner_count, row_total)
+
+    return lax.cond(fits, quick, general, *state)
 
 
 def solution(mesh):

time: 1260 us -> 804 us (0.64)
  waiting for transfers between devices: 536 us -> 191 us
  Pallas kernels: 0 us -> 327 us
  blocking collectives: 226 us -> 61.6 us
  matrix products: 127 us -> 0 us
  local copies, waits for them, and re-layouts: 106 us -> 32.1 us
  other arithmetic: 229 us -> 156 us
  loops' own time: 0 us -> 12.7 us
    pallas_call x0 -> x2, Pallas kernels: none -> 327 us  [run_step(): pl.pallas_call(functools.partial(step_kernel, (n, slots, vocab, vocab_row...]
    reduce_scatter x10 -> x0, waiting for transfers between devices: 250 us -> none  [the longest x6 186 us: scatter_rows(): lax.psum_scatter(value.astype(jnp.bfloat16), 'fsdp', scatter_dimension=ax...]
    all_gather x4 -> x2, waiting for transfers between devices: 151 us -> 22.6 us  [the longest x1 13.5 us: step(): lax.all_gather(attn_w.astype(jnp.bfloat16), 'fsdp', axis=1, tiled=True)]
    dot_general x70 -> x0, matrix products: 127 us -> none  [the longest x2 23.2 us: shards(): jnp.einsum('jrv,jrd->vd', dlogits, rows_all, preferred_element_type=jnp.f...]
    all_gather x11 -> x1, blocking collectives: 149 us -> 45.2 us  [prepare(): world = lax.all_gather(packed, ('grp', 'fsdp'))]
    unnamed x292 -> x16, local copies, waits for them, and re-layouts: 62.6 us -> 6.26 us
    psum x3 -> x1, blocking collectives: 70.4 us -> 16.4 us  [window(): lax.psum(for_sending(deltas), 'grp')]
    scatter-add x2 -> x0, other arithmetic: 39.8 us -> none  [shards(): jax.ops.segment_sum(lax.all_gather(dx_embed.astype(jnp.bfloat16), 'fsdp',...]
  transfers between devices with their start and end apart: 15 -> 3, of which waited for: 15 -> 3; matrix products, arithmetic and copies ran while one was open for 15% -> 8% of each run, Pallas kernels for 0% -> 0%
where the time goes in v2:
time: 804 us; the launch traced here: 795 us
  Pallas kernels  327 us (41%)
  waiting for transfers between devices  191 us (24%)
  other arithmetic  156 us (19%)
  blocking collectives  61.6 us (8%)
  local copies, waits for them, and re-layouts  32.1 us (4%)
  between operations  14.7 us (2%)
  loops' own time  12.7 us (2%)
    pallas_call x2, Pallas kernels, run_step(): pl.pallas_call(functools.partial(step_kernel, (n, slots, vocab, vocab_row...  327 us
    psum x1, waiting for transfers between devices, window(): lax.psum(for_sending(deltas), 'grp')  168 us
    all_gather x1, blocking collectives, prepare(): world = lax.all_gather(packed, ('grp', 'fsdp'))  45.2 us
    convert_element_type x2, other arithmetic, step(): embed_w.astype(jnp.bfloat16)  37.3 us
    convert_element_type x1, other arithmetic, short(): return part.astype(jnp.bfloat16) if part.dtype == jnp.float32 else part  31.9 us
    convert_element_type x1, other arithmetic, window(): new_master[0].astype(jnp.bfloat16)  18.4 us
    convert_element_type x2, other arithmetic, step(): expert_w.astype(jnp.bfloat16)  17.4 us
    psum x1, blocking collectives, window(): lax.psum(for_sending(deltas), 'grp')  16.4 us
  transfers between devices with their start and end apart: 3, of which 3 were waited for; matrix products, arithmetic and copies ran while one was open for 8% of the time, Pallas kernels for 0%

profile of v2, /device:TPU:0, one launch (start us, length us, event | category | flops | bytes accessed | tf_op | source)
XLA Modules:
  0.0 795.2 jit_solution(5662378119422956365)
XLA Ops:
  7.2 2.3 convert_element_type.342
  9.6 0.7 copy.489
  10.3 0.7 copy.488
  11.0 0.7 copy_bitcast_fusion.2
  11.9 1.4 select_reduce_fusion.10
  13.4 0.7 broadcast_add_fusion.3
  14.3 0.7 and_select_fusion.3
  16.9 45.2 %all-gather.8 = s32[32,2,433]{2,1,0:T(2,128)S(1)} all-gather(s32[1,2,433]{2,1,0:T(2,128)S(1)} %bitcast.691), channel_id=7, replica_groups=mesh['grp'=4,'fsdp'=8] {'grp','fsdp'}, dimensions={0}, use_global_device_ids=true | all-gather | bytes 114312 | tf_op jit(solution)/shard_map/all_gather | solution.py:643
  62.2 0.7 slice_reduce_fusion.10
  63.9 1.2 fusion.294
  66.3 9.0 %all-gather.26.cloned.1.call-done = bf16[5,768,768]{2,1,0:T(8,128)(2,1)} async-done(((bf16[5,96,768]{2,1,0:T(8,128)(2,1)}), bf16[5,768,768]{2,1,0:T(8,128)(2,1)}) %all-gather.26.cloned.1.call-update) | async-done | bytes 5898256 | tf_op jit(solution)/shard_map/all_gather | solution.py:935
  76.0 707.5 %conditional.3 = (f32[1,2]{1,0:T(1,128)S(1)}, f32[1,2]{1,0:T(1,128)S(1)}, f32[1,4016,768]{2,1,0:T(8,128)}, f32[1,4016,768]{2,1,0:T(8,128)}, f32[4016,768]{1,0:T(...) conditional(s32[]{:T(128)} %convert_element_type.341, ((), ...), branch_computations={%region_10.98_spmd, %region_97.105_spmd} | conditional | flops 16723800064 | bytes 1117249920
  85.4 1.2 slice_bitcast_fusion.1.seg_lane
  86.6 1.3 broadcast_in_dim_reshape_squeeze.17.id_lane
  88.6 0.7 copy.318.route_col
  90.0 1.3 copy.316.pick_col
  91.3 0.7 slice_subtract_fusion.1
  92.7 0.7 reshape_squeeze.12.route_all
  93.4 1.5 copy.315.slot_col
  94.9 1.5 broadcast_in_dim_reshape_squeeze.20.id_col
  96.3 4.0 convert_element_type.322.expw
  100.3 7.8 convert_element_type.321.eb
  108.1 163.5 %inner_step.2 = (f32[4016,768]{1,0:T(8,128)}, f32[5,96,768]{2,1,0:T(8,128)}, f32[2,2,768,384]{3,2,1,0:T(8,128)}, f32[8,768]{1,0:T(8,128)}, f32[8,128]{1,0:T(8,128)}) custom-call(s32[384,1]{1,0:T(8,128)} %broadcast_in_dim_reshape_squeeze.20.id_col, s32[1,384]{1,0:T(1,128)} %broadcast_in_dim_reshape_squeeze.17.id_lane, s32[256,1]{1,0:T(8,128)} %copy.315.slot_col, ...), custom_call_target="tpu_custom_call" | custom-call | tf_op jit(solution)/shard_map/cond/branch_1_fun/inner_step/pallas_call | solution.py:585
  271.7 1.2 slice.230
  272.9 1.3 multiply_reduce_fusion.1
  275.7 4.5 fusion.17
  281.0 0.7 copy.324.route_col
  283.7 0.7 reshape_squeeze.13.route_all
  284.4 0.8 copy.321.slot_col
  285.2 0.8 broadcast_in_dim_reshape_squeeze.21.id_col
  287.3 13.4 %fusion.16 = (bf16[2,2,768,384]{3,2,1,0:T(8,128)(2,1)}, f32[2,2,768,384]{3,2,1,0:T(8,128)}, f32[2,2,768,384]{3,2,1,0:T(8,128)}) fusion(f32[2,2,768,384]{3,2,1,0:T(8,128)} %get-tuple-element.215, f32[2,2,768,384]{3,2,1,0:T(8,128)} %get-tuple-element.239, f32[]{:T(128)S(6)} %min.26, f32[1,2,2,768,384]{4,3,2,1,0:T(8,128)} %get-tuple-element.238, ...), kind=kLoop, calls=%fused_computation.84 | loop fusion | flops 20054016 | bytes 30670852 | tf_op jit(solution)/shard_map/cond/branch_1_fun/convert_element_type | solution.py:964
  300.7 29.5 %fusion.15 = (bf16[4016,768]{1,0:T(8,128)(2,1)}, f32[4016,768]{1,0:T(8,128)}, f32[4016,768]{1,0:T(8,128)}) fusion(f32[4016,768]{1,0:T(8,128)} %get-tuple-element.213, f32[4016,768]{1,0:T(8,128)} %get-tuple-element.232, f32[]{:T(128)S(6)} %min.26, f32[1,4016,768]{2,1,0:T(8,128)} %get-tuple-element.231, f32[1,4016,768]{2,1,0:T(8,128)} %get-tuple-element.233), kind=kLoop, calls=%fused_computation.83 | loop fusion | flops 52432896 | bytes 80191488 | tf_op jit(solution)/shard_map/cond/branch_1_fun/convert_element_type | solution.py:964
  330.2 13.5 %all-gather.24.cloned.1.call-done.attn = bf16[5,768,768]{2,1,0:T(8,128)(2,1)} async-done(((bf16[5,96,768]{2,1,0:T(8,128)(2,1)}), bf16[5,768,768]{2,1,0:T(8,128)(2,1)}) %all-gather.24.cloned.1.call-update) | async-done | bytes 5898256 | tf_op jit(solution)/shard_map/cond/branch_1_fun/all_gather | solution.py:961
  343.8 163.6 %inner_step.3 = (f32[4016,768]{1,0:T(8,128)}, f32[5,96,768]{2,1,0:T(8,128)}, f32[2,2,768,384]{3,2,1,0:T(8,128)}, f32[8,768]{1,0:T(8,128)}, f32[8,128]{1,0:T(8,128)}) custom-call(s32[384,1]{1,0:T(8,128)} %broadcast_in_dim_reshape_squeeze.21.id_col, s32[1,384]{1,0:T(1,128)} %broadcast_in_dim_reshape_squeeze.19.id_lane, s32[256,1]{1,0:T(8,128)} %copy.321.slot_col, ...), custom_call_target="tpu_custom_call" | custom-call | tf_op jit(solution)/shard_map/cond/branch_1_fun/inner_step/pallas_call | solution.py:585
  507.3 1.4 multiply_reduce_fusion
  508.7 1.2 slice.232
  511.3 31.9 %subtract_convert_fusion = (bf16[4016,768]{1,0:T(8,128)(2,1)}, f32[1,4016,768]{2,1,0:T(8,128)}, f32[1,4016,768]{2,1,0:T(8,128)}) fusion(f32[4016,768]{1,0:T(8,128)} %get-tuple-element.213, f32[4016,768]{1,0:T(8,128)} %get-tuple-element.243, f32[]{:T(128)S(6)} %min.27, f32[4016,768]{1,0:T(8,128)} %get-tuple-element.1071, f32[4016,768]{1,0:T(8,128)} %get-tuple-element.1072), kind=kLoop, calls=%fused_computation.24 | loop fusion | flops 80191488 | bytes 80191488 | tf_op jit(solution)/shard_map/cond/branch_1_fun/convert_element_type | solution.py:38
  543.3 14.7 %fusion.9 = (f32[1,2,2,768,384]{4,3,2,1,0:T(8,128)}, bf16[2,2,768,384]{3,2,1,0:T(8,128)(2,1)}, f32[1,2,2,768,384]{4,3,2,1,0:T(8,128)}) fusion(f32[2,2,768,384]{3,2,1,0:T(8,128)S(1)} %copy-done.20, f32[]{:T(128)S(6)} %min.27, f32[2,2,768,384]{3,2,1,0:T(8,128)} %get-tuple-element.1066, f32[2,2,768,384]{3,2,1,0:T(8,128)S(1)} %bitcast.635, ...), kind=kLoop, calls=%fused_computation.52 | loop fusion | flops 30670848 | bytes 30670852 | tf_op jit(solution)/shard_map/cond/branch_1_fun/broadcast_in_dim | solution.py:893
  558.0 4.0 fusion.11
  562.1 1.3 slice.228
  563.4 1.2 slice.231
  565.4 16.4 %psum.83 = bf16[6,768]{1,0:T(8,128)(2,1)S(1)} all-reduce(bf16[6,768]{1,0:T(8,128)(2,1)S(1)} %get-tuple-element.1109), channel_id=1, replica_groups=mesh['grp'=4,'fsdp'=8] {'grp'}, use_global_device_ids=true, to_apply=%region_103.104 | all-reduce | flops 4608 | bytes 18432 | tf_op jit(solution)/shard_map/cond/branch_1_fun/psum | solution.py:870
  581.8 1.4 maximum_bitcast_fusion
  583.8 168.1 %all-reduce.12.cloned.1.call-done = (bf16[4016,768]{1,0:T(8,128)(2,1)}, bf16[5,96,768]{2,1,0:T(8,128)(2,1)}, bf16[2,2,768,384]{3,2,1,0:T(8,128)(2,1)}) async-done(((bf16[4016,768]{1,0:T(8,128)(2,1)}, bf16[5,96,768]{2,1,0:T(8,128)(2,1)}, bf16[2,2,768,384]{3,2,1,0:T(8,128)(2,1)}), (bf16[4016,768]{1,0:T(8,128)(2,1)}, bf16[5,96,768]{2,1,0:T(8,128)(2,1)}, ...) | async-done | bytes 9265168 | tf_op jit(solution)/shard_map/cond/branch_1_fun/psum | solution.py:870
  752.0 3.3 fusion.270
  755.3 9.6 %fusion.269 = (bf16[2,2,768,384]{3,2,1,0:T(8,128)(2,1)}, f32[2,2,768,384]{3,2,1,0:T(8,128)}, f32[2,2,768,384]{3,2,1,0:T(8,128)}) fusion(f32[2,2,768,384]{3,2,1,0:T(8,128)} %get-tuple-element.215, bf16[2,2,768,384]{3,2,1,0:T(8,128)(2,1)S(1)} %copy-done.23, f32[2,2,768,384]{3,2,1,0:T(8,128)} %get-tuple-element.248), kind=kLoop, calls=%fused_computation.638 | loop fusion | flops 10616832 | bytes 23592960 | tf_op jit(solution)/shard_map/cond/branch_0_fun/convert_element_type | solution.py:896
  764.8 18.4 %fusion.271 = (bf16[4016,768]{1,0:T(8,128)(2,1)}, f32[4016,768]{1,0:T(8,128)S(1)}, f32[4016,768]{1,0:T(8,128)}) fusion(f32[4016,768]{1,0:T(8,128)} %get-tuple-element.213, bf16[4016,768]{1,0:T(8,128)(2,1)} %get-tuple-element.1041, f32[4016,768]{1,0:T(8,128)} %get-tuple-element.244), kind=kLoop, calls=%fused_computation.640 | loop fusion | flops 27758592 | bytes 61685760 | tf_op jit(solution)/shard_map/cond/branch_0_fun/convert_element_type | solution.py:886
  783.5 4.6 copy-done.11
  (122 shorter events, 12.5 us)
Async XLA Ops:
  7.2 68.2 %all-gather.26.cloned.1.call-start = ((), (), s32[]{:S(2)}) async-start(), calls=%async_computation.27 | async-start | bytes 6635520 | tf_op jit(solution)/shard_map/all_gather | solution.py:935
  13.4 3.6 copy-start.129
  85.3 258.4 %all-gather.24.cloned.1.call-start = ((), (), s32[]{:S(2)}) async-start(), calls=%async_computation.25 | async-start | bytes 6635520 | tf_op jit(solution)/shard_map/cond/branch_1_fun/all_gather | solution.py:961
  100.3 7.8 copy-start.25
  100.3 7.8 copy-start.126
  100.3 7.8 copy-start.153
  108.1 167.5 %copy-start.1 = (f32[5,96,768]{2,1,0:T(8,128)S(1)}, f32[5,96,768]{2,1,0:T(8,128)}, u32[]{:S(2)}) copy-start(f32[5,96,768]{2,1,0:T(8,128)} %get-tuple-element.234) | copy-start | bytes 4423684 | tf_op jit(solution)/shard_map/conditional.1
  108.1 167.5 %copy-start.9 = (f32[1,5,96,768]{3,2,1,0:T(8,128)S(1)}, f32[1,5,96,768]{3,2,1,0:T(8,128)}, u32[]{:S(2)}) copy-start(f32[1,5,96,768]{3,2,1,0:T(8,128)} %get-tuple-element.235) | copy-start | bytes 4423684 | tf_op jit(solution)/shard_map/conditional.1
  275.6 4.7 copy-start.89
  275.7 5.3 copy-start.130
  275.7 5.3 copy-start.162
  275.7 6.7 copy-start.151
  275.7 8.7 %copy-start.124 = (s32[1,256]{1,0:T(1,128)S(1)}, s32[1,256]{1,0:T(1,128)}, u32[]{:S(2)}) copy-start(s32[1,256]{1,0:T(1,128)} %get-tuple-element.220.slot_lane) | copy-start | bytes 3076 | tf_op jit(solution)/shard_map/conditional.1
  275.7 10.3 %copy-start.95 = (s32[2,1,256]{2,1,0:T(1,128)S(1)}, s32[2,1,256]{2,1,0:T(1,128)}, u32[]{:S(2)}) copy-start(s32[2,1,256]{2,1,0:T(1,128)} %get-tuple-element.345) | copy-start | bytes 6148 | tf_op jit(solution)/shard_map/conditional.1
  275.7 10.9 %copy-start.53 = (f32[1,6,768]{2,0,1:T(1,128)S(1)}, f32[1,6,768]{2,0,1:T(1,128)}, u32[]{:S(2)}) copy-start(f32[1,6,768]{2,0,1:T(1,128)} %get-tuple-element.949) | copy-start | bytes 55300 | tf_op jit(solution)/shard_map/conditional.1
  275.7 10.9 %copy-start.56 = (f32[1,6,768]{2,0,1:T(1,128)S(1)}, f32[1,6,768]{2,0,1:T(1,128)}, u32[]{:S(2)}) copy-start(f32[1,6,768]{2,0,1:T(1,128)} %get-tuple-element.950) | copy-start | bytes 55300 | tf_op jit(solution)/shard_map/conditional.1
  275.7 10.8 %copy-start.61 = (f32[8,768]{1,0:T(8,128)S(1)}, f32[8,768]{1,0:T(8,128)}, u32[]{:S(2)}) copy-start(f32[8,768]{1,0:T(8,128)} %get-tuple-element.229) | copy-start | bytes 73732 | tf_op jit(solution)/shard_map/conditional.1
  280.3 471.7 %all-reduce.12.cloned.1.call-start = ((), (), s32[]{:S(2)}) async-start(), calls=%async_computation.26 | async-start | bytes 18530304 | tf_op jit(solution)/shard_map/cond/branch_1_fun/psum | solution.py:870
  286.0 14.7 %copy-start.169 = (f32[6]{0:T(128)}, f32[6]{0:T(128)S(1)}, u32[]{:S(2)}) copy-start(f32[6]{0:T(128)S(1)} %compare_select_fusion) | copy-start | bytes 76 | tf_op jit(solution)/shard_map/conditional.1
  300.7 43.0 %copy-start.125 = (s32[1,256]{1,0:T(1,128)S(1)}, s32[1,256]{1,0:T(1,128)}, u32[]{:S(2)}) copy-start(s32[1,256]{1,0:T(1,128)} %get-tuple-element.220.slot_lane) | copy-start | bytes 3076 | tf_op jit(solution)/shard_map/conditional.1
  300.7 43.0 %copy-start.152 = (s32[1,1,16]{2,1,0:T(1,128)S(1)}, s32[1,1,16]{2,1,0:T(1,128)}, u32[]{:S(2)}) copy-start(s32[1,1,16]{2,1,0:T(1,128)} %get-tuple-element.332) | copy-start | bytes 196 | tf_op jit(solution)/shard_map/conditional.1
  343.8 199.4 %slice-start = ((s8[4718592]{0:T(1024)(128)(4,1)}), s8[524288]{0:T(1024)(128)(4,1)S(1)}, s32[]{:S(2)}) async-start(s8[4718592]{0:T(1024)(128)(4,1)} %bitcast.634), calls=%async_computation.28 | async-start | bytes 1048576 | tf_op jit(solution)/shard_map/conditional.1
  511.3 31.9 %slice-start.1 = ((s8[4718592]{0:T(1024)(128)(4,1)}), s8[4194304]{0:T(1024)(128)(4,1)S(1)}, s32[]{:S(2)}) async-start(s8[4718592]{0:T(1024)(128)(4,1)} %bitcast.634), calls=%async_computation.29 | async-start | bytes 8388608 | tf_op jit(solution)/shard_map/conditional.1
  511.3 31.9 %copy-start.20 = (f32[2,2,768,384]{3,2,1,0:T(8,128)S(1)}, f32[2,2,768,384]{3,2,1,0:T(8,128)}, u32[]{:S(2)}) copy-start(f32[2,2,768,384]{3,2,1,0:T(8,128)} %get-tuple-element.247) | copy-start | bytes 14155780 | tf_op jit(solution)/shard_map/conditional.1
  543.2 14.8 %copy-start.15 = (f32[5,96,768]{2,1,0:T(8,128)S(1)}, f32[5,96,768]{2,1,0:T(8,128)}, u32[]{:S(2)}) copy-start(f32[5,96,768]{2,1,0:T(8,128)} %get-tuple-element.1068) | copy-start | bytes 4423684 | tf_op jit(solution)/shard_map/conditional.1
  543.2 14.8 %copy-start.16 = (f32[5,96,768]{2,1,0:T(8,128)S(1)}, f32[5,96,768]{2,1,0:T(8,128)}, u32[]{:S(2)}) copy-start(f32[5,96,768]{2,1,0:T(8,128)} %get-tuple-element.1069) | copy-start | bytes 4423684 | tf_op jit(solution)/shard_map/conditional.1
  543.2 14.8 %copy-start.32 = (f32[5,96,768]{2,1,0:T(8,128)S(1)}, f32[5,96,768]{2,1,0:T(8,128)}, u32[]{:S(2)}) copy-start(f32[5,96,768]{2,1,0:T(8,128)} %get-tuple-element.245) | copy-start | bytes 4423684 | tf_op jit(solution)/shard_map/conditional.1
  562.0 2.6 copy-start.57
  562.0 2.6 copy-start.58
  562.0 2.6 copy-start.62
  562.0 2.6 copy-start.78
  562.0 2.6 copy-start.170
  562.0 21.2 %copy-start.73 = (f32[6,768]{1,0:T(8,128)S(1)}, f32[6,768]{1,0:T(8,128)}, u32[]{:S(2)}) copy-start(f32[6,768]{1,0:T(8,128)} %get-tuple-element.249) | copy-start | bytes 55300 | tf_op jit(solution)/shard_map/conditional.1
  562.0 190.0 %copy-start.18 = (f32[5,96,768]{2,1,0:T(8,128)S(1)}, f32[5,96,768]{2,1,0:T(8,128)}, u32[]{:S(2)}) copy-start(f32[5,96,768]{2,1,0:T(8,128)} %get-tuple-element.246) | copy-start | bytes 4423684 | tf_op jit(solution)/shard_map/conditional.1
  752.0 3.3 copy-start.23
  783.5 4.7 copy-start.11
  783.5 4.9 copy-start.41
  783.5 4.9 copy-start.96
  783.5 4.9 copy-start.97
  783.5 4.9 copy-start.177
  783.5 4.9 copy-start.178
Sparse Core Ops, SparseCore 0:
  10.2 65.1 all-gather.25
  280.4 63.3 all-gather.23
  562.2 189.7 all-reduce.11

commit v3 on v2

--- a/solution.py
+++ b/solution.py
@@ -178,69 +178,268 @@
     return 0.5 * (1.0 + t) + 0.5 * u * (1.0 - t * t) * GELU_C * (1.0 + 3.0 * 0.044715 * u * u)
 
 
+class Links:
+    def __init__(self, n, send, recv):
+        self.n, self.send, self.recv = n, send, recv
+        self.me = lax.axis_index("fsdp")
+
+    def others(self, body):
+        def one_step(k, carry):
+            body(k, lax.rem(self.me + k, self.n))
+            return carry
+
+        lax.fori_loop(1, self.n, one_step, 0)
+
+    def link(self, which, k, source, target, peer, origin):
+        return pltpu.make_async_remote_copy(
+            src_ref=source,
+            dst_ref=target,
+            send_sem=self.send.at[which, k],
+            recv_sem=self.recv.at[which, origin],
+            device_id={"fsdp": peer},
+            device_id_type=MESH,
+        )
+
+    def greet(self, extra=0):
+        barrier = pltpu.get_barrier_semaphore()
+        self.others(
+            lambda k, peer: pl.semaphore_signal(
+                barrier, inc=1, device_id={"fsdp": peer}, device_id_type=MESH
+            )
+        )
+        return barrier
+
+    def spread(self, which, buffer):
+        me = self.me
+        self.others(
+            lambda k, peer: self.link(which, k, buffer.at[me], buffer.at[me], peer, me).start()
+        )
+
+    def deal(self, which, source, target):
+        me = self.me
+        self.others(
+            lambda k, peer: self.link(which, k, source.at[peer], target.at[me], peer, me).start()
+        )
+
+    def arrive(self, which, target):
+        self.others(
+            lambda k, peer: self.link(
+                which, k, target.at[peer], target.at[peer], peer, peer
+            ).wait_recv()
+        )
+
+    def sent(self, which, source):
+        me = self.me
+        self.others(
+            lambda k, peer: self.link(
+                which, k, source.at[peer], source.at[peer], peer, me
+            ).wait_send()
+        )
+
+    def partners(self, body):
+        def one_step(k, carry):
+            body(k, lax.rem(self.me + 2 * k, self.n))
+            return carry
+
+        lax.fori_loop(1, self.n // 2, one_step, 0)
+
+    def relay(self, which, buffer):
+        me, twin = self.me, self.me + 1 - 2 * lax.rem(self.me, 2)
+        self.link(which, self.n // 2, buffer.at[me], buffer.at[me], twin, me).start()
+        self.partners(
+            lambda k, peer: self.link(which, k, buffer.at[me], buffer.at[me], peer, me).start()
+        )
+
+    def relayed(self, which, buffer):
+        me, twin = self.me, self.me + 1 - 2 * lax.rem(self.me, 2)
+        n = self.n
+
+        def pass_on(k, peer):
+            copy = self.link(which, k, buffer.at[peer], buffer.at[peer], peer, peer)
+            copy.wait_recv()
+            self.link(which, n // 2 + k, buffer.at[peer], buffer.at[peer], twin, peer).start()
+
+        self.partners(pass_on)
+
+        def got(k, carry):
+            origin = lax.rem(twin + 2 * k, n)
+            self.link(which, k, buffer.at[origin], buffer.at[origin], twin, origin).wait_recv()
+            return carry
+
+        lax.fori_loop(0, n // 2, got, 0)
+
+    def relay_sent(self, which, buffer):
+        def gone(k, carry):
+            peer = lax.rem(self.me + 1, self.n)
+            self.link(which, k, buffer.at[0], buffer.at[0], peer, 0).wait_send()
+            return carry
+
+        lax.fori_loop(1, self.n, gone, 0)
+
+
+def tiles_of(vocab_rows, body, carry):
+    whole = vocab_rows // TILE
+    carry = lax.fori_loop(
+        0, whole, lambda i, c: body(i, pl.multiple_of(i * TILE, TILE), TILE, c), carry
+    )
+    if vocab_rows % TILE:
+        carry = body(whole, whole * TILE, vocab_rows % TILE, carry)
+    return carry
+
+
 def rows_at_once(n, slots):
     return max(g for g in range(1, n + 1) if n % g == 0 and g * slots <= 512)
 
 
+def share_kernel(n, groups, packed, everyone, worst, marks, send, recv, mark_send, mark_recv):
+    links = Links(n, send, recv)
+    me = links.me
+    group = lax.axis_index("grp")
+
+    def other_groups(body):
+        for k in range(1, groups):
+            body(k, lax.rem(group + k, groups))
+
+    barrier = links.greet()
+    other_groups(
+        lambda k, peer: pl.semaphore_signal(
+            barrier, inc=1, device_id={"grp": peer}, device_id_type=MESH
+        )
+    )
+    pl.semaphore_wait(barrier, n - 1 + groups - 1)
+    everyone[me] = packed[...]
+    links.spread(0, everyone)
+    links.arrive(0, everyone)
+    most = everyone[0]
+    for j in range(1, n):
+        most = jnp.maximum(most, everyone[j])
+    marks[group] = jnp.broadcast_to(most[:1, -128:], (8, 128))
+
+    def mark(k, peer, origin):
+        return pltpu.make_async_remote_copy(
+            src_ref=marks.at[origin],
+            dst_ref=marks.at[origin],
+            send_sem=mark_send.at[k],
+            recv_sem=mark_recv.at[origin],
+            device_id={"grp": peer},
+            device_id_type=MESH,
+        )
+
+    other_groups(lambda k, peer: mark(k, peer, group).start())
+    other_groups(lambda k, peer: mark(k, peer, peer).wait_recv())
+    most = marks[0]
+    for j in range(1, groups):
+        most = jnp.maximum(most, marks[j])
+    worst[...] = most
+    links.sent(0, everyone)
+    other_groups(lambda k, peer: mark(k, peer, group).wait_send())
+
+
+def share(n, packed):
+    groups = lax.axis_size("grp")
+    vmem = pl.BlockSpec(memory_space=pltpu.VMEM)
+    return pl.pallas_call(
+        functools.partial(share_kernel, n, groups),
+        out_shape=(
+            jax.ShapeDtypeStruct((n,) + packed.shape, jnp.int32),
+            jax.ShapeDtypeStruct((8, 128), jnp.int32),
+        ),
+        in_specs=[vmem],
+        out_specs=(vmem, vmem),
+        scratch_shapes=[
+            pltpu.VMEM((groups, 8, 128), jnp.int32),
+            pltpu.SemaphoreType.DMA((1, n)),
+            pltpu.SemaphoreType.DMA((1, n)),
+            pltpu.SemaphoreType.DMA((groups,)),
+            pltpu.SemaphoreType.DMA((groups,)),
+        ],
+        compiler_params=pltpu.CompilerParams(collective_id=1, has_side_effects=True),
+        name="share_ids",
+    )(packed)
+
+
+def fetch_kernel(dims, ints, eb, x_out, id_s, xs, xr, send, recv):
+    n, slots, vocab_rows, tokens, row_count = dims
+    turned = ints[...].astype(F32).T.astype(jnp.int32)
+    id_s[...] = turned[: n * slots, 0:1]
+    slot_col = turned[:tokens, 1:2]
+    links = Links(n, send, recv)
+    me = links.me
+    group = rows_at_once(n, slots)
+    chunk = group * slots
+    pl.semaphore_wait(links.greet(), n - 1)
+
+    def look(c, carry):
+        ids = id_s[pl.ds(pl.multiple_of(c * chunk, chunk), chunk), :]
+
+        def add(i, start, size, acc):
+            hit = (lanes((chunk, size)) + start == ids).astype(F32).astype(LOW)
+            return acc + dot_nn(hit, eb[pl.ds(start, size), :])
+
+        found = tiles_of(vocab_rows, add, jnp.zeros((chunk, D), F32))
+        xs[pl.ds(c * group, group)] = found.astype(LOW).reshape(group, slots, D)
+        return carry
+
+    lax.fori_loop(0, n // group, look, 0)
+    links.deal(0, xs, xr)
+    xr[me] = xs[me]
+    links.arrive(0, xr)
+    x = jnp.zeros((tokens, D), F32)
+    for c in range(n // group):
+        hit = (lanes((tokens, chunk)) + c * chunk == slot_col).astype(F32).astype(LOW)
+        x = x + dot_nn(hit, xr[c * group : (c + 1) * group].reshape(chunk, D))
+    x_out[...] = x.astype(LOW)
+    links.sent(0, xs)
+
+
+def fetch(n, slots, sizes, ints, embed_low):
+    vmem = pl.BlockSpec(memory_space=pltpu.VMEM)
+    vocab_rows = embed_low.shape[0]
+    return pl.pallas_call(
+        functools.partial(fetch_kernel, (n, slots, vocab_rows) + sizes),
+        out_shape=jax.ShapeDtypeStruct((sizes[0], D), LOW),
+        in_specs=[vmem] * 2,
+        out_specs=vmem,
+        scratch_shapes=[
+            pltpu.VMEM((n * slots, 1), jnp.int32),
+            pltpu.VMEM((n, slots, D), LOW),
+            pltpu.VMEM((n, slots, D), LOW),
+            pltpu.SemaphoreType.DMA((1, n)),
+            pltpu.SemaphoreType.DMA((1, n)),
+        ],
+        compiler_params=pltpu.CompilerParams(
+            collective_id=2, has_side_effects=True, vmem_limit_bytes=40 * 1024 * 1024
+        ),
+        name="fetch_rows",
+    )(ints, embed_low)
+
+
 def step_kernel(
     dims,
-    id_col, id_lane, slot_col, slot_lane, pick_col, pick_lane, seg_rows, seg_lane,
-    route_col, route_all, target_lane, vec, eb, attn, expw,
+    ints, vec, x_low, eb_in, attn_in, expw_in,
     dembed_out, dattn_out, dexp_out, dvec_out, loss_out,
-    xs, xr, gr, ball, ys, yr, rows, tops, drs, drr, dyall, dbs, dbr,
+    eb, attn, expw, xs, gr, ball, ys, yr, rows, tops, drs, drr, dyall, dbs, dbr,
     one, pas, par, two, dss, dsr, dvec, logit_s, dlog_s, pre_s, hid_s, dpre_s, flip_s, tile_s,
-    send, recv, out_sem,
+    send, recv, out_sem, load_sem,
 ):
-    n, slots, vocab, vocab_rows, hidden = dims
-    row_count = pick_col.shape[0]
-    tokens = slot_col.shape[0]
+    n, slots, vocab, vocab_rows, hidden, tokens, row_count = dims
     all_rows = n * row_count
     wide = HEADS * row_count
     shard = D // n
     row_total = float(all_rows)
     scale = 2.0 * D ** (-0.5)
     factor_qk = HEAD_DIM ** (-0.5)
-    me = lax.axis_index("fsdp")
-
-    def others(body):
-        def one_step(k, carry):
-            body(k, lax.rem(me + k, n))
-            return carry
-
-        lax.fori_loop(1, n, one_step, 0)
-
-    def link(which, k, source, target, peer, origin):
-        return pltpu.make_async_remote_copy(
-            src_ref=source,
-            dst_ref=target,
-            send_sem=send.at[which, k],
-            recv_sem=recv.at[which, origin],
-            device_id={"fsdp": peer},
-            device_id_type=MESH,
-        )
-
-    def spread(which, buffer):
-        others(lambda k, peer: link(which, k, buffer.at[me], buffer.at[me], peer, me).start())
-
-    def deal(which, source, target):
-        others(lambda k, peer: link(which, k, source.at[peer], target.at[me], peer, me).start())
-
-    def arrive(which, target):
-        others(
-            lambda k, peer: link(which, k, target.at[peer], target.at[peer], peer, peer).wait_recv()
-        )
-
-    def sent(which, source):
-        others(lambda k, peer: link(which, k, source.at[peer], source.at[peer], peer, me).wait_send())
-
-    def tiled(body, carry):
-        whole = vocab_rows // TILE
-        carry = lax.fori_loop(
-            0, whole, lambda i, c: body(i, pl.multiple_of(i * TILE, TILE), TILE, c), carry
-        )
-        if vocab_rows % TILE:
-            carry = body(whole, whole * TILE, vocab_rows % TILE, carry)
-        return carry
+    links = Links(n, send, recv)
+    me = links.me
+    spread, deal, arrive, sent = links.spread, links.deal, links.arrive, links.sent
+    relay, relayed = links.relay, links.relayed
+    tiled = functools.partial(tiles_of, vocab_rows)
+    loads = [
+        pltpu.make_async_copy(source, target, load_sem.at[i])
+        for i, (source, target) in enumerate(((attn_in, attn), (expw_in, expw), (eb_in, eb)))
+    ]
+    for load in loads:
+        load.start()
 
     def added(buffer):
         total = buffer[0].astype(F32)
@@ -248,43 +447,23 @@
             total = total + buffer[j].astype(F32)
         return total
 
-    barrier = pltpu.get_barrier_semaphore()
-    others(
-        lambda k, peer: pl.semaphore_signal(
-            barrier, inc=1, device_id={"fsdp": peer}, device_id_type=MESH
-        )
-    )
-    pl.semaphore_wait(barrier, n - 1)
-
+    pl.semaphore_wait(links.greet(), n - 1)
     group = rows_at_once(n, slots)
     chunk = group * slots
-
-    def look(c, carry):
-        ids = id_col[pl.ds(pl.multiple_of(c * chunk, chunk), chunk), :]
-
-        def add(i, start, size, acc):
-            hit = (lanes((chunk, size)) + start == ids).astype(F32).astype(LOW)
-            return acc + dot_nn(hit, eb[pl.ds(start, size), :])
-
-        found = tiled(add, jnp.zeros((chunk, D), F32))
-        xs[pl.ds(c * group, group)] = found.astype(LOW).reshape(group, slots, D)
-        return carry
-
-    lax.fori_loop(0, n // group, look, 0)
-    deal(X_IN, xs, xr)
-    xr[me] = xs[me]
-    arrive(X_IN, xr)
-    x = jnp.zeros((tokens, D), F32)
-    for c in range(n // group):
-        hit = (lanes((tokens, chunk)) + c * chunk == slot_col[...]).astype(F32).astype(LOW)
-        x = x + dot_nn(hit, xr[c * group : (c + 1) * group].reshape(chunk, D))
+    x = x_low[...].astype(F32)
+    id_lane, slot_lane, pick_lane = ints[0:1, : n * slots], ints[1:2, :tokens], ints[2:3, :row_count]
+    seg_lane, target_lane = ints[4:5, :tokens], ints[7:8, : 2 * all_rows]
+    turned = ints[...].astype(F32).T.astype(jnp.int32)
+    pick_col, seg_rows = turned[:row_count, 2:3], turned[:row_count, 3:4]
+    route_col, route_all = turned[:row_count, 5:6], turned[:all_rows, 6:7]
 
     gain_a, gain_b, gain_c, gain_d = (vec[i : i + 1, :] for i in range(4))
     x_factor = norm_factor(x)
     a = (x * x_factor * gain_a).astype(LOW)
-    pick = (lanes((row_count, tokens)) == pick_col[...]).astype(F32).astype(LOW)
-    x_rows = dot_nn(pick, x.astype(LOW))
+    pick = (lanes((row_count, tokens)) == pick_col).astype(F32).astype(LOW)
+    x_rows = dot_nn(pick, x_low[...])
     a_rows = dot_nn(pick, a).astype(LOW)
+    loads[0].wait()
     q = dot_nn(a_rows, attn[0]).astype(LOW)
     k = dot_nn(a, attn[1]).astype(LOW)
     v = dot_nn(a, attn[2]).astype(LOW)
@@ -303,7 +482,7 @@
 
     q_wide = widen(q)
     scores = dot_nt(q_wide, k) * factor_qk
-    allowed = (lanes((row_count, tokens)) <= pick_col[...]) & (seg_lane[...] == seg_rows[...])
+    allowed = (lanes((row_count, tokens)) <= pick_col) & (seg_lane == seg_rows)
     scores = jnp.where(
         allowed[None], scores.reshape(HEADS, row_count, tokens), -1e30
     ).reshape(wide, tokens)
@@ -325,20 +504,23 @@
     router_exp = [jnp.exp(value - highest) for value in router_logits]
     router_sum = sum(router_exp[1:], router_exp[0])
     router_probs = [value / router_sum for value in router_exp]
-    chosen = [(route_col[...] == e).astype(F32) for e in range(EXPERTS)]
+    chosen = [(route_col == e).astype(F32) for e in range(EXPERTS)]
     gate = sum([p * c for p, c in zip(router_probs[1:], chosen[1:])], router_probs[0] * chosen[0])
-    one[me, 0] = a_rows
-    one[me, 1] = o
-    one[me, 2] = q
+    one[me] = q
     a_turned = a.astype(F32).T.astype(LOW)
-    pas[...] = dot_nt(a_turned, probs_low).reshape(n, shard, wide).astype(LOW)
+    eye = (sublanes((row_count, row_count)) == lanes((row_count, row_count))).astype(F32).astype(LOW)
+    flipped = lambda low_rows: dot_tn(low_rows, eye)
+    pas[:, :, 0:wide] = dot_nt(a_turned, probs_low).reshape(n, shard, wide).astype(LOW)
+    pas[:, :, wide : wide + row_count] = flipped(a_rows).reshape(n, shard, row_count).astype(LOW)
+    pas[:, :, wide + row_count :] = flipped(o).reshape(n, shard, row_count).astype(LOW)
     arrive(B_ROWS, ball)
+    loads[1].wait()
     b_all = ball[...].reshape(all_rows, D)
     y_part = jnp.zeros((all_rows, D), F32)
     for e in range(EXPERTS):
         pre = dot_nn(b_all, expw[e, 0])
         pre_s[e] = pre
-        hid = jnp.where(route_all[...] == e, gelu_of(pre), 0.0).astype(LOW)
+        hid = jnp.where(route_all == e, gelu_of(pre), 0.0).astype(LOW)
         hid_s[e] = hid
         y_part = y_part + dot_nt(hid, expw[e, 1])
     ys[...] = y_part.astype(LOW).reshape(n, row_count, D)
@@ -354,16 +536,16 @@
     middle_factor = norm_factor(middle)
     rows[me, 0] = first
     rows[me, 1] = (middle * middle_factor * gain_d).astype(LOW)
-    spread(HEAD_ROWS, rows)
-    spread(ROWS_ONE, one)
+    relay(HEAD_ROWS, rows)
+    relayed(HEAD_ROWS, rows)
     deal(P_A, pas, par)
     par[me] = pas[me]
-    arrive(HEAD_ROWS, rows)
+    loads[2].wait()
     loss_rows = 2 * all_rows
     head_rows = rows[...].reshape(loss_rows, D)
 
     def target_hit(start, size):
-        return sublanes((size, loss_rows)) + start == target_lane[...]
+        return sublanes((size, loss_rows)) + start == target_lane
 
     def logits_tile(i, start, size, carry):
         top, total, at_target = carry
@@ -387,6 +569,7 @@
     )
     spread(TOPS, tops)
     arrive(TOPS, tops)
+    relay(ROWS_ONE, one)
     top = tops[0, 0:1]
     for j in range(1, n):
         top = jnp.maximum(top, tops[j, 0:1])
@@ -425,7 +608,7 @@
     db_part = jnp.zeros((all_rows, D), F32)
     for e in range(EXPERTS):
         dhid = dot_nn(dy_all, expw[e, 1])
-        slope = jnp.where(route_all[...] == e, gelu_slope(pre_s[e]), 0.0)
+        slope = jnp.where(route_all == e, gelu_slope(pre_s[e]), 0.0)
         dpre = (slope * dhid).astype(LOW)
         dpre_s[e] = dpre
         db_part = db_part + dot_nt(dpre, expw[e, 0])
@@ -470,28 +653,33 @@
     dinput = dot_nt(dk, attn[1]) + dot_nt(dv, attn[2])
     dx, gain_attn = norm_grad(x, x_factor, gain_a, dinput)
     row_back, gain_more = norm_grad(x_rows, norm_factor(x_rows), gain_a, dot_nt(dq, attn[0]))
-    spots = (sublanes((tokens, row_count)) == pick_lane[...]).astype(F32)
+    spots = (sublanes((tokens, row_count)) == pick_lane).astype(F32)
     dx = dx + lax.dot_general(
         spots, row_back + dx_attn, (((1,), (0,)), ((), ())), precision=HIGH,
         preferred_element_type=F32,
     )
     dx_low = dx.astype(LOW)
-    sent(X_IN, xs)
     for c in range(n // group):
-        hit = (sublanes((chunk, tokens)) + c * chunk == slot_lane[...]).astype(F32).astype(LOW)
+        hit = (sublanes((chunk, tokens)) + c * chunk == slot_lane).astype(F32).astype(LOW)
         xs[c * group : (c + 1) * group] = dot_nn(hit, dx_low).astype(LOW).reshape(group, slots, D)
     deal(G_OUT, xs, gr)
     gr[me] = xs[me]
-    spread(ROWS_TWO, two)
+    relay(ROWS_TWO, two)
     dss[...] = dot_nt(a_turned, dscores).reshape(n, shard, wide).astype(LOW)
     deal(DS_A, dss, dsr)
     dsr[me] = dss[me]
 
-    arrive(ROWS_ONE, one)
+    relayed(ROWS_ONE, one)
     arrive(P_A, par)
-    arrive(ROWS_TWO, two)
+    relayed(ROWS_TWO, two)
     arrive(DS_A, dsr)
     mine = pl.ds(pl.multiple_of(me * shard, 8), shard)
+
+    def own_slices(start, right):
+        total = jnp.zeros((shard, D), F32)
+        for j in range(n):
+            total = total + dot_nn(par[j, :, start : start + row_count], right[j])
+        return total
 
     def own_rows(left, right):
         flip_s[...] = left.astype(F32).reshape(all_rows, D).T
@@ -500,13 +688,13 @@
     dkey = jnp.zeros((shard, D), F32)
     dvalue = jnp.zeros((shard, D), F32)
     for j in range(n):
-        dkey = dkey + dot_nn(dsr[j], widen(one[j, 2]))
-        dvalue = dvalue + dot_nn(par[j], widen(two[j, 0]))
+        dkey = dkey + dot_nn(dsr[j], widen(one[j]))
+        dvalue = dvalue + dot_nn(par[j, :, 0:wide], widen(two[j, 0]))
     parts = (
-        own_rows(one[:, 0], two[:, 1]),
+        own_slices(wide, two[:, 1]),
         dkey * factor_qk,
         dvalue,
-        ATTN_GAIN * own_rows(one[:, 1], two[:, 2]),
+        ATTN_GAIN * own_slices(wide + row_count, two[:, 2]),
         own_rows(rows[:, 0], two[:, 3]),
     )
     for i, part in enumerate(parts):
@@ -559,31 +747,27 @@
     for i, start, size in tiles[-2:]:
         leave(i, start, size).wait()
     for which, source in (
-        (B_ROWS, ball), (Y_PART, ys), (HEAD_ROWS, rows), (TOPS, tops), (D_ROWS, drs),
-        (DY_ROWS, dyall), (DB_PART, dbs), (ROWS_ONE, one), (P_A, pas), (ROWS_TWO, two),
-        (DS_A, dss), (G_OUT, xs), (D_VEC, dvec),
+        (B_ROWS, ball), (Y_PART, ys), (TOPS, tops), (D_ROWS, drs), (DY_ROWS, dyall),
+        (DB_PART, dbs), (P_A, pas), (DS_A, dss), (G_OUT, xs), (D_VEC, dvec),
     ):
         sent(which, source)
-
-
-def run_step(n, slots, vocab, number, ints, vec, embed_low, attn_low, expert_low):
-    vocab_rows = -(-vocab // 16) * 16
-    if vocab_rows != vocab:
-        embed_low = jnp.pad(embed_low, ((0, vocab_rows - vocab), (0, 0)))
-    row_count = ints["pick_col"].shape[0]
+    for which, source in ((HEAD_ROWS, rows), (ROWS_ONE, one), (ROWS_TWO, two)):
+        links.relay_sent(which, source)
+
+
+def run_step(n, slots, vocab, sizes, ints, vec, x_low, embed_low, attn_low, expert_low):
+    vocab_rows = embed_low.shape[0]
+    row_count = sizes[1]
     hidden = expert_low.shape[3]
     shard = D // n
     all_rows = n * row_count
     wide = HEADS * row_count
     vmem = pl.BlockSpec(memory_space=pltpu.VMEM)
+    anywhere = pl.BlockSpec(memory_space=pl.ANY)
     low = lambda *shape: pltpu.VMEM(shape, LOW)
     wide_float = lambda *shape: pltpu.VMEM(shape, F32)
-    names = (
-        "id_col", "id_lane", "slot_col", "slot_lane", "pick_col", "pick_lane", "seg_rows",
-        "seg_lane", "route_col", "route_all", "target_lane",
-    )
     outs = pl.pallas_call(
-        functools.partial(step_kernel, (n, slots, vocab, vocab_rows, hidden)),
+        functools.partial(step_kernel, (n, slots, vocab, vocab_rows, hidden) + sizes),
         out_shape=(
             jax.ShapeDtypeStruct((vocab_rows, D), F32),
             jax.ShapeDtypeStruct((5, shard, D), F32),
@@ -591,15 +775,17 @@
             jax.ShapeDtypeStruct((8, D), F32),
             jax.ShapeDtypeStruct((8, 128), F32),
         ),
-        in_specs=[vmem] * 15,
-        out_specs=(pl.BlockSpec(memory_space=pl.ANY), vmem, vmem, vmem, vmem),
+        in_specs=[vmem] * 3 + [anywhere] * 3,
+        out_specs=(anywhere, vmem, vmem, vmem, vmem),
         scratch_shapes=[
-            low(n, slots, D), low(n, slots, D), low(n, slots, D),
+            low(vocab_rows, D), low(5, D, D), low(EXPERTS, 2, D, hidden),
+            low(n, slots, D), low(n, slots, D),
             low(n, row_count, D), low(n, row_count, D), low(n, row_count, D),
             low(n, 2, row_count, D), wide_float(n, 8, 2 * all_rows),
             low(n, 2 * row_count, D), low(n, 2 * row_count, D),
             low(n, row_count, D), low(n, row_count, D), low(n, row_count, D),
-            low(n, 3, row_count, D), low(n, shard, wide), low(n, shard, wide),
+            low(n, row_count, D), low(n, shard, wide + 2 * row_count),
+            low(n, shard, wide + 2 * row_count),
             low(n, 4, row_count, D), low(n, shard, wide), low(n, shard, wide),
             wide_float(n, 8, D),
             wide_float(vocab_rows, 2 * all_rows), low(vocab_rows, 2 * all_rows),
@@ -608,13 +794,162 @@
             pltpu.SemaphoreType.DMA((EXCHANGES, n)),
             pltpu.SemaphoreType.DMA((EXCHANGES, n)),
             pltpu.SemaphoreType.DMA((2,)),
+            pltpu.SemaphoreType.DMA((3,)),
         ],
         compiler_params=pltpu.CompilerParams(
-            collective_id=number, has_side_effects=True, vmem_limit_bytes=60 * 1024 * 1024
+            collective_id=3, has_side_effects=True, vmem_limit_bytes=60 * 1024 * 1024
         ),
         name="inner_step",
-    )(*[ints[name] for name in names], vec, embed_low, attn_low, expert_low)
+    )(ints, vec, x_low, embed_low, attn_low, expert_low)
     return (outs[0][:vocab],) + outs[1:]
+
+
+def sum_kernel(dims, value, vector, total, vector_total, held, first_in, second_in, rest, flat, *sems):
+    rows, quarter, pieces = dims
+    one_s, one_r, two_s, two_r, three_s, three_r, four_s, four_r, rest_s, rest_r = sems
+    group = lax.axis_index("grp")
+    size, width = quarter // pieces, D // 2
+    bits = (lax.rem(group, 2), lax.div(group, 2))
+    flip = lambda bit: group + (1 - 2 * bits[bit]) * (1 + bit)
+    barrier = pltpu.get_barrier_semaphore()
+    for k in range(1, 4):
+        pl.semaphore_signal(
+            barrier, inc=1, device_id={"grp": lax.rem(group + k, 4)}, device_id_type=MESH
+        )
+    pl.semaphore_wait(barrier, 3)
+
+    def place(side, first_bit, second_bit, piece):
+        owner = first_bit + 2 * second_bit if side == 0 else second_bit + 2 * first_bit
+        start = pl.multiple_of((owner * pieces + piece) * size, 16)
+        return pl.ds(start, size), pl.ds(side * width, width)
+
+    def copy(source, target, send, recv, peer):
+        return pltpu.make_async_remote_copy(
+            src_ref=source, dst_ref=target, send_sem=send, recv_sem=recv,
+            device_id={"grp": peer}, device_id_type=MESH,
+        )
+
+    units = [(side, piece) for piece in range(pieces) for side in range(2)]
+
+    def stage_one(u, turn):
+        side, piece = units[u]
+        here, there = bits[side], bits[1 - side]
+        second = there if turn else 1 - there
+        out = place(side, 1 - here, second, piece)
+        return copy(value.at[out], first_in.at[u, turn], one_s.at[u, turn], one_r.at[u, turn], flip(side))
+
+    def stage_two(u):
+        side, piece = units[u]
+        return copy(held.at[u, 0], second_in.at[u], two_s.at[u], two_r.at[u], flip(1 - side))
+
+    def stage_three(u):
+        side, piece = units[u]
+        own = place(side, bits[side], bits[1 - side], piece)
+        return copy(total.at[own], total.at[own], three_s.at[u], three_r.at[u], flip(1 - side))
+
+    def stage_four(u, turn):
+        side, piece = units[u]
+        there = bits[1 - side]
+        own = place(side, bits[side], there if turn == 0 else 1 - there, piece)
+        return copy(total.at[own], total.at[own], four_s.at[u, turn], four_r.at[u, turn], flip(side))
+
+    main = 4 * quarter
+    spare = rows - main
+    flat[group] = vector[...]
+    if spare:
+        rest[group, 0:spare] = value[main:rows]
+
+    def small(which, k, peer, origin):
+        buffer = (rest, flat)[which]
+        return copy(
+            buffer.at[origin], buffer.at[origin], rest_s.at[which, k], rest_r.at[which, origin], peer
+        )
+
+    for u in range(len(units)):
+        stage_one(u, 0).start()
+    for u in range(len(units)):
+        stage_one(u, 1).start()
+    smalls = (0, 1) if spare else (1,)
+    for which in smalls:
+        for k in range(1, 4):
+            small(which, k, lax.rem(group + k, 4), group).start()
+    for u, (side, piece) in enumerate(units):
+        stage_one(u, 0).wait_recv()
+        passed = place(side, bits[side], 1 - bits[1 - side], piece)
+        held[u, 0] = (value[passed].astype(F32) + first_in[u, 0].astype(F32)).astype(LOW)
+        stage_two(u).start()
+    for u, (side, piece) in enumerate(units):
+        stage_one(u, 1).wait_recv()
+        kept = place(side, bits[side], bits[1 - side], piece)
+        held[u, 1] = (value[kept].astype(F32) + first_in[u, 1].astype(F32)).astype(LOW)
+    for u, (side, piece) in enumerate(units):
+        stage_two(u).wait_recv()
+        kept = place(side, bits[side], bits[1 - side], piece)
+        total[kept] = (held[u, 1].astype(F32) + second_in[u].astype(F32)).astype(LOW)
+        stage_three(u).start()
+        stage_four(u, 0).start()
+    for u, (side, piece) in enumerate(units):
+        come = place(side, bits[side], 1 - bits[1 - side], piece)
+        copy(total.at[come], total.at[come], three_s.at[u], three_r.at[u], flip(1 - side)).wait_recv()
+        stage_four(u, 1).start()
+    for which in smalls:
+        for k in range(1, 4):
+            origin = lax.rem(group + k, 4)
+            small(which, k, origin, origin).wait_recv()
+    added = lambda buffer: (buffer[0].astype(F32) + buffer[1].astype(F32)) + (
+        buffer[2].astype(F32) + buffer[3].astype(F32)
+    )
+    vector_total[...] = added(flat)
+    if spare:
+        total[main:rows] = added(rest)[0:spare].astype(LOW)
+    for u, (side, piece) in enumerate(units):
+        there = bits[1 - side]
+        for turn in range(2):
+            come = place(side, 1 - bits[side], there if turn == 0 else 1 - there, piece)
+            copy(
+                total.at[come], total.at[come], four_s.at[u, turn], four_r.at[u, turn], flip(side)
+            ).wait_recv()
+    for u in range(len(units)):
+        stage_one(u, 0).wait_send()
+        stage_one(u, 1).wait_send()
+        stage_two(u).wait_send()
+        stage_three(u).wait_send()
+        stage_four(u, 0).wait_send()
+        stage_four(u, 1).wait_send()
+    for which in smalls:
+        for k in range(1, 4):
+            small(which, k, lax.rem(group + k, 4), group).wait_send()
+
+
+def sum_over_groups(value, vector):
+    rows = value.shape[0]
+    quarter = rows // 64 * 16
+    pieces = 2 if quarter % 32 == 0 else 1
+    spare = -(-(rows - 4 * quarter) // 16) * 16
+    size, units = quarter // pieces, 2 * pieces
+    vmem = pl.BlockSpec(memory_space=pltpu.VMEM)
+    block = lambda *lead: pltpu.VMEM(lead + (size, D // 2), LOW)
+    dma = pltpu.SemaphoreType.DMA
+    return pl.pallas_call(
+        functools.partial(sum_kernel, (rows, quarter, pieces)),
+        out_shape=(
+            jax.ShapeDtypeStruct(value.shape, LOW),
+            jax.ShapeDtypeStruct(vector.shape, F32),
+        ),
+        in_specs=[vmem, vmem],
+        out_specs=(vmem, vmem),
+        scratch_shapes=[
+            block(units, 2), block(units, 2), block(units),
+            pltpu.VMEM((4, max(spare, 16), D), LOW), pltpu.VMEM((4,) + vector.shape, F32),
+            dma((units, 2)), dma((units, 2)), dma((units,)), dma((units,)), dma((units,)),
+            dma((units,)), dma((units, 2)), dma((units, 2)), dma((2, 4)), dma((2, 4)),
+        ],
+        compiler_params=pltpu.CompilerParams(
+            collective_id=4, has_side_effects=True, vmem_limit_bytes=48 * 1024 * 1024
+        ),
+        cost_estimate=pl.CostEstimate(flops=0, bytes_accessed=300_000_000, transcendentals=0),
+        name="sum_groups",
+    )(value, vector)
 
 
 def prepare(n, slots, vocab, tokens, routes, segments, loss_pos):
@@ -638,32 +973,27 @@
     )
     row_routes = jnp.sum(jnp.where(picked, routes[:, None, :], 0), axis=2)
     row_segs = jnp.sum(jnp.where(picked, segments[:, None, :], 0), axis=2)
-    most = jnp.broadcast_to(jnp.max(jnp.where(first, rank, 0)), (steps, 1))
-    packed = jnp.concatenate([ids, row_routes, shifted(1), shifted(2), most], axis=1)
-    world = lax.all_gather(packed, ("grp", "fsdp"))
-    fits = jnp.max(world[:, 0, -1]) < slots
-    everyone = lax.dynamic_slice_in_dim(world, lax.axis_index("grp") * n, n, axis=0)[:, :, :-1]
+    most = jnp.broadcast_to(jnp.max(jnp.where(first, rank, 0)), (steps, 128))
+    filler = jnp.zeros((steps, -(n * slots + 3 * row_count) % 128), jnp.int32)
+    packed = jnp.concatenate([ids, row_routes, shifted(1), shifted(2), filler, most], axis=1)
+    everyone, worst = share(n, packed)
+    fits = worst[0, 127] < slots
     wanted = lax.dynamic_slice_in_dim(everyone, lax.axis_index("fsdp") * slots, slots, axis=2) - start
     after = n * slots
-    result = []
-    for s in range(steps):
-        want = wanted[:, s].reshape(n * slots)
-        targets = everyone[:, s, after + row_count :].reshape(1, n * 2 * row_count) - start
-        result.append(
-            dict(
-                id_col=want[:, None],
-                id_lane=want[None, :],
-                slot_col=slot[s][:, None],
-                slot_lane=slot[s][None, :],
-                pick_col=loss_pos[s][:, None],
-                pick_lane=loss_pos[s][None, :],
-                seg_rows=row_segs[s][:, None],
-                seg_lane=segments[s][None, :],
-                route_col=row_routes[s][:, None],
-                route_all=everyone[:, s, after : after + row_count].reshape(n * row_count, 1),
-                target_lane=targets,
-            )
-        )
+    rows = lambda part: jnp.swapaxes(part, 0, 1).reshape(steps, -1)
+    lines = [
+        rows(wanted),
+        slot,
+        loss_pos,
+        row_segs,
+        segments,
+        row_routes,
+        rows(everyone[:, :, after : after + row_count]),
+        rows(everyone[:, :, after + row_count : after + 3 * row_count]) - start,
+    ]
+    longest = -(-max(line.shape[1] for line in lines) // 128) * 128
+    fill = lambda line: jnp.pad(line, ((0, 0), (0, longest - line.shape[1])))
+    result = jnp.stack([fill(line) for line in lines], axis=1)
     return result, fits
 
 
@@ -902,6 +1232,89 @@
     )
 
 
+def adam_quick(weight, first_moment, second, gradient, step_float, rate_here, decay_here):
+    first_new = BETA_ONE * first_moment + (1.0 - BETA_ONE) * gradient
+    second_new = BETA_TWO * second + (1.0 - BETA_TWO) * gradient * gradient
+    first_hat = first_new * (1.0 / (1.0 - BETA_ONE**step_float))
+    second_hat = second_new * (1.0 / (1.0 - BETA_TWO**step_float))
+    weight_new = weight - rate_here * (
+        first_hat / (jnp.sqrt(second_hat) + ADAM_EPS) + decay_here * weight
+    )
+    return (weight_new, first_new, second_new)
+
+
+def quick_window(n, slots, sizes, steps, x_start, lows, masters, firsts, seconds, outers, row_total):
+    embedding, attention, experts, vectors = masters
+    vocab = embedding.shape[0]
+    threshold = 0.05 / math.sqrt(row_total)
+    vector_rates = jnp.where(jnp.arange(vectors.shape[0])[:, None] < 4, LR_GAIN, LR_ROUTER)
+    rate_list = (LR_EMBED, LR_MATRIX, LR_MATRIX, vector_rates)
+    decay_list = (DECAY, DECAY, DECAY, 0.0)
+    taken = []
+
+    def replay(k, factors):
+        state = (masters[k], firsts[k], seconds[k])
+        for s, factor in enumerate(factors):
+            gradient = taken[s][k] * factor
+            state = adam_quick(
+                *state, gradient, float(STEP0 + s + 1), rate_list[k], decay_list[k]
+            )
+        return state
+
+    loss_list, norm_list, factor_list = [], [], []
+    vector_state = (vectors, firsts[3], seconds[3])
+    for s in range(steps.shape[0]):
+        ints = steps[s]
+        if s:
+            again = lax.optimization_barrier(tuple(factor_list))
+            attn_low = lax.all_gather(
+                replay(1, again)[0].astype(jnp.bfloat16), "fsdp", axis=1, tiled=True
+            )
+            expert_low = replay(2, again)[0].astype(jnp.bfloat16)
+            embed_low = padded(replay(0, again)[0].astype(jnp.bfloat16))
+            x_low = fetch(n, slots, sizes, ints, embed_low)
+        else:
+            (embed_low, attn_low, expert_low), x_low = lows, x_start
+        *grads, shared, loss = run_step(
+            n, slots, vocab, sizes, ints, vector_state[0], x_low, embed_low, attn_low, expert_low
+        )
+        dvector = shared[: vectors.shape[0]]
+        norm_value = jnp.sqrt(shared[6, 0] + jnp.sum(dvector * dvector))
+        factor = jnp.minimum(1.0, threshold / norm_value)
+        taken.append(grads)
+        loss_list.append(loss[0, 0])
+        norm_list.append(norm_value)
+        factor_list.append(factor)
+        vector_gradient = dvector * factor
+        vector_state = adam_quick(
+            *vector_state, vector_gradient, float(STEP0 + s + 1), vector_rates, 0.0
+        )
+    again = lax.optimization_barrier(tuple(factor_list))
+    states = [replay(k, again) for k in range(3)] + [vector_state]
+    deltas = [master - state[0] for master, state in zip(masters, states)]
+    matrix_sums = lax.psum(for_sending((deltas[1], deltas[2])), "grp")
+    embed_sum, vector_sum = sum_over_groups(
+        deltas[0].astype(jnp.bfloat16), jnp.pad(deltas[3], ((0, 2), (0, 0)))
+    )
+    sums = (embed_sum, matrix_sums[0], matrix_sums[1], vector_sum[: vectors.shape[0]])
+    results = [jnp.stack(loss_list)[None], jnp.stack(norm_list)[None]]
+    for k in range(4):
+        delta_mean = sums[k].astype(jnp.float32) / lax.axis_size("grp")
+        outer_new = OUTER_MOMENTUM * outers[k] + delta_mean
+        master_new = masters[k] - OUTER_RATE * (delta_mean + OUTER_MOMENTUM * outer_new)
+        if k == 3:
+            results.append(vector_gradient[None])
+        results += [states[k][1][None], states[k][2][None], master_new, outer_new]
+        if k < 3:
+            results.append(master_new.astype(jnp.bfloat16))
+    return tuple(results)
+
+
+def padded(embed_low):
+    extra = -embed_low.shape[0] % 16
+    return jnp.pad(embed_low, ((0, extra), (0, 0))) if extra else embed_low
+
+
 def shards(
     tokens,
     routes,
@@ -932,7 +1345,13 @@
     steps, fits = prepare(
         n, slots, vocab_shard, tokens[:, 0], routes[:, 0, :, 0], segments[:, 0], loss_pos[:, 0]
     )
-    attn_start = lax.all_gather(attention.astype(jnp.bfloat16), "fsdp", axis=1, tiled=True)
+    lows = (
+        padded(embedding.astype(jnp.bfloat16)),
+        lax.all_gather(attention.astype(jnp.bfloat16), "fsdp", axis=1, tiled=True),
+        experts.astype(jnp.bfloat16),
+    )
+    sizes = (tokens.shape[2], loss_pos.shape[2])
+    x_start = fetch(n, slots, sizes, steps[0], lows[0])
     state = (
         embedding,
         embedding_first,
@@ -953,19 +1372,13 @@
     )
 
     def quick(*state):
-        def step(inner_step, weights):
-            embed_w, attn_w, expert_w, vector_w = weights
-            if inner_step == 0:
-                attn_low = attn_start
-            else:
-                attn_low = lax.all_gather(attn_w.astype(jnp.bfloat16), "fsdp", axis=1, tiled=True)
-            dembed, dattn, dexpert, dvector_all, loss = run_step(
-                n, slots, vocab_shard, 1, steps[inner_step], vector_w,
-                embed_w.astype(jnp.bfloat16), attn_low, expert_w.astype(jnp.bfloat16),
-            )
-            return dembed, dattn, dexpert, dvector_all[:6], dvector_all[6, 0], loss[0, 0]
-
-        return window(step, *state, inner_count, row_total)
+        masters, firsts, seconds, outers = (
+            [state[4 * k + part] for k in range(4)] for part in range(4)
+        )
+        firsts, seconds = [value[0] for value in firsts], [value[0] for value in seconds]
+        return quick_window(
+            n, slots, sizes, steps, x_start, lows, masters, firsts, seconds, outers, row_total
+        )
 
     def general(*state):
         all_ids = lax.all_gather(tokens[:, 0, :], "fsdp", axis=1, tiled=True)

time: 804 us -> 671 us (0.83)
  waiting for transfers between devices: 191 us -> 18.6 us
  Pallas kernels: 327 us -> 447 us
  blocking collectives: 61.6 us -> 0 us
  local copies, waits for them, and re-layouts: 32.1 us -> 15.3 us
    pallas_call x0 -> x4, Pallas kernels: none -> 210 us  [the longest x1 134 us: sum_over_groups(): pl.pallas_call(functools.partial(sum_kernel, (rows, quarter, pieces)), ou...]
    psum x1, waiting for transfers between devices: 168 us -> 0.01 us  [quick_window(): matrix_sums = lax.psum(for_sending((deltas[1], deltas[2])), 'grp')]
    pallas_call x2, Pallas kernels: 327 us -> 238 us  [run_step(): pl.pallas_call(functools.partial(step_kernel, (n, slots, vocab, vocab_row...]
    all_gather x1 -> x0, blocking collectives: 45.2 us -> none  [prepare(): world = lax.all_gather(packed, ('grp', 'fsdp'))]
    convert_element_type x1, other arithmetic: 31.9 us -> 6.45 us  [short(): return part.astype(jnp.bfloat16) if part.dtype == jnp.float32 else part]
    convert_element_type x5 -> x6, other arithmetic: 59.2 us -> 84.1 us  [the longest x1 38.3 us: quick_window(): deltas[0].astype(jnp.bfloat16)]
    psum x1 -> x0, blocking collectives: 16.4 us -> none  [window(): lax.psum(for_sending(deltas), 'grp')]
    another operation x85 -> x34, local copies, waits for them, and re-layouts: 14.1 us -> 3.68 us  [the longest x2 2.26 us: prepare(): want[:, None]]
  transfers between devices with their start and end apart: 3 -> 3, of which waited for: 3 -> 2; matrix products, arithmetic and copies ran while one was open for 8% -> 18% of each run, Pallas kernels for 0% -> 32%
where the time goes in v3:
time: 671 us; the launch traced here: 662 us
  Pallas kernels  447 us (67%)
  other arithmetic  154 us (23%)
  waiting for transfers between devices  18.6 us (3%)
  local copies, waits for them, and re-layouts  15.3 us (2%)
  between operations  14.9 us (2%)
  loops' own time  11.7 us (2%)
    pallas_call x2, Pallas kernels, run_step(): pl.pallas_call(functools.partial(step_kernel, (n, slots, vocab, vocab_row...  238 us
    pallas_call x1, Pallas kernels, sum_over_groups(): pl.pallas_call(functools.partial(sum_kernel, (rows, quarter, pieces)), ou...  134 us
    pallas_call x2, Pallas kernels, fetch(): pl.pallas_call(functools.partial(fetch_kernel, (n, slots, vocab_rows) + s...  60.4 us
    convert_element_type x1, other arithmetic, quick_window(): deltas[0].astype(jnp.bfloat16)  38.3 us
    convert_element_type x1, other arithmetic, window(): new_master[0].astype(jnp.bfloat16)  20.5 us
    convert_element_type x1, other arithmetic, quick_window(): embed_low = padded(replay(0, again)[0].astype(jnp.bfloat16))  20.2 us
    broadcast_in_dim x2, other arithmetic, quick_window(): results += [states[k][1][None], states[k][2][None], master_new, outer_new]  16 us
    pallas_call x1, Pallas kernels, share(): pl.pallas_call(functools.partial(share_kernel, n, groups), out_shape=(jax...  14.7 us
  transfers between devices with their start and end apart: 3, of which 2 were waited for; matrix products, arithmetic and copies ran while one was open for 18% of the time, Pallas kernels for 32%

profile of v3, /device:TPU:0, one launch (start us, length us, event | category | flops | bytes accessed | tf_op | source)
XLA Modules:
  0.0 661.6 jit_solution(1127331201438319582)
XLA Ops:
  7.2 2.3 convert_element_type.343
  9.6 0.7 copy.419
  10.3 0.7 copy.418
  11.0 0.7 pad.29
  11.7 0.7 broadcast_add_fusion.3
  12.3 0.7 copy_bitcast_fusion.2
  13.0 1.0 select_reduce_fusion.10
  14.4 0.7 and_select_fusion.3
  15.6 0.6 select_reduce_fusion.14
  16.3 0.3 select_reduce_fusion.8
  16.6 0.6 broadcast_in_dim.427
  17.2 0.7 concatenate.39.packed
  17.9 14.7 %share_ids.1 = (s32[8,2,640]{2,1,0:T(2,128)}, s32[8,128]{1,0:T(8,128)}) custom-call(s32[2,640]{1,0:T(2,128)} %concatenate.39.packed), custom_call_target="tpu_custom_call" | custom-call | tf_op jit(solution)/shard_map/share_ids/pallas_call | solution.py:341
  32.6 1.3 slice.203
  34.5 0.8 subtract_bitcast_fusion.1
  35.4 0.7 slice_bitcast_fusion.57
  36.2 0.8 subtract_bitcast_fusion
  37.1 4.0 convert_element_type.344
  41.1 7.9 %convert_element_type.342.eb = bf16[4016,768]{1,0:T(8,128)(2,1)} convert(f32[4016,768]{1,0:T(8,128)} %param.30) | non-fusion elementwise | flops 3084288 | bytes 18505728 | tf_op jit(solution)/shard_map/convert_element_type | solution.py:1349
  49.2 31.1 %fetch_rows.3 = bf16[256,768]{1,0:T(8,128)(2,1)} custom-call(s32[8,384]{1,0:T(8,128)S(1)} %slice_bitcast_fusion.56.ints, bf16[4016,768]{1,0:T(8,128)(2,1)} %convert_element_type.342.eb), custom_call_target="tpu_custom_call" | custom-call | tf_op jit(solution)/shard_map/fetch_rows/pallas_call | solution.py:398
  80.3 7.5 %all-gather.24.cloned.1.call-done = bf16[5,768,768]{2,1,0:T(8,128)(2,1)} async-done(((bf16[5,96,768]{2,1,0:T(8,128)(2,1)}), bf16[5,768,768]{2,1,0:T(8,128)(2,1)}) %all-gather.24.cloned.1.call-update) | async-done | bytes 5898256 | tf_op jit(solution)/shard_map/all_gather | solution.py:1350
  87.9 566.3 %conditional.3 = (f32[1,2]{1,0:T(1,128)S(1)}, f32[1,2]{1,0:T(1,128)S(1)}, f32[1,4016,768]{2,1,0:T(8,128)}, f32[1,4016,768]{2,1,0:T(8,128)}, f32[4016,768]{1,0:T(...) conditional(s32[]{:T(128)} %bitcast.159, ((), ...), branch_computations={%region_9.97_spmd, %region_96.102_spmd} | conditional | flops 16723800064 | bytes 1105357056
  96.5 0.6 slice_bitcast_fusion.1
  97.1 118.8 %inner_step.2 = (f32[4016,768]{1,0:T(8,128)}, f32[5,96,768]{2,1,0:T(8,128)}, f32[2,2,768,384]{3,2,1,0:T(8,128)}, f32[8,768]{1,0:T(8,128)}, f32[8,128]{1,0:T(8,128)}) custom-call(s32[8,384]{1,0:T(8,128)} %get-tuple-element.922.ints, f32[6,768]{1,0:T(8,128)S(1)} %get-tuple-element.166.vec, bf16[256,768]{1,0:T(8,128)(2,1)} %get-tuple-element.167.x_low, ...), custom_call_target="tpu_custom_call" | custom-call | tf_op jit(solution)/shard_map/cond/branch_1_fun/inner_step/pallas_call | solution.py:769
  215.9 1.2 slice.194
  217.1 1.3 multiply_reduce_fusion.1
  219.8 3.9 subtract_convert_fusion.5
  223.8 1.2 slice.191
  225.0 20.2 %subtract_convert_fusion.1.eb.eb_in = bf16[4016,768]{1,0:T(8,128)(2,1)S(1)} fusion(f32[4016,768]{1,0:T(8,128)} %get-tuple-element.175, f32[4016,768]{1,0:T(8,128)} %get-tuple-element.177, f32[1,4016,768]{2,1,0:T(8,128)} %get-tuple-element.178, f32[1,4016,768]{2,1,0:T(8,128)} %get-tuple-element.176, f32[]{:T(128)S(6)} %min.26), kind=kLoop, calls=%fused_computation.35 | loop fusion | flops 52432896 | bytes 55517188 | tf_op jit(solution)/shard_map/cond/branch_1_fun/convert_element_type | solution.py:1274
  245.3 29.4 %fetch_rows.2.x_low = bf16[256,768]{1,0:T(8,128)(2,1)S(1)} custom-call(s32[8,384]{1,0:T(8,128)S(1)} %get-tuple-element.923.ints, bf16[4016,768]{1,0:T(8,128)(2,1)S(1)} %subtract_convert_fusion.1.eb.eb_in), custom_call_target="tpu_custom_call" | custom-call | tf_op jit(solution)/shard_map/cond/branch_1_fun/fetch_rows/pallas_call | solution.py:398
  274.6 2.7 copy-done
  277.3 0.7 copy-done.1
  278.0 0.7 multiply_subtract_fusion.4.vec
  278.7 9.6 %subtract_convert_fusion.3.expw_in = bf16[2,2,768,384]{3,2,1,0:T(8,128)(2,1)} fusion(f32[2,2,768,384]{3,2,1,0:T(8,128)} %get-tuple-element.183, f32[2,2,768,384]{3,2,1,0:T(8,128)} %get-tuple-element.185, f32[1,2,2,768,384]{4,3,2,1,0:T(8,128)} %get-tuple-element.186, f32[1,2,2,768,384]{4,3,2,1,0:T(8,128)} %get-tuple-element.184, f32[]{:T(128)S(6)} %min.26), kind=kLoop, calls=%fused_computation.57 | loop fusion | flops 20054016 | bytes 21233668 | tf_op jit(solution)/shard_map/cond/branch_1_fun/convert_element_type | solution.py:1273
  288.3 11.0 %all-gather.22.cloned.1.call-done.attn_in = bf16[5,768,768]{2,1,0:T(8,128)(2,1)} async-done(((bf16[5,96,768]{2,1,0:T(8,128)(2,1)}), bf16[5,768,768]{2,1,0:T(8,128)(2,1)}) %all-gather.22.cloned.1.call-update) | async-done | bytes 5898256 | tf_op jit(solution)/shard_map/cond/branch_1_fun/all_gather | solution.py:1270
  299.3 119.1 %inner_step.3 = (f32[4016,768]{1,0:T(8,128)}, f32[5,96,768]{2,1,0:T(8,128)}, f32[2,2,768,384]{3,2,1,0:T(8,128)}, f32[8,768]{1,0:T(8,128)}, f32[8,128]{1,0:T(8,128)}) custom-call(s32[8,384]{1,0:T(8,128)} %copy-done.2, f32[6,768]{1,0:T(8,128)} %multiply_subtract_fusion.4.vec, bf16[256,768]{1,0:T(8,128)(2,1)} %copy-done.1, bf16[4016,768]{1,0:T(8,128)(2,1)} %copy-done, ...), custom_call_target="tpu_custom_call" | custom-call | tf_op jit(solution)/shard_map/cond/branch_1_fun/inner_step/pallas_call | solution.py:769
  418.4 1.4 multiply_reduce_fusion
  419.8 1.2 slice.196
  422.4 6.5 subtract_convert_fusion.4
  428.8 16.0 %fusion.21 = (f32[1,2,2,768,384]{4,3,2,1,0:T(8,128)}, bf16[2,2,768,384]{3,2,1,0:T(8,128)(2,1)}, f32[1,2,2,768,384]{4,3,2,1,0:T(8,128)}) fusion(f32[2,2,768,384]{3,2,1,0:T(8,128)S(1)} %copy-done.18, f32[]{:T(128)S(6)} %min.27, f32[2,2,768,384]{3,2,1,0:T(8,128)} %get-tuple-element.185, f32[]{:T(128)S(6)} %min.26, ...), kind=kLoop, calls=%fused_computation.59 | loop fusion | flops 40108032 | bytes 35389448 | tf_op jit(solution)/shard_map/cond/branch_1_fun/broadcast_in_dim | solution.py:1307
  444.8 38.3 %subtract_convert_fusion = (bf16[4016,768]{1,0:T(8,128)(2,1)}, f32[1,4016,768]{2,1,0:T(8,128)}, f32[1,4016,768]{2,1,0:T(8,128)}) fusion(f32[4016,768]{1,0:T(8,128)} %get-tuple-element.175, f32[4016,768]{1,0:T(8,128)} %get-tuple-element.190, f32[]{:T(128)S(6)} %min.27, f32[4016,768]{1,0:T(8,128)} %get-tuple-element.177, f32[]{:T(128)S(6)} %min.26, ...), kind=kLoop, calls=%fused_computation.33 | loop fusion | flops 104865792 | bytes 92528648 | tf_op jit(solution)/shard_map/cond/branch_1_fun/convert_element_type | solution.py:1297
  483.2 1.2 slice.195
  484.5 134.4 %sum_groups.1 = (bf16[4016,768]{1,0:T(8,128)(2,1)S(1)}, f32[8,768]{1,0:T(8,128)S(1)}) custom-call(bf16[4016,768]{1,0:T(8,128)(2,1)} %get-tuple-element.909.value, f32[8,768]{1,0:T(8,128)S(1)} %pad.20.vector), custom_call_target="tpu_custom_call" | custom-call | bytes 300000000 | tf_op jit(solution)/shard_map/cond/branch_1_fun/sum_groups/pallas_call | solution.py:933
  619.0 1.4 maximum_bitcast_fusion
  620.4 20.5 %fusion.289 = (bf16[4016,768]{1,0:T(8,128)(2,1)}, f32[4016,768]{1,0:T(8,128)}, f32[4016,768]{1,0:T(8,128)}) fusion(f32[4016,768]{1,0:T(8,128)} %get-tuple-element.175, bf16[4016,768]{1,0:T(8,128)(2,1)S(1)} %get-tuple-element.192, f32[4016,768]{1,0:T(8,128)} %get-tuple-element.193), kind=kLoop, calls=%fused_computation.659 | loop fusion | flops 27758592 | bytes 61685760 | tf_op jit(solution)/shard_map/cond/branch_0_fun/convert_element_type | solution.py:1216
  640.9 3.5 fusion.288
  644.4 9.6 %fusion.287 = (bf16[2,2,768,384]{3,2,1,0:T(8,128)(2,1)}, f32[2,2,768,384]{3,2,1,0:T(8,128)}, f32[2,2,768,384]{3,2,1,0:T(8,128)}) fusion(f32[2,2,768,384]{3,2,1,0:T(8,128)} %get-tuple-element.183, bf16[2,2,768,384]{3,2,1,0:T(8,128)(2,1)S(1)} %copy-done.21, f32[2,2,768,384]{3,2,1,0:T(8,128)} %get-tuple-element.197), kind=kLoop, calls=%fused_computation.657 | loop fusion | flops 10616832 | bytes 23592960 | tf_op jit(solution)/shard_map/cond/branch_0_fun/convert_element_type | solution.py:1226
  654.3 0.5 copy-done.84
  (92 shorter events, 1.7 us)
Async XLA Ops:
  7.2 80.6 %all-gather.24.cloned.1.call-start = ((), (), s32[]{:S(2)}) async-start(), calls=%async_computation.27 | async-start | bytes 6635520 | tf_op jit(solution)/shard_map/all_gather | solution.py:1350
  49.1 38.7 %copy-start.3 = (f32[5,96,768]{2,1,0:T(8,128)S(1)}, f32[5,96,768]{2,1,0:T(8,128)}, u32[]{:S(2)}) copy-start(f32[5,96,768]{2,1,0:T(8,128)} %param.34) | copy-start | bytes 4423684
  49.1 38.7 %copy-start.10 = (f32[1,5,96,768]{3,2,1,0:T(8,128)S(1)}, f32[1,5,96,768]{3,2,1,0:T(8,128)}, u32[]{:S(2)}) copy-start(f32[1,5,96,768]{3,2,1,0:T(8,128)} %param.35) | copy-start | bytes 4423684
  49.1 38.7 %copy-start.22 = (f32[6,768]{1,0:T(8,128)S(1)}, f32[6,768]{1,0:T(8,128)}, u32[]{:S(2)}) copy-start(f32[6,768]{1,0:T(8,128)} %param.42) | copy-start | bytes 55300
  49.1 38.7 %copy-start.48 = (f32[1,6,768]{2,0,1:T(1,128)S(1)}, f32[1,6,768]{2,0,1:T(1,128)}, u32[]{:S(2)}) copy-start(f32[1,6,768]{2,0,1:T(1,128)} %param.43) | copy-start | bytes 55300
  49.1 38.7 %copy-start.80 = (s32[2,1,256]{2,1,0:T(1,128)S(1)}, s32[2,1,256]{2,1,0:T(1,128)}, u32[]{:S(2)}) copy-start(s32[2,1,256]{2,1,0:T(1,128)} %param.26) | copy-start | bytes 6148
  49.1 38.7 %copy-start.83 = (s32[2,1,16]{2,1,0:T(1,128)S(1)}, s32[2,1,16]{2,1,0:T(1,128)}, u32[]{:S(2)}) copy-start(s32[2,1,16]{2,1,0:T(1,128)} %param.29) | copy-start | bytes 388
  49.1 38.7 %copy-start.128 = (s32[2,1,256]{2,1,0:T(1,128)S(1)}, s32[2,1,256]{2,1,0:T(1,128)}, u32[]{:S(2)}) copy-start(s32[2,1,256]{2,1,0:T(1,128)} %param.28) | copy-start | bytes 6148
  49.1 38.7 %copy-start.129 = (s32[2,1,256,1]{2,3,1,0:T(1,128)S(1)}, s32[2,1,256,1]{2,3,1,0:T(1,128)}, u32[]{:S(2)}) copy-start(s32[2,1,256,1]{2,3,1,0:T(1,128)} %param.27) | copy-start | bytes 6148
  96.4 202.9 %all-gather.22.cloned.1.call-start = ((), (), s32[]{:S(2)}) async-start(), calls=%async_computation.25 | async-start | bytes 6635520 | tf_op jit(solution)/shard_map/cond/branch_1_fun/all_gather | solution.py:1270
  97.1 148.2 %copy-start.2 = (s32[8,384]{1,0:T(8,128)}, s32[8,384]{1,0:T(8,128)S(1)}, u32[]{:S(2)}) copy-start(s32[8,384]{1,0:T(8,128)S(1)} %get-tuple-element.923.ints) | copy-start | bytes 36868 | tf_op jit(solution)/shard_map/conditional.1
  223.7 417.2 %all-reduce.20.cloned.1.call-start = ((), (), s32[]{:S(2)}) async-start(), calls=%async_computation.26 | async-start | bytes 6193152 | tf_op jit(solution)/shard_map/cond/branch_1_fun/psum | solution.py:1295
  245.2 32.8 %copy-start.50 = (f32[1,6,768]{2,0,1:T(1,128)S(1)}, f32[1,6,768]{2,0,1:T(1,128)}, u32[]{:S(2)}) copy-start(f32[1,6,768]{2,0,1:T(1,128)} %get-tuple-element.781) | copy-start | bytes 55300 | tf_op jit(solution)/shard_map/conditional.1
  245.2 32.8 %copy-start.55 = (f32[8,768]{1,0:T(8,128)S(1)}, f32[8,768]{1,0:T(8,128)}, u32[]{:S(2)}) copy-start(f32[8,768]{1,0:T(8,128)} %get-tuple-element.173) | copy-start | bytes 73732 | tf_op jit(solution)/shard_map/conditional.1
  274.6 2.7 copy-start
  277.3 0.7 copy-start.1
  422.3 6.5 copy-start.18
  444.8 39.6 %copy-start.58 = (f32[6,768]{1,0:T(8,128)S(1)}, f32[6,768]{1,0:T(8,128)}, u32[]{:S(2)}) copy-start(f32[6,768]{1,0:T(8,128)} %multiply_subtract_fusion.4.vec) | copy-start | bytes 55300 | tf_op jit(solution)/shard_map/conditional.1
  444.8 39.6 %copy-start.68 = (f32[8,768]{1,0:T(8,128)S(1)}, f32[8,768]{1,0:T(8,128)}, u32[]{:S(2)}) copy-start(f32[8,768]{1,0:T(8,128)} %get-tuple-element.188) | copy-start | bytes 73732 | tf_op jit(solution)/shard_map/conditional.1
  483.2 137.2 %copy-start.70 = (f32[6,768]{1,0:T(8,128)S(1)}, f32[6,768]{1,0:T(8,128)}, u32[]{:S(2)}) copy-start(f32[6,768]{1,0:T(8,128)} %get-tuple-element.199) | copy-start | bytes 55300 | tf_op jit(solution)/shard_map/conditional.1
  620.4 20.5 %copy-start.16 = (f32[5,96,768]{2,1,0:T(8,128)S(1)}, f32[5,96,768]{2,1,0:T(8,128)}, u32[]{:S(2)}) copy-start(f32[5,96,768]{2,1,0:T(8,128)} %get-tuple-element.195) | copy-start | bytes 4423684 | tf_op jit(solution)/shard_map/conditional.1
  640.9 3.5 copy-start.21
  654.2 0.6 copy-start.84
  654.2 0.6 copy-start.85
  654.2 0.6 copy-start.86
  654.2 0.6 copy-start.87
  654.3 0.6 copy-start.88
  654.3 0.6 copy-start.157
  654.3 0.6 copy-start.158
Sparse Core Ops, SparseCore 0:
  10.3 77.4 all-gather.23
  223.8 75.4 all-gather.21
  444.9 115.6 all-reduce.19

commit v4 on v3

--- a/solution.py
+++ b/solution.py
@@ -131,8 +131,8 @@
 MESH = pl.DeviceIdType.MESH
 F32 = jnp.float32
 LOW = jnp.bfloat16
-X_IN, B_ROWS, Y_PART, HEAD_ROWS, TOPS, D_ROWS, DY_ROWS, DB_PART = range(8)
-ROWS_ONE, P_A, ROWS_TWO, DS_A, G_OUT, D_VEC, EXCHANGES = range(8, 15)
+B_ROWS, Y_PART, HEAD_ROWS, TOPS, D_ROWS, DY_ROWS, DB_PART = range(7)
+Q_ROWS, P_A, MIDDLE_ROWS, BRANCH_ROWS, DQ_ROWS, DS_A, G_OUT, D_VEC, SQUARES, EXCHANGES = range(7, 17)
 
 
 def dot_nn(left, right):
@@ -417,9 +417,9 @@
 def step_kernel(
     dims,
     ints, vec, x_low, eb_in, attn_in, expw_in,
-    dembed_out, dattn_out, dexp_out, dvec_out, loss_out,
+    dembed_out, dattn_out, dexp_out, dvec_out, loss_out, norm_out, factor_out,
     eb, attn, expw, xs, gr, ball, ys, yr, rows, tops, drs, drr, dyall, dbs, dbr,
-    one, pas, par, two, dss, dsr, dvec, logit_s, dlog_s, pre_s, hid_s, dpre_s, flip_s, tile_s,
+    q_all, pas, par, middle_all, branch_all, dq_all, dss, dsr, dvec, sums, logit_s, dlog_s, pre_s, hid_s, dpre_s, flip_s, tile_s, part_s, hit_s,
     send, recv, out_sem, load_sem,
 ):
     n, slots, vocab, vocab_rows, hidden, tokens, row_count = dims
@@ -506,7 +506,7 @@
     router_probs = [value / router_sum for value in router_exp]
     chosen = [(route_col == e).astype(F32) for e in range(EXPERTS)]
     gate = sum([p * c for p, c in zip(router_probs[1:], chosen[1:])], router_probs[0] * chosen[0])
-    one[me] = q
+    q_all[me] = q
     a_turned = a.astype(F32).T.astype(LOW)
     eye = (sublanes((row_count, row_count)) == lanes((row_count, row_count))).astype(F32).astype(LOW)
     flipped = lambda low_rows: dot_tn(low_rows, eye)
@@ -569,7 +569,7 @@
     )
     spread(TOPS, tops)
     arrive(TOPS, tops)
-    relay(ROWS_ONE, one)
+    relay(Q_ROWS, q_all)
     top = tops[0, 0:1]
     for j in range(1, n):
         top = jnp.maximum(top, tops[j, 0:1])
@@ -581,7 +581,7 @@
     is_first = lax.rem(lanes((1, loss_rows)), 2 * row_count) < row_count
     weight = jnp.where(is_first, 1.0, SECOND_WEIGHT) / row_total
     loss = jnp.sum(weight * (logsum - at_target), axis=-1, keepdims=True)
-    loss_out[...] = jnp.broadcast_to(loss, loss_out.shape)
+    loss_out[...] = loss
 
     def dlogits_tile(i, start, size, acc):
         soft = jnp.exp(logit_s[pl.ds(start, size), :] - logsum)
@@ -604,6 +604,8 @@
     dyall[me] = (gate * dz).astype(LOW)
     spread(DY_ROWS, dyall)
     arrive(DY_ROWS, dyall)
+    middle_all[me] = dmiddle_low
+    relay(MIDDLE_ROWS, middle_all)
     dy_all = dyall[...].reshape(all_rows, D)
     db_part = jnp.zeros((all_rows, D), F32)
     for e in range(EXPERTS):
@@ -624,8 +626,8 @@
     for e in range(EXPERTS):
         up = dot_tn(b_all, dpre_s[e])
         down = dot_tn(dy_all, hid_s[e])
-        dexp_out[e, 0] = up
-        dexp_out[e, 1] = down
+        dexp_out[e, 0] = up.astype(LOW)
+        dexp_out[e, 1] = down.astype(LOW)
         hidden_squares = hidden_squares + squared(up) + squared(down)
     arrive(DB_PART, dbr)
     prob_grads = [c * dgate for c in chosen]
@@ -639,15 +641,15 @@
     dx_attn = dz + dx_part
 
     dbranch = dx_attn.astype(LOW)
+    branch_all[me] = dbranch
+    relay(BRANCH_ROWS, branch_all)
     do = (ATTN_GAIN * dot_nt(dbranch, attn[3])).astype(LOW)
     do_wide = widen(do)
     dprobs = dot_nt(do_wide, v)
     dscores = (probs * (dprobs - jnp.sum(probs * dprobs, axis=-1, keepdims=True))).astype(LOW)
     dq = (narrow(dot_nn(dscores, k)) * factor_qk).astype(LOW)
-    two[me, 0] = do
-    two[me, 1] = dq
-    two[me, 2] = dbranch
-    two[me, 3] = dmiddle_low
+    dq_all[me] = dq
+    relay(DQ_ROWS, dq_all)
     dk = (dot_tn(dscores, q_wide) * factor_qk).astype(LOW)
     dv = dot_tn(probs_low, do_wide).astype(LOW)
     dinput = dot_nt(dk, attn[1]) + dot_nt(dv, attn[2])
@@ -664,15 +666,16 @@
         xs[c * group : (c + 1) * group] = dot_nn(hit, dx_low).astype(LOW).reshape(group, slots, D)
     deal(G_OUT, xs, gr)
     gr[me] = xs[me]
-    relay(ROWS_TWO, two)
+    line = sublanes((8, D))
+    shares = jnp.zeros((8, D), F32)
+    for i, value in enumerate([gain_attn + gain_more, gain_ffn, gain_final, gain_mtp] + drouter):
+        shares = jnp.where(line == i, value, shares)
+    dvec[me] = shares
+    relay(D_VEC, dvec)
     dss[...] = dot_nt(a_turned, dscores).reshape(n, shard, wide).astype(LOW)
     deal(DS_A, dss, dsr)
     dsr[me] = dss[me]
 
-    relayed(ROWS_ONE, one)
-    arrive(P_A, par)
-    relayed(ROWS_TWO, two)
-    arrive(DS_A, dsr)
     mine = pl.ds(pl.multiple_of(me * shard, 8), shard)
 
     def own_slices(start, right):
@@ -685,22 +688,29 @@
         flip_s[...] = left.astype(F32).reshape(all_rows, D).T
         return dot_nn(flip_s[mine, :].astype(LOW), right.reshape(all_rows, D))
 
-    dkey = jnp.zeros((shard, D), F32)
+    def keep(i, part):
+        dattn_out[i] = part.astype(LOW)
+        return squared(part)
+
+    arrive(P_A, par)
+    relayed(MIDDLE_ROWS, middle_all)
+    squares = squares + keep(4, own_rows(rows[:, 0], middle_all[...]))
+    relayed(BRANCH_ROWS, branch_all)
+    squares = squares + keep(3, ATTN_GAIN * own_slices(wide + row_count, branch_all))
+    do_all = ATTN_GAIN * dot_nt(branch_all[...].reshape(all_rows, D), attn[3])
     dvalue = jnp.zeros((shard, D), F32)
     for j in range(n):
-        dkey = dkey + dot_nn(dsr[j], widen(one[j]))
-        dvalue = dvalue + dot_nn(par[j, :, 0:wide], widen(two[j, 0]))
-    parts = (
-        own_slices(wide, two[:, 1]),
-        dkey * factor_qk,
-        dvalue,
-        ATTN_GAIN * own_slices(wide + row_count, two[:, 2]),
-        own_rows(rows[:, 0], two[:, 3]),
-    )
-    for i, part in enumerate(parts):
-        dattn_out[i] = part
-        squares = squares + squared(part)
-
+        do_one = do_all[j * row_count : (j + 1) * row_count].astype(LOW)
+        dvalue = dvalue + dot_nn(par[j, :, 0:wide], widen(do_one))
+    squares = squares + keep(2, dvalue)
+
+    def ready_tile(i, start, size, carry):
+        part_s[pl.ds(start, size), :] = scale * dot_nn(dlog_s[pl.ds(start, size), :], head_rows)
+        hit = (sublanes((size, n * slots)) + start == id_lane).astype(F32)
+        hit_s[pl.ds(start, size), :] = hit.astype(LOW)
+        return carry
+
+    tiled(ready_tile, 0)
     arrive(G_OUT, gr)
     whole = vocab_rows // TILE
 
@@ -711,11 +721,9 @@
         )
 
     def dembed_tile(i, start, size, acc):
-        value = scale * dot_nn(dlog_s[pl.ds(start, size), :], head_rows)
-        for c in range(n // group):
-            ids = id_lane[:, c * chunk : (c + 1) * chunk]
-            hit = (sublanes((size, chunk)) + start == ids).astype(F32).astype(LOW)
-            value = value + dot_nn(hit, gr[c * group : (c + 1) * group].reshape(chunk, D))
+        value = part_s[pl.ds(start, size), :] + dot_nn(
+            hit_s[pl.ds(start, size), :], gr[...].reshape(n * slots, D)
+        )
 
         def free():
             leave(i - 2, start - 2 * TILE, TILE).wait()
@@ -725,33 +733,47 @@
                 free()
         else:
             pl.when(i >= 2)(free)
-        tile_s[lax.rem(i, 2), pl.ds(0, size)] = value
+        tile_s[lax.rem(i, 2), pl.ds(0, size)] = value.astype(LOW)
         leave(i, start, size).start()
         return acc + squared(value)
 
     squares = tiled(dembed_tile, squares)
+    relayed(Q_ROWS, q_all)
+    relayed(DQ_ROWS, dq_all)
+    squares = squares + keep(0, own_slices(wide, dq_all))
+    arrive(DS_A, dsr)
+    dkey = jnp.zeros((shard, D), F32)
+    for j in range(n):
+        dkey = dkey + dot_nn(dsr[j], widen(q_all[j]))
+    squares = squares + keep(1, dkey * factor_qk)
     tiles = [(i, i * TILE, TILE) for i in range(whole)]
     if vocab_rows % TILE:
         tiles.append((whole, whole * TILE, vocab_rows % TILE))
     total_squares = jnp.sum(squares, axis=-1, keepdims=True) + jnp.sum(
         hidden_squares, axis=-1, keepdims=True
     )
-    line = sublanes((8, D))
-    share = jnp.broadcast_to(total_squares, (8, D))
-    for i, value in enumerate([gain_attn + gain_more, gain_ffn, gain_final, gain_mtp] + drouter):
-        share = jnp.where(line == i, value, share)
-    dvec[me] = share
-    spread(D_VEC, dvec)
-    arrive(D_VEC, dvec)
-    dvec_out[...] = added(dvec)
+    sums[me] = jnp.broadcast_to(total_squares, (8, 128))
+    spread(SQUARES, sums)
+    relayed(D_VEC, dvec)
+    arrive(SQUARES, sums)
+    shared = added(dvec)
+    dvector = shared[0 : 4 + EXPERTS]
+    dvec_out[...] = dvector
+    own = jnp.sum(squared(dvector), axis=-1, keepdims=True)
+    norm = jnp.sqrt(added(sums)[0:1, 0:1] + own)
+    norm_out[...] = norm
+    factor_out[...] = jnp.minimum(1.0, 0.05 / math.sqrt(row_total) / norm)
     for i, start, size in tiles[-2:]:
         leave(i, start, size).wait()
     for which, source in (
         (B_ROWS, ball), (Y_PART, ys), (TOPS, tops), (D_ROWS, drs), (DY_ROWS, dyall),
-        (DB_PART, dbs), (P_A, pas), (DS_A, dss), (G_OUT, xs), (D_VEC, dvec),
+        (DB_PART, dbs), (P_A, pas), (DS_A, dss), (G_OUT, xs), (SQUARES, sums),
     ):
         sent(which, source)
-    for which, source in ((HEAD_ROWS, rows), (ROWS_ONE, one), (ROWS_TWO, two)):
+    for which, source in (
+        (HEAD_ROWS, rows), (Q_ROWS, q_all), (MIDDLE_ROWS, middle_all),
+        (BRANCH_ROWS, branch_all), (DQ_ROWS, dq_all), (D_VEC, dvec),
+    ):
         links.relay_sent(which, source)
 
 
@@ -769,14 +791,16 @@
     outs = pl.pallas_call(
         functools.partial(step_kernel, (n, slots, vocab, vocab_rows, hidden) + sizes),
         out_shape=(
-            jax.ShapeDtypeStruct((vocab_rows, D), F32),
-            jax.ShapeDtypeStruct((5, shard, D), F32),
-            jax.ShapeDtypeStruct((EXPERTS, 2, D, hidden), F32),
-            jax.ShapeDtypeStruct((8, D), F32),
-            jax.ShapeDtypeStruct((8, 128), F32),
+            jax.ShapeDtypeStruct((vocab_rows, D), LOW),
+            jax.ShapeDtypeStruct((5, shard, D), LOW),
+            jax.ShapeDtypeStruct((EXPERTS, 2, D, hidden), LOW),
+            jax.ShapeDtypeStruct((4 + EXPERTS, D), F32),
+            jax.ShapeDtypeStruct((1, 1), F32),
+            jax.ShapeDtypeStruct((1, 1), F32),
+            jax.ShapeDtypeStruct((1, 1), F32),
         ),
         in_specs=[vmem] * 3 + [anywhere] * 3,
-        out_specs=(anywhere, vmem, vmem, vmem, vmem),
+        out_specs=(anywhere, vmem, vmem, vmem, vmem, vmem, vmem),
         scratch_shapes=[
             low(vocab_rows, D), low(5, D, D), low(EXPERTS, 2, D, hidden),
             low(n, slots, D), low(n, slots, D),
@@ -786,11 +810,13 @@
             low(n, row_count, D), low(n, row_count, D), low(n, row_count, D),
             low(n, row_count, D), low(n, shard, wide + 2 * row_count),
             low(n, shard, wide + 2 * row_count),
-            low(n, 4, row_count, D), low(n, shard, wide), low(n, shard, wide),
-            wide_float(n, 8, D),
+            low(n, row_count, D), low(n, row_count, D), low(n, row_count, D),
+            low(n, shard, wide), low(n, shard, wide),
+            wide_float(n, 8, D), wide_float(n, 8, 128),
             wide_float(vocab_rows, 2 * all_rows), low(vocab_rows, 2 * all_rows),
             wide_float(EXPERTS, all_rows, hidden), low(EXPERTS, all_rows, hidden),
-            low(EXPERTS, all_rows, hidden), wide_float(D, all_rows), wide_float(2, TILE, D),
+            low(EXPERTS, all_rows, hidden), wide_float(D, all_rows), low(2, TILE, D),
+            wide_float(vocab_rows, D), low(vocab_rows, n * slots),
             pltpu.SemaphoreType.DMA((EXCHANGES, n)),
             pltpu.SemaphoreType.DMA((EXCHANGES, n)),
             pltpu.SemaphoreType.DMA((2,)),
@@ -804,11 +830,15 @@
     return (outs[0][:vocab],) + outs[1:]
 
 
-def sum_kernel(dims, value, vector, total, vector_total, held, first_in, second_in, rest, flat, *sems):
-    rows, quarter, pieces = dims
+def sum_kernel(shapes, *refs):
+    count = len(shapes)
+    values, vector, refs = refs[:count], refs[count], refs[count + 1 :]
+    totals, vector_total, refs = refs[:count], refs[count], refs[count + 1 :]
+    helds, first_ins, second_ins, rests = (refs[i * count : (i + 1) * count] for i in range(4))
+    flat, *sems = refs[4 * count :]
     one_s, one_r, two_s, two_r, three_s, three_r, four_s, four_r, rest_s, rest_r = sems
     group = lax.axis_index("grp")
-    size, width = quarter // pieces, D // 2
+    width = D // 2
     bits = (lax.rem(group, 2), lax.div(group, 2))
     flip = lambda bit: group + (1 - 2 * bits[bit]) * (1 + bit)
     barrier = pltpu.get_barrier_semaphore()
@@ -817,8 +847,17 @@
             barrier, inc=1, device_id={"grp": lax.rem(group + k, 4)}, device_id_type=MESH
         )
     pl.semaphore_wait(barrier, 3)
-
-    def place(side, first_bit, second_bit, piece):
+    units = [
+        (array, side, piece, piece * 2 + side)
+        for array, (rows, quarter, pieces) in enumerate(shapes)
+        for piece in range(pieces)
+        for side in range(2)
+    ]
+
+    def place(u, first_bit, second_bit):
+        array, side, piece, slot = units[u]
+        rows, quarter, pieces = shapes[array]
+        size = quarter // pieces
         owner = first_bit + 2 * second_bit if side == 0 else second_bit + 2 * first_bit
         start = pl.multiple_of((owner * pieces + piece) * size, 16)
         return pl.ds(start, size), pl.ds(side * width, width)
@@ -829,127 +868,139 @@
             device_id={"grp": peer}, device_id_type=MESH,
         )
 
-    units = [(side, piece) for piece in range(pieces) for side in range(2)]
-
     def stage_one(u, turn):
-        side, piece = units[u]
+        array, side, piece, slot = units[u]
         here, there = bits[side], bits[1 - side]
-        second = there if turn else 1 - there
-        out = place(side, 1 - here, second, piece)
-        return copy(value.at[out], first_in.at[u, turn], one_s.at[u, turn], one_r.at[u, turn], flip(side))
+        out = place(u, 1 - here, there if turn else 1 - there)
+        return copy(
+            values[array].at[out], first_ins[array].at[slot, turn],
+            one_s.at[u, turn], one_r.at[u, turn], flip(side),
+        )
 
     def stage_two(u):
-        side, piece = units[u]
-        return copy(held.at[u, 0], second_in.at[u], two_s.at[u], two_r.at[u], flip(1 - side))
-
-    def stage_three(u):
-        side, piece = units[u]
-        own = place(side, bits[side], bits[1 - side], piece)
-        return copy(total.at[own], total.at[own], three_s.at[u], three_r.at[u], flip(1 - side))
-
-    def stage_four(u, turn):
-        side, piece = units[u]
+        array, side, piece, slot = units[u]
+        return copy(
+            helds[array].at[slot, 0], second_ins[array].at[slot], two_s.at[u], two_r.at[u], flip(1 - side)
+        )
+
+    def stage_three(u, other=False):
+        array, side, piece, slot = units[u]
         there = bits[1 - side]
-        own = place(side, bits[side], there if turn == 0 else 1 - there, piece)
-        return copy(total.at[own], total.at[own], four_s.at[u, turn], four_r.at[u, turn], flip(side))
-
-    main = 4 * quarter
-    spare = rows - main
+        block = totals[array].at[place(u, bits[side], 1 - there if other else there)]
+        return copy(block, block, three_s.at[u], three_r.at[u], flip(1 - side))
+
+    def stage_four(u, turn, other=False):
+        array, side, piece, slot = units[u]
+        here, there = bits[side], bits[1 - side]
+        block = totals[array].at[
+            place(u, 1 - here if other else here, there if turn == 0 else 1 - there)
+        ]
+        return copy(block, block, four_s.at[u, turn], four_r.at[u, turn], flip(side))
+
     flat[group] = vector[...]
-    if spare:
-        rest[group, 0:spare] = value[main:rows]
-
-    def small(which, k, peer, origin):
-        buffer = (rest, flat)[which]
+    smalls = [(count, flat)]
+    for array, (rows, quarter, pieces) in enumerate(shapes):
+        spare = rows - 4 * quarter
+        if spare:
+            rests[array][group, 0:spare] = values[array][4 * quarter : rows]
+            smalls.append((array, rests[array]))
+
+    def small(which, buffer, k, peer, origin):
         return copy(
             buffer.at[origin], buffer.at[origin], rest_s.at[which, k], rest_r.at[which, origin], peer
         )
 
-    for u in range(len(units)):
-        stage_one(u, 0).start()
-    for u in range(len(units)):
-        stage_one(u, 1).start()
-    smalls = (0, 1) if spare else (1,)
-    for which in smalls:
+    every = range(len(units))
+    for turn in range(2):
+        for u in every:
+            stage_one(u, turn).start()
+    for which, buffer in smalls:
         for k in range(1, 4):
-            small(which, k, lax.rem(group + k, 4), group).start()
-    for u, (side, piece) in enumerate(units):
-        stage_one(u, 0).wait_recv()
-        passed = place(side, bits[side], 1 - bits[1 - side], piece)
-        held[u, 0] = (value[passed].astype(F32) + first_in[u, 0].astype(F32)).astype(LOW)
-        stage_two(u).start()
-    for u, (side, piece) in enumerate(units):
-        stage_one(u, 1).wait_recv()
-        kept = place(side, bits[side], bits[1 - side], piece)
-        held[u, 1] = (value[kept].astype(F32) + first_in[u, 1].astype(F32)).astype(LOW)
-    for u, (side, piece) in enumerate(units):
+            small(which, buffer, k, lax.rem(group + k, 4), group).start()
+    for turn in range(2):
+        for u in every:
+            array, side, piece, slot = units[u]
+            there = bits[1 - side]
+            stage_one(u, turn).wait_recv()
+            mine = place(u, bits[side], there if turn else 1 - there)
+            helds[array][slot, turn] = (
+                values[array][mine].astype(F32) + first_ins[array][slot, turn].astype(F32)
+            ).astype(LOW)
+            if turn == 0:
+                stage_two(u).start()
+    for u in every:
+        array, side, piece, slot = units[u]
         stage_two(u).wait_recv()
-        kept = place(side, bits[side], bits[1 - side], piece)
-        total[kept] = (held[u, 1].astype(F32) + second_in[u].astype(F32)).astype(LOW)
+        mine = place(u, bits[side], bits[1 - side])
+        totals[array][mine] = (
+            helds[array][slot, 1].astype(F32) + second_ins[array][slot].astype(F32)
+        ).astype(LOW)
         stage_three(u).start()
         stage_four(u, 0).start()
-    for u, (side, piece) in enumerate(units):
-        come = place(side, bits[side], 1 - bits[1 - side], piece)
-        copy(total.at[come], total.at[come], three_s.at[u], three_r.at[u], flip(1 - side)).wait_recv()
+    for u in every:
+        stage_three(u, True).wait_recv()
         stage_four(u, 1).start()
-    for which in smalls:
+    for which, buffer in smalls:
         for k in range(1, 4):
             origin = lax.rem(group + k, 4)
-            small(which, k, origin, origin).wait_recv()
+            small(which, buffer, k, origin, origin).wait_recv()
     added = lambda buffer: (buffer[0].astype(F32) + buffer[1].astype(F32)) + (
         buffer[2].astype(F32) + buffer[3].astype(F32)
     )
     vector_total[...] = added(flat)
-    if spare:
-        total[main:rows] = added(rest)[0:spare].astype(LOW)
-    for u, (side, piece) in enumerate(units):
-        there = bits[1 - side]
+    for array, buffer in smalls[1:]:
+        rows, quarter, pieces = shapes[array]
+        totals[array][4 * quarter : rows] = added(buffer)[0 : rows - 4 * quarter].astype(LOW)
+    for u in every:
         for turn in range(2):
-            come = place(side, 1 - bits[side], there if turn == 0 else 1 - there, piece)
-            copy(
-                total.at[come], total.at[come], four_s.at[u, turn], four_r.at[u, turn], flip(side)
-            ).wait_recv()
-    for u in range(len(units)):
-        stage_one(u, 0).wait_send()
-        stage_one(u, 1).wait_send()
+            stage_four(u, turn, True).wait_recv()
+    for u in every:
         stage_two(u).wait_send()
         stage_three(u).wait_send()
-        stage_four(u, 0).wait_send()
-        stage_four(u, 1).wait_send()
-    for which in smalls:
+        for turn in range(2):
+            stage_one(u, turn).wait_send()
+            stage_four(u, turn).wait_send()
+    for which, buffer in smalls:
         for k in range(1, 4):
-            small(which, k, lax.rem(group + k, 4), group).wait_send()
-
-
-def sum_over_groups(value, vector):
-    rows = value.shape[0]
-    quarter = rows // 64 * 16
-    pieces = 2 if quarter % 32 == 0 else 1
-    spare = -(-(rows - 4 * quarter) // 16) * 16
-    size, units = quarter // pieces, 2 * pieces
+            small(which, buffer, k, lax.rem(group + k, 4), group).wait_send()
+
+
+def sum_over_groups(values, vector):
+    shapes = []
+    for value in values:
+        rows = value.shape[0]
+        quarter = rows // 64 * 16
+        shapes.append((rows, quarter, 2 if quarter % 32 == 0 and quarter > 256 else 1))
+    units = sum(2 * pieces for rows, quarter, pieces in shapes)
     vmem = pl.BlockSpec(memory_space=pltpu.VMEM)
-    block = lambda *lead: pltpu.VMEM(lead + (size, D // 2), LOW)
+    scratch = []
+    for lead in ((2,), (2,), ()):
+        for rows, quarter, pieces in shapes:
+            scratch.append(pltpu.VMEM((2 * pieces,) + lead + (quarter // pieces, D // 2), LOW))
+    for rows, quarter, pieces in shapes:
+        spare = -(-(rows - 4 * quarter) // 16) * 16
+        scratch.append(pltpu.VMEM((4, max(spare, 16), D), LOW))
     dma = pltpu.SemaphoreType.DMA
-    return pl.pallas_call(
-        functools.partial(sum_kernel, (rows, quarter, pieces)),
-        out_shape=(
-            jax.ShapeDtypeStruct(value.shape, LOW),
-            jax.ShapeDtypeStruct(vector.shape, F32),
-        ),
-        in_specs=[vmem, vmem],
-        out_specs=(vmem, vmem),
-        scratch_shapes=[
-            block(units, 2), block(units, 2), block(units),
-            pltpu.VMEM((4, max(spare, 16), D), LOW), pltpu.VMEM((4,) + vector.shape, F32),
+    count = len(values)
+    *totals, vector_total = pl.pallas_call(
+        functools.partial(sum_kernel, tuple(shapes)),
+        out_shape=[jax.ShapeDtypeStruct(value.shape, LOW) for value in values]
+        + [jax.ShapeDtypeStruct(vector.shape, F32)],
+        in_specs=[vmem] * (count + 1),
+        out_specs=[vmem] * (count + 1),
+        scratch_shapes=scratch
+        + [
+            pltpu.VMEM((4,) + vector.shape, F32),
             dma((units, 2)), dma((units, 2)), dma((units,)), dma((units,)), dma((units,)),
-            dma((units,)), dma((units, 2)), dma((units, 2)), dma((2, 4)), dma((2, 4)),
+            dma((units,)), dma((units, 2)), dma((units, 2)), dma((count + 1, 4)), dma((count + 1, 4)),
         ],
         compiler_params=pltpu.CompilerParams(
-            collective_id=4, has_side_effects=True, vmem_limit_bytes=48 * 1024 * 1024
+            collective_id=4, has_side_effects=True, vmem_limit_bytes=52 * 1024 * 1024
         ),
         cost_estimate=pl.CostEstimate(flops=0, bytes_accessed=300_000_000, transcendentals=0),
         name="sum_groups",
-    )(value, vector)
+    )(*values, vector)
+    return totals, vector_total
 
 
 def prepare(n, slots, vocab, tokens, routes, segments, loss_pos):
@@ -1243,10 +1294,9 @@
     return (weight_new, first_new, second_new)
 
 
-def quick_window(n, slots, sizes, steps, x_start, lows, masters, firsts, seconds, outers, row_total):
+def quick_window(n, slots, sizes, steps, x_start, lows, masters, firsts, seconds, outers):
     embedding, attention, experts, vectors = masters
     vocab = embedding.shape[0]
-    threshold = 0.05 / math.sqrt(row_total)
     vector_rates = jnp.where(jnp.arange(vectors.shape[0])[:, None] < 4, LR_GAIN, LR_ROUTER)
     rate_list = (LR_EMBED, LR_MATRIX, LR_MATRIX, vector_rates)
     decay_list = (DECAY, DECAY, DECAY, 0.0)
@@ -1255,7 +1305,7 @@
     def replay(k, factors):
         state = (masters[k], firsts[k], seconds[k])
         for s, factor in enumerate(factors):
-            gradient = taken[s][k] * factor
+            gradient = taken[s][k].astype(jnp.float32) * factor
             state = adam_quick(
                 *state, gradient, float(STEP0 + s + 1), rate_list[k], decay_list[k]
             )
@@ -1275,14 +1325,12 @@
             x_low = fetch(n, slots, sizes, ints, embed_low)
         else:
             (embed_low, attn_low, expert_low), x_low = lows, x_start
-        *grads, shared, loss = run_step(
+        *grads, dvector, loss, norm_value, factor = run_step(
             n, slots, vocab, sizes, ints, vector_state[0], x_low, embed_low, attn_low, expert_low
         )
-        dvector = shared[: vectors.shape[0]]
-        norm_value = jnp.sqrt(shared[6, 0] + jnp.sum(dvector * dvector))
-        factor = jnp.minimum(1.0, threshold / norm_value)
+        loss, norm_value, factor = loss[0, 0], norm_value[0, 0], factor[0, 0]
         taken.append(grads)
-        loss_list.append(loss[0, 0])
+        loss_list.append(loss)
         norm_list.append(norm_value)
         factor_list.append(factor)
         vector_gradient = dvector * factor
@@ -1290,13 +1338,17 @@
             *vector_state, vector_gradient, float(STEP0 + s + 1), vector_rates, 0.0
         )
     again = lax.optimization_barrier(tuple(factor_list))
-    states = [replay(k, again) for k in range(3)] + [vector_state]
-    deltas = [master - state[0] for master, state in zip(masters, states)]
-    matrix_sums = lax.psum(for_sending((deltas[1], deltas[2])), "grp")
-    embed_sum, vector_sum = sum_over_groups(
-        deltas[0].astype(jnp.bfloat16), jnp.pad(deltas[3], ((0, 2), (0, 0)))
-    )
-    sums = (embed_sum, matrix_sums[0], matrix_sums[1], vector_sum[: vectors.shape[0]])
+    low_delta = lambda k, state: (masters[k] - state[0]).astype(jnp.bfloat16)
+    expert_state = replay(2, again)
+    expert_delta = low_delta(2, expert_state)
+    expert_sum = lax.psum(expert_delta, "grp")
+    *again, expert_delta = lax.optimization_barrier((*again, expert_delta))
+    states = [replay(0, again), replay(1, again), expert_state, vector_state]
+    attn_delta = low_delta(1, states[1])
+    (embed_sum, attn_sum), vector_sum = sum_over_groups(
+        (low_delta(0, states[0]), attn_delta.reshape(-1, D)), vectors - vector_state[0]
+    )
+    sums = (embed_sum, attn_sum.reshape(attn_delta.shape), expert_sum, vector_sum)
     results = [jnp.stack(loss_list)[None], jnp.stack(norm_list)[None]]
     for k in range(4):
         delta_mean = sums[k].astype(jnp.float32) / lax.axis_size("grp")
@@ -1377,7 +1429,7 @@
         )
         firsts, seconds = [value[0] for value in firsts], [value[0] for value in seconds]
         return quick_window(
-            n, slots, sizes, steps, x_start, lows, masters, firsts, seconds, outers, row_total
+            n, slots, sizes, steps, x_start, lows, masters, firsts, seconds, outers
         )
 
     def general(*state):

time: 671 us -> 647 us (0.964)
  Pallas kernels: 447 us -> 427 us
    pallas_call x2, Pallas kernels: 238 us -> 217 us  [run_step(): pl.pallas_call(functools.partial(step_kernel, (n, slots, vocab, vocab_row...]
    broadcast_in_dim x2 -> x3, other arithmetic: 16 us -> 26.8 us  [quick_window(): results += [states[k][1][None], states[k][2][None], master_new, outer_new]]
    convert_element_type x2 -> x1, other arithmetic: 44.8 us -> 36.7 us  [quick_window(): low_delta = lambda k, state: (masters[k] - state[0]).astype(jnp.bfloat16)]
  transfers between devices with their start and end apart: 3 -> 3, of which waited for: 2 -> 2; matrix products, arithmetic and copies ran while one was open for 18% -> 19% of each run, Pallas kernels for 32% -> 33%
where the time goes in v4:
time: 647 us; the launch traced here: 637 us
  Pallas kernels  427 us (66%)
  other arithmetic  153 us (24%)
  waiting for transfers between devices  21.2 us (3%)
  between operations  14.9 us (2%)
  local copies, waits for them, and re-layouts  11.8 us (2%)
  loops' own time  9.04 us (1%)
    pallas_call x2, Pallas kernels, run_step(): pl.pallas_call(functools.partial(step_kernel, (n, slots, vocab, vocab_row...  217 us
    pallas_call x1, Pallas kernels, sum_over_groups(): pl.pallas_call(functools.partial(sum_kernel, tuple(shapes)), out_shape=[j...  138 us
    pallas_call x2, Pallas kernels, fetch(): pl.pallas_call(functools.partial(fetch_kernel, (n, slots, vocab_rows) + s...  57.3 us
    convert_element_type x1, other arithmetic, quick_window(): low_delta = lambda k, state: (masters[k] - state[0]).astype(jnp.bfloat16)  36.7 us
    broadcast_in_dim x3, other arithmetic, quick_window(): results += [states[k][1][None], states[k][2][None], master_new, outer_new]  26.8 us
    convert_element_type x1, other arithmetic, window(): new_master[0].astype(jnp.bfloat16)  19.8 us
    convert_element_type x1, other arithmetic, quick_window(): embed_low = padded(replay(0, again)[0].astype(jnp.bfloat16))  19.1 us
    pallas_call x1, Pallas kernels, share(): pl.pallas_call(functools.partial(share_kernel, n, groups), out_shape=(jax...  14.7 us
  transfers between devices with their start and end apart: 3, of which 2 were waited for; matrix products, arithmetic and copies ran while one was open for 19% of the time, Pallas kernels for 33%

profile of v4, /device:TPU:0, one launch (start us, length us, event | category | flops | bytes accessed | tf_op | source)
XLA Modules:
  0.0 637.1 jit_solution(8353436915503888639)
XLA Ops:
  7.2 2.3 convert_element_type.363
  9.6 0.7 copy.419
  10.3 0.7 copy.418
  11.0 0.7 pad.25
  11.7 0.7 broadcast_add_fusion.3
  12.3 0.7 copy_bitcast_fusion.2
  13.0 1.0 select_reduce_fusion.10
  14.1 0.3 fusion.305
  14.4 0.7 and_select_fusion.3
  15.1 0.3 convert_reduce_fusion
  15.3 0.3 select_reduce_fusion.9
  15.6 0.6 select_reduce_fusion.14
  16.3 0.3 select_reduce_fusion.8
  16.6 0.6 broadcast_in_dim.427
  17.2 0.7 concatenate.39.packed
  17.9 14.7 %share_ids.1 = (s32[8,2,640]{2,1,0:T(2,128)}, s32[8,128]{1,0:T(8,128)}) custom-call(s32[2,640]{1,0:T(2,128)} %concatenate.39.packed), custom_call_target="tpu_custom_call" | custom-call | tf_op jit(solution)/shard_map/share_ids/pallas_call | solution.py:341
  32.6 1.3 slice.182
  34.5 0.8 subtract_bitcast_fusion.1
  35.4 0.7 slice_bitcast_fusion.57
  36.2 0.8 subtract_bitcast_fusion
  37.1 4.0 convert_element_type.364
  41.1 7.8 %convert_element_type.362.eb = bf16[4016,768]{1,0:T(8,128)(2,1)} convert(f32[4016,768]{1,0:T(8,128)} %param.30) | non-fusion elementwise | flops 3084288 | bytes 18505728 | tf_op jit(solution)/shard_map/convert_element_type | solution.py:1401
  49.0 31.2 %fetch_rows.3 = bf16[256,768]{1,0:T(8,128)(2,1)} custom-call(s32[8,384]{1,0:T(8,128)S(1)} %slice_bitcast_fusion.56.ints, bf16[4016,768]{1,0:T(8,128)(2,1)} %convert_element_type.362.eb), custom_call_target="tpu_custom_call" | custom-call | tf_op jit(solution)/shard_map/fetch_rows/pallas_call | solution.py:398
  80.2 7.6 %all-gather.24.cloned.1.call-done = bf16[5,768,768]{2,1,0:T(8,128)(2,1)} async-done(((bf16[5,96,768]{2,1,0:T(8,128)(2,1)}), bf16[5,768,768]{2,1,0:T(8,128)(2,1)}) %all-gather.24.cloned.1.call-update) | async-done | bytes 5898256 | tf_op jit(solution)/shard_map/all_gather | solution.py:1402
  87.8 541.8 %conditional.3 = (f32[1,2]{1,0:T(1,128)S(1)}, f32[1,2]{1,0:T(1,128)S(1)}, f32[1,4016,768]{2,1,0:T(8,128)}, f32[1,4016,768]{2,1,0:T(8,128)}, f32[4016,768]{1,0:T(...) conditional(s32[]{:T(128)} %bitcast.161, ((), ...), branch_computations={%region_9.97_spmd, %region_96.99_spmd} | conditional | flops 16723800064 | bytes 1105412352
  96.5 0.5 copy-done.60
  97.0 1.3 slice_bitcast_fusion.1
  98.4 108.5 %inner_step.2 = (bf16[4016,768]{1,0:T(8,128)(2,1)}, bf16[5,96,768]{2,1,0:T(8,128)(2,1)}, bf16[2,2,768,384]{3,2,1,0:T(8,128)(2,1)}, f32[6,768]{1,0:T(8,128)}, f32...) custom-call(s32[8,384]{1,0:T(8,128)} %get-tuple-element.927.ints, f32[6,768]{1,0:T(8,128)S(1)} %get-tuple-element.166.vec, ...), custom_call_target="tpu_custom_call" | custom-call | tf_op jit(solution)/shard_map/cond/branch_1_fun/inner_step/pallas_call | solution.py:791
  206.9 4.4 fusion.51
  211.3 19.1 %fusion.16.eb.eb_in = bf16[4016,768]{1,0:T(8,128)(2,1)S(1)} fusion(f32[4016,768]{1,0:T(8,128)} %get-tuple-element.176, bf16[4016,768]{1,0:T(8,128)(2,1)} %get-tuple-element.178, f32[1,4016,768]{2,1,0:T(8,128)} %get-tuple-element.179, f32[1,4016,768]{2,1,0:T(8,128)} %get-tuple-element.177, f32[]{:T(128)} %bitcast.134), kind=kLoop, calls=%fused_computation.43 | loop fusion | flops 55517184 | bytes 49348612 | tf_op jit(solution)/shard_map/cond/branch_1_fun/convert_element_type | solution.py:1324
  230.5 26.1 %fetch_rows.2.x_low = bf16[256,768]{1,0:T(8,128)(2,1)S(1)} custom-call(s32[8,384]{1,0:T(8,128)S(1)} %get-tuple-element.928.ints, bf16[4016,768]{1,0:T(8,128)(2,1)S(1)} %fusion.16.eb.eb_in), custom_call_target="tpu_custom_call" | custom-call | tf_op jit(solution)/shard_map/cond/branch_1_fun/fetch_rows/pallas_call | solution.py:398
  256.6 2.7 copy-done
  259.2 0.7 copy-done.1
  260.0 1.3 multiply_subtract_fusion.4.vec
  261.3 8.9 %fusion.33.expw_in = bf16[2,2,768,384]{3,2,1,0:T(8,128)(2,1)} fusion(f32[2,2,768,384]{3,2,1,0:T(8,128)} %get-tuple-element.184, bf16[2,2,768,384]{3,2,1,0:T(8,128)(2,1)S(1)} %copy-done.14, f32[1,2,2,768,384]{4,3,2,1,0:T(8,128)} %get-tuple-element.187, f32[1,2,2,768,384]{4,3,2,1,0:T(8,128)} %get-tuple-element.185, f32[]{:T(128)} %bitcast.134), kind=kLoop, calls=%fused_computation.71 | loop fusion | flops 21233664 | bytes 18874372 | tf_op jit(solution)/shard_map/cond/branch_1_fun/convert_element_type | solution.py:1323
  270.1 13.5 %all-gather.22.cloned.1.call-done.attn_in = bf16[5,768,768]{2,1,0:T(8,128)(2,1)} async-done(((bf16[5,96,768]{2,1,0:T(8,128)(2,1)}), bf16[5,768,768]{2,1,0:T(8,128)(2,1)}) %all-gather.22.cloned.1.call-update) | async-done | bytes 5898256 | tf_op jit(solution)/shard_map/cond/branch_1_fun/all_gather | solution.py:1320
  283.7 108.5 %inner_step.3 = (bf16[4016,768]{1,0:T(8,128)(2,1)}, bf16[5,96,768]{2,1,0:T(8,128)(2,1)}, bf16[2,2,768,384]{3,2,1,0:T(8,128)(2,1)}, f32[6,768]{1,0:T(8,128)}, f32...) custom-call(s32[8,384]{1,0:T(8,128)} %copy-done.2, f32[6,768]{1,0:T(8,128)} %multiply_subtract_fusion.4.vec, ...), custom_call_target="tpu_custom_call" | custom-call | tf_op jit(solution)/shard_map/cond/branch_1_fun/inner_step/pallas_call | solution.py:791
  392.2 2.1 fusion.57
  394.4 17.4 %fusion.35 = (f32[1,2,2,768,384]{4,3,2,1,0:T(8,128)}, bf16[2,2,768,384]{3,2,1,0:T(8,128)(2,1)}, f32[1,2,2,768,384]{4,3,2,1,0:T(8,128)}) fusion(bf16[2,2,768,384]{3,2,1,0:T(8,128)(2,1)} %get-tuple-element.194, bf16[2,2,768,384]{3,2,1,0:T(8,128)(2,1)} %get-tuple-element.186, f32[1,2,2,768,384]{4,3,2,1,0:T(8,128)} %get-tuple-element.187, f32[]{:T(128)} %bitcast.147, ...), kind=kLoop, calls=%fused_computation.73 | loop fusion | flops 42467328 | bytes 30670856 | tf_op jit(solution)/shard_map/cond/branch_1_fun/broadcast_in_dim | solution.py:1359
  411.8 7.3 %fusion.53 = (f32[1,5,96,768]{3,2,1,0:T(8,128)}, bf16[5,96,768]{2,1,0:T(8,128)(2,1)S(1)}, f32[1,5,96,768]{3,2,1,0:T(8,128)}) fusion(bf16[5,96,768]{2,1,0:T(8,128)(2,1)} %get-tuple-element.198, bf16[5,96,768]{2,1,0:T(8,128)(2,1)} %get-tuple-element.182, f32[1,5,96,768]{3,2,1,0:T(8,128)} %get-tuple-element.183, f32[]{:T(128)} %bitcast.147, f32[]{:T(128)} %bitcast.134, ...), kind=kLoop, calls=%fused_computation.102 | loop fusion | flops 13271040 | bytes 9584648 | tf_op jit(solution)/shard_map/cond/branch_1_fun/broadcast_in_dim | solution.py:1359
  419.1 36.7 %subtract_convert_fusion = (bf16[4016,768]{1,0:T(8,128)(2,1)}, f32[1,4016,768]{2,1,0:T(8,128)}, f32[1,4016,768]{2,1,0:T(8,128)}) fusion(f32[4016,768]{1,0:T(8,128)} %get-tuple-element.176, bf16[4016,768]{1,0:T(8,128)(2,1)} %get-tuple-element.196, bf16[4016,768]{1,0:T(8,128)(2,1)} %get-tuple-element.178, f32[1,4016,768]{2,1,0:T(8,128)} %get-tuple-element.177, ...), kind=kLoop, calls=%fused_computation.39 | loop fusion | flops 111034368 | bytes 80191496 | tf_op jit(solution)/shard_map/cond/branch_1_fun/convert_element_type | solution.py:1341
  455.8 138.0 %sum_groups.1 = (bf16[4016,768]{1,0:T(8,128)(2,1)}, bf16[480,768]{1,0:T(8,128)(2,1)S(1)}, f32[6,768]{1,0:T(8,128)S(1)}) custom-call(bf16[4016,768]{1,0:T(8,128)(2,1)} %get-tuple-element.914.refs_0_, bf16[480,768]{1,0:T(8,128)(2,1)S(1)} %bitcast.636, f32[6,768]{1,0:T(8,128)S(1)} %get-tuple-element.924.refs_2_), custom_call_target="tpu_custom_call" | custom-call | bytes 300000000 | tf_op jit(solution)/shard_map/cond/branch_1_fun/sum_groups/pallas_call | solution.py:985
  593.8 0.1 convert_multiply_fusion.10
  594.0 2.4 fusion.308
  596.4 3.2 maximum_bitcast_fusion
  599.5 19.8 %fusion.309 = (bf16[4016,768]{1,0:T(8,128)(2,1)}, f32[4016,768]{1,0:T(8,128)}, f32[4016,768]{1,0:T(8,128)}) fusion(f32[4016,768]{1,0:T(8,128)} %get-tuple-element.176, bf16[4016,768]{1,0:T(8,128)(2,1)S(1)} %copy-done.16, f32[4016,768]{1,0:T(8,128)} %get-tuple-element.201), kind=kLoop, calls=%fused_computation.676 | loop fusion | flops 27758592 | bytes 61685760 | tf_op jit(solution)/shard_map/cond/branch_0_fun/convert_element_type | solution.py:1267
  619.3 10.1 %fusion.307 = (bf16[2,2,768,384]{3,2,1,0:T(8,128)(2,1)}, f32[2,2,768,384]{3,2,1,0:T(8,128)}, f32[2,2,768,384]{3,2,1,0:T(8,128)}) fusion(f32[2,2,768,384]{3,2,1,0:T(8,128)} %get-tuple-element.184, bf16[2,2,768,384]{3,2,1,0:T(8,128)(2,1)} %all-reduce.18.cloned.1.call-done, f32[2,2,768,384]{3,2,1,0:T(8,128)} %get-tuple-element.204), kind=kLoop, calls=%fused_computation.674 | loop fusion | flops 10616832 | bytes 23592960 | tf_op jit(solution)/shard_map/cond/branch_0_fun/convert_element_type | solution.py:1277
  629.7 0.5 copy-done.86
  (86 shorter events, 0.9 us)
Async XLA Ops:
  7.2 80.6 %all-gather.24.cloned.1.call-start = ((), (), s32[]{:S(2)}) async-start(), calls=%async_computation.27 | async-start | bytes 6635520 | tf_op jit(solution)/shard_map/all_gather | solution.py:1402
  48.9 38.9 %copy-start.3 = (f32[5,96,768]{2,1,0:T(8,128)S(1)}, f32[5,96,768]{2,1,0:T(8,128)}, u32[]{:S(2)}) copy-start(f32[5,96,768]{2,1,0:T(8,128)} %param.34) | copy-start | bytes 4423684
  48.9 38.9 %copy-start.10 = (f32[1,5,96,768]{3,2,1,0:T(8,128)S(1)}, f32[1,5,96,768]{3,2,1,0:T(8,128)}, u32[]{:S(2)}) copy-start(f32[1,5,96,768]{3,2,1,0:T(8,128)} %param.35) | copy-start | bytes 4423684
  48.9 38.9 %copy-start.22 = (f32[6,768]{1,0:T(8,128)S(1)}, f32[6,768]{1,0:T(8,128)}, u32[]{:S(2)}) copy-start(f32[6,768]{1,0:T(8,128)} %param.42) | copy-start | bytes 55300
  48.9 38.9 %copy-start.82 = (s32[2,1,256]{2,1,0:T(1,128)S(1)}, s32[2,1,256]{2,1,0:T(1,128)}, u32[]{:S(2)}) copy-start(s32[2,1,256]{2,1,0:T(1,128)} %param.26) | copy-start | bytes 6148
  48.9 38.9 %copy-start.85 = (s32[2,1,16]{2,1,0:T(1,128)S(1)}, s32[2,1,16]{2,1,0:T(1,128)}, u32[]{:S(2)}) copy-start(s32[2,1,16]{2,1,0:T(1,128)} %param.29) | copy-start | bytes 388
  48.9 38.9 %copy-start.128 = (s32[2,1,256]{2,1,0:T(1,128)S(1)}, s32[2,1,256]{2,1,0:T(1,128)}, u32[]{:S(2)}) copy-start(s32[2,1,256]{2,1,0:T(1,128)} %param.28) | copy-start | bytes 6148
  48.9 38.9 %copy-start.129 = (s32[2,1,256,1]{2,3,1,0:T(1,128)S(1)}, s32[2,1,256,1]{2,3,1,0:T(1,128)}, u32[]{:S(2)}) copy-start(s32[2,1,256,1]{2,3,1,0:T(1,128)} %param.27) | copy-start | bytes 6148
  96.4 0.6 copy-start.60
  96.4 187.2 %all-gather.22.cloned.1.call-start = ((), (), s32[]{:S(2)}) async-start(), calls=%async_computation.25 | async-start | bytes 6635520 | tf_op jit(solution)/shard_map/cond/branch_1_fun/all_gather | solution.py:1320
  98.4 132.1 %copy-start.2 = (s32[8,384]{1,0:T(8,128)}, s32[8,384]{1,0:T(8,128)S(1)}, u32[]{:S(2)}) copy-start(s32[8,384]{1,0:T(8,128)S(1)} %get-tuple-element.928.ints) | copy-start | bytes 36868 | tf_op jit(solution)/shard_map/conditional.1
  211.3 408.0 %all-reduce.18.cloned.1.call-start = ((), (), s32[]{:S(2)}) async-start(), calls=%async_computation.26 | async-start | bytes 4718592 | tf_op jit(solution)/shard_map/cond/branch_1_fun/psum | solution.py:1344
  230.4 29.5 %copy-start.49 = (f32[1,6,768]{2,0,1:T(1,128)S(1)}, f32[1,6,768]{2,0,1:T(1,128)}, u32[]{:S(2)}) copy-start(f32[1,6,768]{2,0,1:T(1,128)} %get-tuple-element.787) | copy-start | bytes 55300 | tf_op jit(solution)/shard_map/conditional.1
  230.5 29.5 %copy-start.51 = (f32[1,6,768]{2,0,1:T(1,128)S(1)}, f32[1,6,768]{2,0,1:T(1,128)}, u32[]{:S(2)}) copy-start(f32[1,6,768]{2,0,1:T(1,128)} %get-tuple-element.788) | copy-start | bytes 55300 | tf_op jit(solution)/shard_map/conditional.1
  230.5 29.5 %copy-start.69 = (f32[6,768]{1,0:T(8,128)S(1)}, f32[6,768]{1,0:T(8,128)}, u32[]{:S(2)}) copy-start(f32[6,768]{1,0:T(8,128)} %get-tuple-element.173) | copy-start | bytes 55300 | tf_op jit(solution)/shard_map/conditional.1
  230.5 30.8 %copy-start.14 = (bf16[2,2,768,384]{3,2,1,0:T(8,128)(2,1)S(1)}, bf16[2,2,768,384]{3,2,1,0:T(8,128)(2,1)}, u32[]{:S(2)}) copy-start(bf16[2,2,768,384]{3,2,1,0:T(8,128)(2,1)} %get-tuple-element.186) | copy-start | bytes 7077892 | tf_op jit(solution)/shard_map/conditional.1
  256.6 2.7 copy-start
  259.2 0.7 copy-start.1
  270.1 122.1 %copy-start.57 = (f32[6,768]{1,0:T(8,128)S(1)}, f32[6,768]{1,0:T(8,128)}, u32[]{:S(2)}) copy-start(f32[6,768]{1,0:T(8,128)} %multiply_subtract_fusion.4.vec) | copy-start | bytes 55300 | tf_op jit(solution)/shard_map/conditional.1
  455.8 138.2 %copy-start.71 = (f32[6,768]{1,0:T(8,128)S(1)}, f32[6,768]{1,0:T(8,128)}, u32[]{:S(2)}) copy-start(f32[6,768]{1,0:T(8,128)} %get-tuple-element.206) | copy-start | bytes 55300 | tf_op jit(solution)/shard_map/conditional.1
  455.8 138.2 %copy-start.18 = (f32[5,96,768]{2,1,0:T(8,128)S(1)}, f32[5,96,768]{2,1,0:T(8,128)}, u32[]{:S(2)}) copy-start(f32[5,96,768]{2,1,0:T(8,128)} %get-tuple-element.203) | copy-start | bytes 4423684 | tf_op jit(solution)/shard_map/conditional.1
  593.8 5.7 copy-start.16
  629.6 0.6 copy-start.86
  629.7 0.6 copy-start.87
  629.7 0.6 copy-start.88
  629.7 0.6 copy-start.89
  629.7 0.6 copy-start.90
  629.7 0.6 copy-start.157
  629.7 0.6 copy-start.158
Sparse Core Ops, SparseCore 0:
  10.2 77.5 all-gather.23
  211.4 72.2 all-gather.21
  411.9 88.3 all-reduce.17

commit v5 on v4

--- a/solution.py
+++ b/solution.py
@@ -414,6 +414,10 @@
     )(ints, embed_low)
 
 
+def packs(shard, wide):
+    return wide == 192 and shard % 32 == 0
+
+
 def step_kernel(
     dims,
     ints, vec, x_low, eb_in, attn_in, expw_in,
@@ -426,6 +430,7 @@
     all_rows = n * row_count
     wide = HEADS * row_count
     shard = D // n
+    packed = packs(shard, wide)
     row_total = float(all_rows)
     scale = 2.0 * D ** (-0.5)
     factor_qk = HEAD_DIM ** (-0.5)
@@ -672,7 +677,13 @@
         shares = jnp.where(line == i, value, shares)
     dvec[me] = shares
     relay(D_VEC, dvec)
-    dss[...] = dot_nt(a_turned, dscores).reshape(n, shard, wide).astype(LOW)
+    turned_scores = dot_nt(a_turned, dscores).reshape(n, shard, wide)
+    if packed:
+        dss[:, 0:shard] = turned_scores[:, :, 0:128].astype(LOW)
+        dss[:, shard:, 0 : wide - 128] = turned_scores[:, : shard // 2, 128:].astype(LOW)
+        dss[:, shard:, wide - 128 :] = turned_scores[:, shard // 2 :, 128:].astype(LOW)
+    else:
+        dss[...] = turned_scores.astype(LOW)
     deal(DS_A, dss, dsr)
     dsr[me] = dss[me]
 
@@ -744,7 +755,15 @@
     arrive(DS_A, dsr)
     dkey = jnp.zeros((shard, D), F32)
     for j in range(n):
-        dkey = dkey + dot_nn(dsr[j], widen(q_all[j]))
+        q_one = widen(q_all[j])
+        if packed:
+            tail = q_one[128:wide]
+            upper = dot_nn(dsr[j, shard:, 0 : wide - 128], tail)
+            lower = dot_nn(dsr[j, shard:, wide - 128 :], tail)
+            dkey = dkey + dot_nn(dsr[j, 0:shard], q_one[0:128])
+            dkey = dkey + jnp.concatenate([upper, lower], axis=0)
+        else:
+            dkey = dkey + dot_nn(dsr[j], q_one)
     squares = squares + keep(1, dkey * factor_qk)
     tiles = [(i, i * TILE, TILE) for i in range(whole)]
     if vocab_rows % TILE:
@@ -784,6 +803,7 @@
     shard = D // n
     all_rows = n * row_count
     wide = HEADS * row_count
+    score_shape = (n, shard + shard // 2, 128) if packs(shard, wide) else (n, shard, wide)
     vmem = pl.BlockSpec(memory_space=pltpu.VMEM)
     anywhere = pl.BlockSpec(memory_space=pl.ANY)
     low = lambda *shape: pltpu.VMEM(shape, LOW)
@@ -811,7 +831,7 @@
             low(n, row_count, D), low(n, shard, wide + 2 * row_count),
             low(n, shard, wide + 2 * row_count),
             low(n, row_count, D), low(n, row_count, D), low(n, row_count, D),
-            low(n, shard, wide), low(n, shard, wide),
+            low(*score_shape), low(*score_shape),
             wide_float(n, 8, D), wide_float(n, 8, 128),
             wide_float(vocab_rows, 2 * all_rows), low(vocab_rows, 2 * all_rows),
             wide_float(EXPERTS, all_rows, hidden), low(EXPERTS, all_rows, hidden),
@@ -834,8 +854,16 @@
     count = len(shapes)
     values, vector, refs = refs[:count], refs[count], refs[count + 1 :]
     totals, vector_total, refs = refs[:count], refs[count], refs[count + 1 :]
-    helds, first_ins, second_ins, rests = (refs[i * count : (i + 1) * count] for i in range(4))
-    flat, *sems = refs[4 * count :]
+    helds, first_ins, second_ins, rests, nears = (
+        refs[i * count : (i + 1) * count] for i in range(5)
+    )
+    flat, load_sem, *sems = refs[5 * count :]
+    loads = [
+        pltpu.make_async_copy(value, near, load_sem.at[array])
+        for array, (value, near) in enumerate(zip(values, nears))
+    ]
+    for load in loads:
+        load.start()
     one_s, one_r, two_s, two_r, three_s, three_r, four_s, four_r, rest_s, rest_r = sems
     group = lax.axis_index("grp")
     width = D // 2
@@ -897,12 +925,18 @@
         ]
         return copy(block, block, four_s.at[u, turn], four_r.at[u, turn], flip(side))
 
+    every = range(len(units))
+    for turn in range(2):
+        for u in every:
+            stage_one(u, turn).start()
+    for load in loads:
+        load.wait()
     flat[group] = vector[...]
     smalls = [(count, flat)]
     for array, (rows, quarter, pieces) in enumerate(shapes):
         spare = rows - 4 * quarter
         if spare:
-            rests[array][group, 0:spare] = values[array][4 * quarter : rows]
+            rests[array][group, 0:spare] = nears[array][4 * quarter : rows]
             smalls.append((array, rests[array]))
 
     def small(which, buffer, k, peer, origin):
@@ -910,10 +944,6 @@
             buffer.at[origin], buffer.at[origin], rest_s.at[which, k], rest_r.at[which, origin], peer
         )
 
-    every = range(len(units))
-    for turn in range(2):
-        for u in every:
-            stage_one(u, turn).start()
     for which, buffer in smalls:
         for k in range(1, 4):
             small(which, buffer, k, lax.rem(group + k, 4), group).start()
@@ -924,7 +954,7 @@
             stage_one(u, turn).wait_recv()
             mine = place(u, bits[side], there if turn else 1 - there)
             helds[array][slot, turn] = (
-                values[array][mine].astype(F32) + first_ins[array][slot, turn].astype(F32)
+                nears[array][mine].astype(F32) + first_ins[array][slot, turn].astype(F32)
             ).astype(LOW)
             if turn == 0:
                 stage_two(u).start()
@@ -986,11 +1016,13 @@
         functools.partial(sum_kernel, tuple(shapes)),
         out_shape=[jax.ShapeDtypeStruct(value.shape, LOW) for value in values]
         + [jax.ShapeDtypeStruct(vector.shape, F32)],
-        in_specs=[vmem] * (count + 1),
+        in_specs=[pl.BlockSpec(memory_space=pl.ANY)] * count + [vmem],
         out_specs=[vmem] * (count + 1),
         scratch_shapes=scratch
+        + [pltpu.VMEM(value.shape, LOW) for value in values]
         + [
             pltpu.VMEM((4,) + vector.shape, F32),
+            dma((count,)),
             dma((units, 2)), dma((units, 2)), dma((units,)), dma((units,)), dma((units,)),
             dma((units,)), dma((units, 2)), dma((units, 2)), dma((count + 1, 4)), dma((count + 1, 4)),
         ],
@@ -1283,15 +1315,15 @@
     )
 
 
-def adam_quick(weight, first_moment, second, gradient, step_float, rate_here, decay_here):
+def adam_move(move, first_moment, second, gradient, step_float, rate_here, decay_here):
     first_new = BETA_ONE * first_moment + (1.0 - BETA_ONE) * gradient
     second_new = BETA_TWO * second + (1.0 - BETA_TWO) * gradient * gradient
     first_hat = first_new * (1.0 / (1.0 - BETA_ONE**step_float))
     second_hat = second_new * (1.0 / (1.0 - BETA_TWO**step_float))
-    weight_new = weight - rate_here * (
-        first_hat / (jnp.sqrt(second_hat) + ADAM_EPS) + decay_here * weight
-    )
-    return (weight_new, first_new, second_new)
+    step = rate_here * (first_hat / (jnp.sqrt(second_hat) + ADAM_EPS))
+    if move is not None:
+        step = (1.0 - rate_here * decay_here) * move + step
+    return (step, first_new, second_new)
 
 
 def quick_window(n, slots, sizes, steps, x_start, lows, masters, firsts, seconds, outers):
@@ -1303,13 +1335,19 @@
     taken = []
 
     def replay(k, factors):
-        state = (masters[k], firsts[k], seconds[k])
+        state = (None, firsts[k], seconds[k])
         for s, factor in enumerate(factors):
             gradient = taken[s][k].astype(jnp.float32) * factor
-            state = adam_quick(
+            state = adam_move(
                 *state, gradient, float(STEP0 + s + 1), rate_list[k], decay_list[k]
             )
         return state
+
+    def left(k, count):
+        return (1.0 - rate_list[k] * decay_list[k]) ** count
+
+    def moved(k, factors):
+        return left(k, len(factors)) * masters[k] - replay(k, factors)[0]
 
     loss_list, norm_list, factor_list = [], [], []
     vector_state = (vectors, firsts[3], seconds[3])
@@ -1318,10 +1356,10 @@
         if s:
             again = lax.optimization_barrier(tuple(factor_list))
             attn_low = lax.all_gather(
-                replay(1, again)[0].astype(jnp.bfloat16), "fsdp", axis=1, tiled=True
+                moved(1, again).astype(jnp.bfloat16), "fsdp", axis=1, tiled=True
             )
-            expert_low = replay(2, again)[0].astype(jnp.bfloat16)
-            embed_low = padded(replay(0, again)[0].astype(jnp.bfloat16))
+            expert_low = moved(2, again).astype(jnp.bfloat16)
+            embed_low = padded(moved(0, again).astype(jnp.bfloat16))
             x_low = fetch(n, slots, sizes, ints, embed_low)
         else:
             (embed_low, attn_low, expert_low), x_low = lows, x_start
@@ -1334,11 +1372,11 @@
         norm_list.append(norm_value)
         factor_list.append(factor)
         vector_gradient = dvector * factor
-        vector_state = adam_quick(
+        vector_state = adam_update(
             *vector_state, vector_gradient, float(STEP0 + s + 1), vector_rates, 0.0
         )
     again = lax.optimization_barrier(tuple(factor_list))
-    low_delta = lambda k, state: (masters[k] - state[0]).astype(jnp.bfloat16)
+    low_delta = lambda k, state: state[0].astype(jnp.bfloat16)
     expert_state = replay(2, again)
     expert_delta = low_delta(2, expert_state)
     expert_sum = lax.psum(expert_delta, "grp")
@@ -1351,7 +1389,9 @@
     sums = (embed_sum, attn_sum.reshape(attn_delta.shape), expert_sum, vector_sum)
     results = [jnp.stack(loss_list)[None], jnp.stack(norm_list)[None]]
     for k in range(4):
-        delta_mean = sums[k].astype(jnp.float32) / lax.axis_size("grp")
+        delta_mean = sums[k].astype(jnp.float32) * (1.0 / lax.axis_size("grp"))
+        if k < 3:
+            delta_mean = delta_mean + (1.0 - left(k, len(factor_list))) * masters[k]
         outer_new = OUTER_MOMENTUM * outers[k] + delta_mean
         master_new = masters[k] - OUTER_RATE * (delta_mean + OUTER_MOMENTUM * outer_new)
         if k == 3:

time: 647 us -> 638 us (0.986)
  other arithmetic: 153 us -> 142 us
    convert_element_type x4, other arithmetic: 69 us -> 60.5 us  [the longest x1 28.4 us: quick_window(): low_delta = lambda k, state: state[0].astype(jnp.bfloat16)]
  transfers between devices with their start and end apart: 3 -> 3, of which waited for: 2 -> 2; matrix products, arithmetic and copies ran while one was open for 19% -> 18% of each run, Pallas kernels for 33% -> 34%
where the time goes in v5:
time: 638 us; the launch traced here: 629 us
  Pallas kernels  430 us (67%)
  other arithmetic  142 us (22%)
  waiting for transfers between devices  21.4 us (3%)
  between operations  14.9 us (2%)
  local copies, waits for them, and re-layouts  11.8 us (2%)
  loops' own time  9.05 us (1%)
    pallas_call x2, Pallas kernels, run_step(): pl.pallas_call(functools.partial(step_kernel, (n, slots, vocab, vocab_row...  216 us
    pallas_call x1, Pallas kernels, sum_over_groups(): pl.pallas_call(functools.partial(sum_kernel, tuple(shapes)), out_shape=[j...  142 us
    pallas_call x2, Pallas kernels, fetch(): pl.pallas_call(functools.partial(fetch_kernel, (n, slots, vocab_rows) + s...  57.3 us
    convert_element_type x1, other arithmetic, quick_window(): low_delta = lambda k, state: state[0].astype(jnp.bfloat16)  28.4 us
    broadcast_in_dim x3, other arithmetic, quick_window(): results += [states[k][1][None], states[k][2][None], master_new, outer_new]  26.3 us
    convert_element_type x1, other arithmetic, window(): new_master[0].astype(jnp.bfloat16)  20 us
    convert_element_type x1, other arithmetic, quick_window(): embed_low = padded(moved(0, again).astype(jnp.bfloat16))  19 us
    pallas_call x1, Pallas kernels, share(): pl.pallas_call(functools.partial(share_kernel, n, groups), out_shape=(jax...  14.7 us
  transfers between devices with their start and end apart: 3, of which 2 were waited for; matrix products, arithmetic and copies ran while one was open for 18% of the time, Pallas kernels for 34%

profile of v5, /device:TPU:0, one launch (start us, length us, event | category | flops | bytes accessed | tf_op | source)
XLA Modules:
  0.0 628.9 jit_solution(17146360539407153220)
XLA Ops:
  7.2 2.3 convert_element_type.363
  9.6 0.7 copy.419
  10.3 0.7 copy.418
  11.0 0.7 pad.25
  11.7 0.7 broadcast_add_fusion.3
  12.3 0.7 copy_bitcast_fusion.2
  13.0 1.0 select_reduce_fusion.10
  14.1 0.3 fusion.302
  14.4 0.7 and_select_fusion.3
  15.1 0.3 convert_reduce_fusion
  15.3 0.3 select_reduce_fusion.9
  15.6 0.6 select_reduce_fusion.14
  16.3 0.3 select_reduce_fusion.8
  16.6 0.6 broadcast_in_dim.427
  17.2 0.7 concatenate.39.packed
  17.9 14.7 %share_ids.1 = (s32[8,2,640]{2,1,0:T(2,128)}, s32[8,128]{1,0:T(8,128)}) custom-call(s32[2,640]{1,0:T(2,128)} %concatenate.39.packed), custom_call_target="tpu_custom_call" | custom-call | tf_op jit(solution)/shard_map/share_ids/pallas_call | solution.py:341
  32.6 1.3 slice.182
  34.5 0.8 subtract_bitcast_fusion.1
  35.4 0.7 slice_bitcast_fusion.57
  36.2 0.8 subtract_bitcast_fusion
  37.1 4.0 convert_element_type.364
  41.1 7.8 %convert_element_type.362.eb = bf16[4016,768]{1,0:T(8,128)(2,1)} convert(f32[4016,768]{1,0:T(8,128)} %param.30) | non-fusion elementwise | flops 3084288 | bytes 18505728 | tf_op jit(solution)/shard_map/convert_element_type | solution.py:1441
  49.0 31.2 %fetch_rows.3 = bf16[256,768]{1,0:T(8,128)(2,1)} custom-call(s32[8,384]{1,0:T(8,128)S(1)} %slice_bitcast_fusion.56.ints, bf16[4016,768]{1,0:T(8,128)(2,1)} %convert_element_type.362.eb), custom_call_target="tpu_custom_call" | custom-call | tf_op jit(solution)/shard_map/fetch_rows/pallas_call | solution.py:398
  80.2 7.6 %all-gather.24.cloned.1.call-done = bf16[5,768,768]{2,1,0:T(8,128)(2,1)} async-done(((bf16[5,96,768]{2,1,0:T(8,128)(2,1)}), bf16[5,768,768]{2,1,0:T(8,128)(2,1)}) %all-gather.24.cloned.1.call-update) | async-done | bytes 5898256 | tf_op jit(solution)/shard_map/all_gather | solution.py:1442
  87.8 533.6 %conditional.3 = (f32[1,2]{1,0:T(1,128)S(1)}, f32[1,2]{1,0:T(1,128)S(1)}, f32[1,4016,768]{2,1,0:T(8,128)}, f32[1,4016,768]{2,1,0:T(8,128)}, f32[4016,768]{1,0:T(...) conditional(s32[]{:T(128)} %bitcast.161, ((), ...), branch_computations={%region_9.97_spmd, %region_96.99_spmd} | conditional | flops 16723800064 | bytes 1105412352
  96.5 0.5 copy-done.61
  97.1 1.3 slice_bitcast_fusion.1
  98.4 107.8 %inner_step.2 = (bf16[4016,768]{1,0:T(8,128)(2,1)}, bf16[5,96,768]{2,1,0:T(8,128)(2,1)}, bf16[2,2,768,384]{3,2,1,0:T(8,128)(2,1)}, f32[6,768]{1,0:T(8,128)}, f32...) custom-call(s32[8,384]{1,0:T(8,128)} %get-tuple-element.927.ints, f32[6,768]{1,0:T(8,128)S(1)} %get-tuple-element.166.vec, ...), custom_call_target="tpu_custom_call" | custom-call | tf_op jit(solution)/shard_map/cond/branch_1_fun/inner_step/pallas_call | solution.py:811
  206.2 4.4 fusion.48
  210.6 19.0 %fusion.15.eb.eb_in = bf16[4016,768]{1,0:T(8,128)(2,1)S(1)} fusion(bf16[4016,768]{1,0:T(8,128)(2,1)} %get-tuple-element.178, f32[4016,768]{1,0:T(8,128)} %get-tuple-element.176, f32[1,4016,768]{2,1,0:T(8,128)} %get-tuple-element.179, f32[1,4016,768]{2,1,0:T(8,128)} %get-tuple-element.177, f32[]{:T(128)} %bitcast.134), kind=kLoop, calls=%fused_computation.42 | loop fusion | flops 52432896 | bytes 49348612 | tf_op jit(solution)/shard_map/cond/branch_1_fun/convert_element_type | solution.py:1362
  229.7 26.1 %fetch_rows.2.x_low = bf16[256,768]{1,0:T(8,128)(2,1)S(1)} custom-call(s32[8,384]{1,0:T(8,128)S(1)} %get-tuple-element.928.ints, bf16[4016,768]{1,0:T(8,128)(2,1)S(1)} %fusion.15.eb.eb_in), custom_call_target="tpu_custom_call" | custom-call | tf_op jit(solution)/shard_map/cond/branch_1_fun/fetch_rows/pallas_call | solution.py:398
  255.7 2.7 copy-done
  258.4 0.7 copy-done.1
  259.2 1.3 multiply_subtract_fusion.4.vec
  260.5 8.7 %fusion.31.expw_in = bf16[2,2,768,384]{3,2,1,0:T(8,128)(2,1)} fusion(bf16[2,2,768,384]{3,2,1,0:T(8,128)(2,1)S(1)} %copy-done.14, f32[2,2,768,384]{3,2,1,0:T(8,128)} %get-tuple-element.184, f32[1,2,2,768,384]{4,3,2,1,0:T(8,128)} %get-tuple-element.187, f32[1,2,2,768,384]{4,3,2,1,0:T(8,128)} %get-tuple-element.185, f32[]{:T(128)} %bitcast.134), kind=kLoop, calls=%fused_computation.69 | loop fusion | flops 20054016 | bytes 18874372 | tf_op jit(solution)/shard_map/cond/branch_1_fun/convert_element_type | solution.py:1361
  269.2 13.8 %all-gather.22.cloned.1.call-done.attn_in = bf16[5,768,768]{2,1,0:T(8,128)(2,1)} async-done(((bf16[5,96,768]{2,1,0:T(8,128)(2,1)}), bf16[5,768,768]{2,1,0:T(8,128)(2,1)}) %all-gather.22.cloned.1.call-update) | async-done | bytes 5898256 | tf_op jit(solution)/shard_map/cond/branch_1_fun/all_gather | solution.py:1358
  283.0 107.8 %inner_step.3 = (bf16[4016,768]{1,0:T(8,128)(2,1)}, bf16[5,96,768]{2,1,0:T(8,128)(2,1)}, bf16[2,2,768,384]{3,2,1,0:T(8,128)(2,1)}, f32[6,768]{1,0:T(8,128)}, f32...) custom-call(s32[8,384]{1,0:T(8,128)} %copy-done.2, f32[6,768]{1,0:T(8,128)} %multiply_subtract_fusion.4.vec, ...), custom_call_target="tpu_custom_call" | custom-call | tf_op jit(solution)/shard_map/cond/branch_1_fun/inner_step/pallas_call | solution.py:811
  390.8 2.1 fusion.54
  392.9 16.8 %fusion.33 = (f32[1,2,2,768,384]{4,3,2,1,0:T(8,128)}, bf16[2,2,768,384]{3,2,1,0:T(8,128)(2,1)}, f32[1,2,2,768,384]{4,3,2,1,0:T(8,128)}) fusion(bf16[2,2,768,384]{3,2,1,0:T(8,128)(2,1)} %get-tuple-element.194, bf16[2,2,768,384]{3,2,1,0:T(8,128)(2,1)} %get-tuple-element.186, f32[1,2,2,768,384]{4,3,2,1,0:T(8,128)} %get-tuple-element.187, f32[]{:T(128)} %bitcast.147, ...), kind=kLoop, calls=%fused_computation.71 | loop fusion | flops 35389440 | bytes 25952264 | tf_op jit(solution)/shard_map/cond/branch_1_fun/broadcast_in_dim | solution.py:1399
  409.7 7.4 %fusion.50 = (f32[1,5,96,768]{3,2,1,0:T(8,128)}, bf16[5,96,768]{2,1,0:T(8,128)(2,1)S(1)}, f32[1,5,96,768]{3,2,1,0:T(8,128)}) fusion(bf16[5,96,768]{2,1,0:T(8,128)(2,1)} %get-tuple-element.198, bf16[5,96,768]{2,1,0:T(8,128)(2,1)} %get-tuple-element.182, f32[1,5,96,768]{3,2,1,0:T(8,128)} %get-tuple-element.183, f32[]{:T(128)} %bitcast.147, f32[]{:T(128)} %bitcast.134, ...), kind=kLoop, calls=%fused_computation.100 | loop fusion | flops 11059200 | bytes 8110088 | tf_op jit(solution)/shard_map/cond/branch_1_fun/broadcast_in_dim | solution.py:1399
  417.2 28.4 %add_convert_fusion = (bf16[4016,768]{1,0:T(8,128)(2,1)}, f32[1,4016,768]{2,1,0:T(8,128)}, f32[1,4016,768]{2,1,0:T(8,128)}) fusion(bf16[4016,768]{1,0:T(8,128)(2,1)S(1)} %copy-done.16, bf16[4016,768]{1,0:T(8,128)(2,1)} %get-tuple-element.178, f32[1,4016,768]{2,1,0:T(8,128)} %get-tuple-element.177, f32[]{:T(128)} %bitcast.147, f32[]{:T(128)} %bitcast.134, ...), kind=kLoop, calls=%fused_computation.38 | loop fusion | flops 92528640 | bytes 67854344 | tf_op jit(solution)/shard_map/cond/branch_1_fun/convert_element_type | solution.py:1379
  445.6 142.1 %sum_groups.1 = (bf16[4016,768]{1,0:T(8,128)(2,1)}, bf16[480,768]{1,0:T(8,128)(2,1)S(1)}, f32[6,768]{1,0:T(8,128)S(1)}) custom-call(bf16[4016,768]{1,0:T(8,128)(2,1)} %get-tuple-element.914.refs_0_, bf16[480,768]{1,0:T(8,128)(2,1)S(1)} %bitcast.636, f32[6,768]{1,0:T(8,128)S(1)} %get-tuple-element.924.refs_2_), custom_call_target="tpu_custom_call" | custom-call | bytes 300000000 | tf_op jit(solution)/shard_map/cond/branch_1_fun/sum_groups/pallas_call | solution.py:1015
  587.6 0.1 convert_multiply_fusion.8
  587.8 2.4 fusion.305
  590.2 3.1 maximum_bitcast_fusion
  593.3 20.0 %fusion.306 = (bf16[4016,768]{1,0:T(8,128)(2,1)}, f32[4016,768]{1,0:T(8,128)}, f32[4016,768]{1,0:T(8,128)}) fusion(f32[4016,768]{1,0:T(8,128)} %get-tuple-element.176, bf16[4016,768]{1,0:T(8,128)(2,1)S(1)} %copy-done.17, f32[4016,768]{1,0:T(8,128)} %get-tuple-element.201), kind=kLoop, calls=%fused_computation.674 | loop fusion | flops 33927168 | bytes 61685760 | tf_op jit(solution)/shard_map/cond/branch_0_fun/convert_element_type | solution.py:1299
  613.3 8.0 %fusion.304 = (bf16[2,2,768,384]{3,2,1,0:T(8,128)(2,1)}, f32[2,2,768,384]{3,2,1,0:T(8,128)}, f32[2,2,768,384]{3,2,1,0:T(8,128)}) fusion(f32[2,2,768,384]{3,2,1,0:T(8,128)} %get-tuple-element.184, bf16[2,2,768,384]{3,2,1,0:T(8,128)(2,1)} %all-reduce.18.cloned.1.call-done, f32[2,2,768,384]{3,2,1,0:T(8,128)} %get-tuple-element.204), kind=kLoop, calls=%fused_computation.672 | loop fusion | flops 12976128 | bytes 23592960 | tf_op jit(solution)/shard_map/cond/branch_0_fun/convert_element_type | solution.py:1309
  621.5 0.5 copy-done.87
  (88 shorter events, 0.9 us)
Async XLA Ops:
  7.2 80.6 %all-gather.24.cloned.1.call-start = ((), (), s32[]{:S(2)}) async-start(), calls=%async_computation.27 | async-start | bytes 6635520 | tf_op jit(solution)/shard_map/all_gather | solution.py:1442
  48.9 38.9 %copy-start.3 = (f32[5,96,768]{2,1,0:T(8,128)S(1)}, f32[5,96,768]{2,1,0:T(8,128)}, u32[]{:S(2)}) copy-start(f32[5,96,768]{2,1,0:T(8,128)} %param.34) | copy-start | bytes 4423684
  48.9 38.9 %copy-start.10 = (f32[1,5,96,768]{3,2,1,0:T(8,128)S(1)}, f32[1,5,96,768]{3,2,1,0:T(8,128)}, u32[]{:S(2)}) copy-start(f32[1,5,96,768]{3,2,1,0:T(8,128)} %param.35) | copy-start | bytes 4423684
  48.9 38.9 %copy-start.23 = (f32[6,768]{1,0:T(8,128)S(1)}, f32[6,768]{1,0:T(8,128)}, u32[]{:S(2)}) copy-start(f32[6,768]{1,0:T(8,128)} %param.42) | copy-start | bytes 55300
  48.9 38.9 %copy-start.83 = (s32[2,1,256]{2,1,0:T(1,128)S(1)}, s32[2,1,256]{2,1,0:T(1,128)}, u32[]{:S(2)}) copy-start(s32[2,1,256]{2,1,0:T(1,128)} %param.26) | copy-start | bytes 6148
  48.9 38.9 %copy-start.86 = (s32[2,1,16]{2,1,0:T(1,128)S(1)}, s32[2,1,16]{2,1,0:T(1,128)}, u32[]{:S(2)}) copy-start(s32[2,1,16]{2,1,0:T(1,128)} %param.29) | copy-start | bytes 388
  48.9 38.9 %copy-start.129 = (s32[2,1,256]{2,1,0:T(1,128)S(1)}, s32[2,1,256]{2,1,0:T(1,128)}, u32[]{:S(2)}) copy-start(s32[2,1,256]{2,1,0:T(1,128)} %param.28) | copy-start | bytes 6148
  48.9 38.9 %copy-start.130 = (s32[2,1,256,1]{2,3,1,0:T(1,128)S(1)}, s32[2,1,256,1]{2,3,1,0:T(1,128)}, u32[]{:S(2)}) copy-start(s32[2,1,256,1]{2,3,1,0:T(1,128)} %param.27) | copy-start | bytes 6148
  96.4 0.6 copy-start.61
  96.5 186.5 %all-gather.22.cloned.1.call-start = ((), (), s32[]{:S(2)}) async-start(), calls=%async_computation.25 | async-start | bytes 6635520 | tf_op jit(solution)/shard_map/cond/branch_1_fun/all_gather | solution.py:1358
  98.4 131.3 %copy-start.2 = (s32[8,384]{1,0:T(8,128)}, s32[8,384]{1,0:T(8,128)S(1)}, u32[]{:S(2)}) copy-start(s32[8,384]{1,0:T(8,128)S(1)} %get-tuple-element.928.ints) | copy-start | bytes 36868 | tf_op jit(solution)/shard_map/conditional.1
  210.6 402.7 %all-reduce.18.cloned.1.call-start = ((), (), s32[]{:S(2)}) async-start(), calls=%async_computation.26 | async-start | bytes 4718592 | tf_op jit(solution)/shard_map/cond/branch_1_fun/psum | solution.py:1382
  229.6 29.5 %copy-start.50 = (f32[1,6,768]{2,0,1:T(1,128)S(1)}, f32[1,6,768]{2,0,1:T(1,128)}, u32[]{:S(2)}) copy-start(f32[1,6,768]{2,0,1:T(1,128)} %get-tuple-element.787) | copy-start | bytes 55300 | tf_op jit(solution)/shard_map/conditional.1
  229.6 29.5 %copy-start.52 = (f32[1,6,768]{2,0,1:T(1,128)S(1)}, f32[1,6,768]{2,0,1:T(1,128)}, u32[]{:S(2)}) copy-start(f32[1,6,768]{2,0,1:T(1,128)} %get-tuple-element.788) | copy-start | bytes 55300 | tf_op jit(solution)/shard_map/conditional.1
  229.6 29.5 %copy-start.70 = (f32[6,768]{1,0:T(8,128)S(1)}, f32[6,768]{1,0:T(8,128)}, u32[]{:S(2)}) copy-start(f32[6,768]{1,0:T(8,128)} %get-tuple-element.173) | copy-start | bytes 55300 | tf_op jit(solution)/shard_map/conditional.1
  229.6 30.8 %copy-start.14 = (bf16[2,2,768,384]{3,2,1,0:T(8,128)(2,1)S(1)}, bf16[2,2,768,384]{3,2,1,0:T(8,128)(2,1)}, u32[]{:S(2)}) copy-start(bf16[2,2,768,384]{3,2,1,0:T(8,128)(2,1)} %get-tuple-element.186) | copy-start | bytes 7077892 | tf_op jit(solution)/shard_map/conditional.1
  255.7 2.7 copy-start
  258.4 0.7 copy-start.1
  269.2 121.6 %copy-start.58 = (f32[6,768]{1,0:T(8,128)S(1)}, f32[6,768]{1,0:T(8,128)}, u32[]{:S(2)}) copy-start(f32[6,768]{1,0:T(8,128)} %multiply_subtract_fusion.4.vec) | copy-start | bytes 55300 | tf_op jit(solution)/shard_map/conditional.1
  409.7 7.4 %copy-start.16 = (bf16[4016,768]{1,0:T(8,128)(2,1)S(1)}, bf16[4016,768]{1,0:T(8,128)(2,1)}, u32[]{:S(2)}) copy-start(bf16[4016,768]{1,0:T(8,128)(2,1)} %get-tuple-element.196) | copy-start | bytes 18505732 | tf_op jit(solution)/shard_map/conditional.1
  445.5 142.2 %copy-start.72 = (f32[6,768]{1,0:T(8,128)S(1)}, f32[6,768]{1,0:T(8,128)}, u32[]{:S(2)}) copy-start(f32[6,768]{1,0:T(8,128)} %get-tuple-element.206) | copy-start | bytes 55300 | tf_op jit(solution)/shard_map/conditional.1
  445.5 142.2 %copy-start.19 = (f32[5,96,768]{2,1,0:T(8,128)S(1)}, f32[5,96,768]{2,1,0:T(8,128)}, u32[]{:S(2)}) copy-start(f32[5,96,768]{2,1,0:T(8,128)} %get-tuple-element.203) | copy-start | bytes 4423684 | tf_op jit(solution)/shard_map/conditional.1
  587.6 5.7 copy-start.17
  621.5 0.6 copy-start.87
  621.5 0.6 copy-start.88
  621.5 0.6 copy-start.89
  621.5 0.6 copy-start.90
  621.5 0.6 copy-start.91
  621.5 0.6 copy-start.158
  621.5 0.6 copy-start.159
Sparse Core Ops, SparseCore 0:
  10.2 77.5 all-gather.23
  210.7 72.2 all-gather.21
  409.8 91.5 all-reduce.17

commit v6 on v5

--- a/solution.py
+++ b/solution.py
@@ -1366,7 +1366,7 @@
         *grads, dvector, loss, norm_value, factor = run_step(
             n, slots, vocab, sizes, ints, vector_state[0], x_low, embed_low, attn_low, expert_low
         )
-        loss, norm_value, factor = loss[0, 0], norm_value[0, 0], factor[0, 0]
+        factor = factor[0, 0]
         taken.append(grads)
         loss_list.append(loss)
         norm_list.append(norm_value)
@@ -1387,7 +1387,7 @@
         (low_delta(0, states[0]), attn_delta.reshape(-1, D)), vectors - vector_state[0]
     )
     sums = (embed_sum, attn_sum.reshape(attn_delta.shape), expert_sum, vector_sum)
-    results = [jnp.stack(loss_list)[None], jnp.stack(norm_list)[None]]
+    results = [jnp.concatenate(loss_list, axis=1), jnp.concatenate(norm_list, axis=1)]
     for k in range(4):
         delta_mean = sums[k].astype(jnp.float32) * (1.0 / lax.axis_size("grp"))
         if k < 3:

time: 638 us -> 638 us (level)
  no operation moved by 1% of the time
where the time goes in v6:
time: 638 us; the launch traced here: 629 us
  Pallas kernels  430 us (67%)
  other arithmetic  142 us (22%)
  waiting for transfers between devices  21.4 us (3%)
  between operations  14.9 us (2%)
  local copies, waits for them, and re-layouts  11.8 us (2%)
  loops' own time  9.05 us (1%)
    pallas_call x2, Pallas kernels, run_step(): pl.pallas_call(functools.partial(step_kernel, (n, slots, vocab, vocab_row...  216 us
    pallas_call x1, Pallas kernels, sum_over_groups(): pl.pallas_call(functools.partial(sum_kernel, tuple(shapes)), out_shape=[j...  142 us
    pallas_call x2, Pallas kernels, fetch(): pl.pallas_call(functools.partial(fetch_kernel, (n, slots, vocab_rows) + s...  57.3 us
    convert_element_type x1, other arithmetic, quick_window(): low_delta = lambda k, state: state[0].astype(jnp.bfloat16)  28.4 us
    broadcast_in_dim x3, other arithmetic, quick_window(): results += [states[k][1][None], states[k][2][None], master_new, outer_new]  26.3 us
    convert_element_type x1, other arithmetic, window(): new_master[0].astype(jnp.bfloat16)  20 us
    convert_element_type x1, other arithmetic, quick_window(): embed_low = padded(moved(0, again).astype(jnp.bfloat16))  19 us
    pallas_call x1, Pallas kernels, share(): pl.pallas_call(functools.partial(share_kernel, n, groups), out_shape=(jax...  14.7 us
  transfers between devices with their start and end apart: 3, of which 2 were waited for; matrix products, arithmetic and copies ran while one was open for 18% of the time, Pallas kernels for 34%

profile of v6, /device:TPU:0, one launch (start us, length us, event | category | flops | bytes accessed | tf_op | source)
XLA Modules:
  0.0 628.9 jit_solution(17984819783572461150)
XLA Ops:
  7.2 2.3 convert_element_type.363
  9.6 0.7 copy.419
  10.3 0.7 copy.418
  11.0 0.7 pad.25
  11.7 0.7 broadcast_add_fusion.3
  12.3 0.7 copy_bitcast_fusion.2
  13.0 1.0 select_reduce_fusion.10
  14.1 0.3 fusion.302
  14.4 0.7 and_select_fusion.3
  15.1 0.3 convert_reduce_fusion
  15.3 0.3 select_reduce_fusion.9
  15.6 0.6 select_reduce_fusion.14
  16.3 0.3 select_reduce_fusion.8
  16.6 0.6 broadcast_in_dim.421
  17.2 0.7 concatenate.45.packed
  17.9 14.7 %share_ids.1 = (s32[8,2,640]{2,1,0:T(2,128)}, s32[8,128]{1,0:T(8,128)}) custom-call(s32[2,640]{1,0:T(2,128)} %concatenate.45.packed), custom_call_target="tpu_custom_call" | custom-call | tf_op jit(solution)/shard_map/share_ids/pallas_call | solution.py:341
  32.6 1.3 slice.182
  34.5 0.8 subtract_bitcast_fusion.1
  35.4 0.7 slice_bitcast_fusion.57
  36.2 0.8 subtract_bitcast_fusion
  37.1 4.0 convert_element_type.364
  41.1 7.8 %convert_element_type.362.eb = bf16[4016,768]{1,0:T(8,128)(2,1)} convert(f32[4016,768]{1,0:T(8,128)} %param.30) | non-fusion elementwise | flops 3084288 | bytes 18505728 | tf_op jit(solution)/shard_map/convert_element_type | solution.py:1441
  49.0 31.2 %fetch_rows.3 = bf16[256,768]{1,0:T(8,128)(2,1)} custom-call(s32[8,384]{1,0:T(8,128)S(1)} %slice_bitcast_fusion.56.ints, bf16[4016,768]{1,0:T(8,128)(2,1)} %convert_element_type.362.eb), custom_call_target="tpu_custom_call" | custom-call | tf_op jit(solution)/shard_map/fetch_rows/pallas_call | solution.py:398
  80.2 7.6 %all-gather.24.cloned.1.call-done = bf16[5,768,768]{2,1,0:T(8,128)(2,1)} async-done(((bf16[5,96,768]{2,1,0:T(8,128)(2,1)}), bf16[5,768,768]{2,1,0:T(8,128)(2,1)}) %all-gather.24.cloned.1.call-update) | async-done | bytes 5898256 | tf_op jit(solution)/shard_map/all_gather | solution.py:1442
  87.8 533.6 %conditional.3 = (f32[1,2]{1,0:T(1,128)S(1)}, f32[1,2]{1,0:T(1,128)S(1)}, f32[1,4016,768]{2,1,0:T(8,128)}, f32[1,4016,768]{2,1,0:T(8,128)}, f32[4016,768]{1,0:T(...) conditional(s32[]{:T(128)} %bitcast.155, ((), ...), branch_computations={%region_9.97_spmd, %region_96.99_spmd} | conditional | flops 16723800064 | bytes 1105412352
  96.5 0.5 copy-done.61
  97.1 1.3 slice_bitcast_fusion.1
  98.4 107.8 %inner_step.2 = (bf16[4016,768]{1,0:T(8,128)(2,1)}, bf16[5,96,768]{2,1,0:T(8,128)(2,1)}, bf16[2,2,768,384]{3,2,1,0:T(8,128)(2,1)}, f32[6,768]{1,0:T(8,128)}, f32...) custom-call(s32[8,384]{1,0:T(8,128)} %get-tuple-element.927.ints, f32[6,768]{1,0:T(8,128)S(1)} %get-tuple-element.166.vec, ...), custom_call_target="tpu_custom_call" | custom-call | tf_op jit(solution)/shard_map/cond/branch_1_fun/inner_step/pallas_call | solution.py:811
  206.2 4.4 fusion.48
  210.6 19.0 %fusion.15.eb.eb_in = bf16[4016,768]{1,0:T(8,128)(2,1)S(1)} fusion(bf16[4016,768]{1,0:T(8,128)(2,1)} %get-tuple-element.178, f32[4016,768]{1,0:T(8,128)} %get-tuple-element.176, f32[1,4016,768]{2,1,0:T(8,128)} %get-tuple-element.179, f32[1,4016,768]{2,1,0:T(8,128)} %get-tuple-element.177, f32[]{:T(128)} %bitcast.133), kind=kLoop, calls=%fused_computation.42 | loop fusion | flops 52432896 | bytes 49348612 | tf_op jit(solution)/shard_map/cond/branch_1_fun/convert_element_type | solution.py:1362
  229.7 26.1 %fetch_rows.2.x_low = bf16[256,768]{1,0:T(8,128)(2,1)S(1)} custom-call(s32[8,384]{1,0:T(8,128)S(1)} %get-tuple-element.928.ints, bf16[4016,768]{1,0:T(8,128)(2,1)S(1)} %fusion.15.eb.eb_in), custom_call_target="tpu_custom_call" | custom-call | tf_op jit(solution)/shard_map/cond/branch_1_fun/fetch_rows/pallas_call | solution.py:398
  255.7 2.7 copy-done
  258.4 0.7 copy-done.1
  259.2 1.3 multiply_subtract_fusion.4.vec
  260.5 8.7 %fusion.31.expw_in = bf16[2,2,768,384]{3,2,1,0:T(8,128)(2,1)} fusion(bf16[2,2,768,384]{3,2,1,0:T(8,128)(2,1)S(1)} %copy-done.14, f32[2,2,768,384]{3,2,1,0:T(8,128)} %get-tuple-element.184, f32[1,2,2,768,384]{4,3,2,1,0:T(8,128)} %get-tuple-element.187, f32[1,2,2,768,384]{4,3,2,1,0:T(8,128)} %get-tuple-element.185, f32[]{:T(128)} %bitcast.133), kind=kLoop, calls=%fused_computation.69 | loop fusion | flops 20054016 | bytes 18874372 | tf_op jit(solution)/shard_map/cond/branch_1_fun/convert_element_type | solution.py:1361
  269.2 13.8 %all-gather.22.cloned.1.call-done.attn_in = bf16[5,768,768]{2,1,0:T(8,128)(2,1)} async-done(((bf16[5,96,768]{2,1,0:T(8,128)(2,1)}), bf16[5,768,768]{2,1,0:T(8,128)(2,1)}) %all-gather.22.cloned.1.call-update) | async-done | bytes 5898256 | tf_op jit(solution)/shard_map/cond/branch_1_fun/all_gather | solution.py:1358
  283.0 107.8 %inner_step.3 = (bf16[4016,768]{1,0:T(8,128)(2,1)}, bf16[5,96,768]{2,1,0:T(8,128)(2,1)}, bf16[2,2,768,384]{3,2,1,0:T(8,128)(2,1)}, f32[6,768]{1,0:T(8,128)}, f32...) custom-call(s32[8,384]{1,0:T(8,128)} %copy-done.2, f32[6,768]{1,0:T(8,128)} %multiply_subtract_fusion.4.vec, ...), custom_call_target="tpu_custom_call" | custom-call | tf_op jit(solution)/shard_map/cond/branch_1_fun/inner_step/pallas_call | solution.py:811
  390.8 2.1 fusion.54
  392.9 16.8 %fusion.33 = (f32[1,2,2,768,384]{4,3,2,1,0:T(8,128)}, bf16[2,2,768,384]{3,2,1,0:T(8,128)(2,1)}, f32[1,2,2,768,384]{4,3,2,1,0:T(8,128)}) fusion(bf16[2,2,768,384]{3,2,1,0:T(8,128)(2,1)} %get-tuple-element.194, bf16[2,2,768,384]{3,2,1,0:T(8,128)(2,1)} %get-tuple-element.186, f32[1,2,2,768,384]{4,3,2,1,0:T(8,128)} %get-tuple-element.187, f32[]{:T(128)} %bitcast.141, ...), kind=kLoop, calls=%fused_computation.71 | loop fusion | flops 35389440 | bytes 25952264 | tf_op jit(solution)/shard_map/cond/branch_1_fun/broadcast_in_dim | solution.py:1399
  409.7 7.4 %fusion.50 = (f32[1,5,96,768]{3,2,1,0:T(8,128)}, bf16[5,96,768]{2,1,0:T(8,128)(2,1)S(1)}, f32[1,5,96,768]{3,2,1,0:T(8,128)}) fusion(bf16[5,96,768]{2,1,0:T(8,128)(2,1)} %get-tuple-element.198, bf16[5,96,768]{2,1,0:T(8,128)(2,1)} %get-tuple-element.182, f32[1,5,96,768]{3,2,1,0:T(8,128)} %get-tuple-element.183, f32[]{:T(128)} %bitcast.141, f32[]{:T(128)} %bitcast.133, ...), kind=kLoop, calls=%fused_computation.100 | loop fusion | flops 11059200 | bytes 8110088 | tf_op jit(solution)/shard_map/cond/branch_1_fun/broadcast_in_dim | solution.py:1399
  417.2 28.4 %add_convert_fusion = (bf16[4016,768]{1,0:T(8,128)(2,1)}, f32[1,4016,768]{2,1,0:T(8,128)}, f32[1,4016,768]{2,1,0:T(8,128)}) fusion(bf16[4016,768]{1,0:T(8,128)(2,1)S(1)} %copy-done.16, bf16[4016,768]{1,0:T(8,128)(2,1)} %get-tuple-element.178, f32[1,4016,768]{2,1,0:T(8,128)} %get-tuple-element.177, f32[]{:T(128)} %bitcast.141, f32[]{:T(128)} %bitcast.133, ...), kind=kLoop, calls=%fused_computation.38 | loop fusion | flops 92528640 | bytes 67854344 | tf_op jit(solution)/shard_map/cond/branch_1_fun/convert_element_type | solution.py:1379
  445.6 142.1 %sum_groups.1 = (bf16[4016,768]{1,0:T(8,128)(2,1)}, bf16[480,768]{1,0:T(8,128)(2,1)S(1)}, f32[6,768]{1,0:T(8,128)S(1)}) custom-call(bf16[4016,768]{1,0:T(8,128)(2,1)} %get-tuple-element.914.refs_0_, bf16[480,768]{1,0:T(8,128)(2,1)S(1)} %bitcast.628, f32[6,768]{1,0:T(8,128)S(1)} %get-tuple-element.924.refs_2_), custom_call_target="tpu_custom_call" | custom-call | bytes 300000000 | tf_op jit(solution)/shard_map/cond/branch_1_fun/sum_groups/pallas_call | solution.py:1015
  587.6 0.1 convert_multiply_fusion.8
  587.8 2.4 fusion.305
  590.2 3.1 pad_maximum_fusion
  593.3 20.0 %fusion.306 = (bf16[4016,768]{1,0:T(8,128)(2,1)}, f32[4016,768]{1,0:T(8,128)}, f32[4016,768]{1,0:T(8,128)}) fusion(f32[4016,768]{1,0:T(8,128)} %get-tuple-element.176, bf16[4016,768]{1,0:T(8,128)(2,1)S(1)} %copy-done.17, f32[4016,768]{1,0:T(8,128)} %get-tuple-element.201), kind=kLoop, calls=%fused_computation.674 | loop fusion | flops 33927168 | bytes 61685760 | tf_op jit(solution)/shard_map/cond/branch_0_fun/convert_element_type | solution.py:1299
  613.3 8.0 %fusion.304 = (bf16[2,2,768,384]{3,2,1,0:T(8,128)(2,1)}, f32[2,2,768,384]{3,2,1,0:T(8,128)}, f32[2,2,768,384]{3,2,1,0:T(8,128)}) fusion(f32[2,2,768,384]{3,2,1,0:T(8,128)} %get-tuple-element.184, bf16[2,2,768,384]{3,2,1,0:T(8,128)(2,1)} %all-reduce.18.cloned.1.call-done, f32[2,2,768,384]{3,2,1,0:T(8,128)} %get-tuple-element.204), kind=kLoop, calls=%fused_computation.672 | loop fusion | flops 12976128 | bytes 23592960 | tf_op jit(solution)/shard_map/cond/branch_0_fun/convert_element_type | solution.py:1309
  621.5 0.5 copy-done.87
  (88 shorter events, 0.9 us)
Async XLA Ops:
  7.2 80.6 %all-gather.24.cloned.1.call-start = ((), (), s32[]{:S(2)}) async-start(), calls=%async_computation.27 | async-start | bytes 6635520 | tf_op jit(solution)/shard_map/all_gather | solution.py:1442
  48.9 38.9 %copy-start.3 = (f32[5,96,768]{2,1,0:T(8,128)S(1)}, f32[5,96,768]{2,1,0:T(8,128)}, u32[]{:S(2)}) copy-start(f32[5,96,768]{2,1,0:T(8,128)} %param.34) | copy-start | bytes 4423684
  48.9 38.9 %copy-start.10 = (f32[1,5,96,768]{3,2,1,0:T(8,128)S(1)}, f32[1,5,96,768]{3,2,1,0:T(8,128)}, u32[]{:S(2)}) copy-start(f32[1,5,96,768]{3,2,1,0:T(8,128)} %param.35) | copy-start | bytes 4423684
  48.9 38.9 %copy-start.23 = (f32[6,768]{1,0:T(8,128)S(1)}, f32[6,768]{1,0:T(8,128)}, u32[]{:S(2)}) copy-start(f32[6,768]{1,0:T(8,128)} %param.42) | copy-start | bytes 55300
  48.9 38.9 %copy-start.83 = (s32[2,1,256]{2,1,0:T(1,128)S(1)}, s32[2,1,256]{2,1,0:T(1,128)}, u32[]{:S(2)}) copy-start(s32[2,1,256]{2,1,0:T(1,128)} %param.26) | copy-start | bytes 6148
  48.9 38.9 %copy-start.86 = (s32[2,1,16]{2,1,0:T(1,128)S(1)}, s32[2,1,16]{2,1,0:T(1,128)}, u32[]{:S(2)}) copy-start(s32[2,1,16]{2,1,0:T(1,128)} %param.29) | copy-start | bytes 388
  48.9 38.9 %copy-start.129 = (s32[2,1,256]{2,1,0:T(1,128)S(1)}, s32[2,1,256]{2,1,0:T(1,128)}, u32[]{:S(2)}) copy-start(s32[2,1,256]{2,1,0:T(1,128)} %param.28) | copy-start | bytes 6148
  48.9 38.9 %copy-start.130 = (s32[2,1,256,1]{2,3,1,0:T(1,128)S(1)}, s32[2,1,256,1]{2,3,1,0:T(1,128)}, u32[]{:S(2)}) copy-start(s32[2,1,256,1]{2,3,1,0:T(1,128)} %param.27) | copy-start | bytes 6148
  96.4 0.6 copy-start.61
  96.5 186.5 %all-gather.22.cloned.1.call-start = ((), (), s32[]{:S(2)}) async-start(), calls=%async_computation.25 | async-start | bytes 6635520 | tf_op jit(solution)/shard_map/cond/branch_1_fun/all_gather | solution.py:1358
  98.4 131.3 %copy-start.2 = (s32[8,384]{1,0:T(8,128)}, s32[8,384]{1,0:T(8,128)S(1)}, u32[]{:S(2)}) copy-start(s32[8,384]{1,0:T(8,128)S(1)} %get-tuple-element.928.ints) | copy-start | bytes 36868 | tf_op jit(solution)/shard_map/conditional.1
  210.6 402.7 %all-reduce.18.cloned.1.call-start = ((), (), s32[]{:S(2)}) async-start(), calls=%async_computation.26 | async-start | bytes 4718592 | tf_op jit(solution)/shard_map/cond/branch_1_fun/psum | solution.py:1382
  229.6 29.5 %copy-start.50 = (f32[1,6,768]{2,0,1:T(1,128)S(1)}, f32[1,6,768]{2,0,1:T(1,128)}, u32[]{:S(2)}) copy-start(f32[1,6,768]{2,0,1:T(1,128)} %get-tuple-element.787) | copy-start | bytes 55300 | tf_op jit(solution)/shard_map/conditional.1
  229.6 29.5 %copy-start.52 = (f32[1,6,768]{2,0,1:T(1,128)S(1)}, f32[1,6,768]{2,0,1:T(1,128)}, u32[]{:S(2)}) copy-start(f32[1,6,768]{2,0,1:T(1,128)} %get-tuple-element.788) | copy-start | bytes 55300 | tf_op jit(solution)/shard_map/conditional.1
  229.6 29.5 %copy-start.70 = (f32[6,768]{1,0:T(8,128)S(1)}, f32[6,768]{1,0:T(8,128)}, u32[]{:S(2)}) copy-start(f32[6,768]{1,0:T(8,128)} %get-tuple-element.173) | copy-start | bytes 55300 | tf_op jit(solution)/shard_map/conditional.1
  229.6 30.8 %copy-start.14 = (bf16[2,2,768,384]{3,2,1,0:T(8,128)(2,1)S(1)}, bf16[2,2,768,384]{3,2,1,0:T(8,128)(2,1)}, u32[]{:S(2)}) copy-start(bf16[2,2,768,384]{3,2,1,0:T(8,128)(2,1)} %get-tuple-element.186) | copy-start | bytes 7077892 | tf_op jit(solution)/shard_map/conditional.1
  255.7 2.7 copy-start
  258.4 0.7 copy-start.1
  269.2 121.6 %copy-start.58 = (f32[6,768]{1,0:T(8,128)S(1)}, f32[6,768]{1,0:T(8,128)}, u32[]{:S(2)}) copy-start(f32[6,768]{1,0:T(8,128)} %multiply_subtract_fusion.4.vec) | copy-start | bytes 55300 | tf_op jit(solution)/shard_map/conditional.1
  409.7 7.4 %copy-start.16 = (bf16[4016,768]{1,0:T(8,128)(2,1)S(1)}, bf16[4016,768]{1,0:T(8,128)(2,1)}, u32[]{:S(2)}) copy-start(bf16[4016,768]{1,0:T(8,128)(2,1)} %get-tuple-element.196) | copy-start | bytes 18505732 | tf_op jit(solution)/shard_map/conditional.1
  445.5 142.2 %copy-start.72 = (f32[6,768]{1,0:T(8,128)S(1)}, f32[6,768]{1,0:T(8,128)}, u32[]{:S(2)}) copy-start(f32[6,768]{1,0:T(8,128)} %get-tuple-element.206) | copy-start | bytes 55300 | tf_op jit(solution)/shard_map/conditional.1
  445.5 142.2 %copy-start.19 = (f32[5,96,768]{2,1,0:T(8,128)S(1)}, f32[5,96,768]{2,1,0:T(8,128)}, u32[]{:S(2)}) copy-start(f32[5,96,768]{2,1,0:T(8,128)} %get-tuple-element.203) | copy-start | bytes 4423684 | tf_op jit(solution)/shard_map/conditional.1
  587.6 5.7 copy-start.17
  621.5 0.6 copy-start.87
  621.5 0.6 copy-start.88
  621.5 0.6 copy-start.89
  621.5 0.6 copy-start.90
  621.5 0.6 copy-start.91
  621.5 0.6 copy-start.158
  621.5 0.6 copy-start.159
Sparse Core Ops, SparseCore 0:
  10.2 77.5 all-gather.23
  210.7 72.2 all-gather.21
  409.8 91.5 all-reduce.17
